TPU v7x, 512 devices: a whole 4x4x16 slice. The times are simulated.
512 devices in a mesh: tile: 64 (over z_lo, y, core), fsdp: 8 (over x, z_hi).
Axes of the slice: x: 4, y: 4, z: 16 (z_hi: 2, z_lo: 8; z = z_hi * 8 + z_lo), core: 2. Of those that a mesh axis runs over, the one named last changes fastest.
Arguments:
- tokens: bfloat16 [8, 64, 16, 16, 1024], P('fsdp', 'tile'), may hold values from -6 to 6
- w_qkv: bfloat16 [1024, 1536], P('fsdp')
- w_out: bfloat16 [512, 1024], P('fsdp'), may hold values from -0.25 to 0.25
- rel_bias: float32 [8, 15, 15], replicated, may hold values from -4 to 4
- seam_codes: int32 [64, 3], P('tile'), may hold values from 0 to 3
- corner_open: int32 [64], P('tile'), may hold values from 0 to 1, as said below
- grad_out: bfloat16 [8, 64, 16, 16, 1024], P('fsdp', 'tile'), may hold values from -6 to 6
Outputs:
- output: bfloat16 [8, 64, 16, 16, 1024], P('fsdp', 'tile')
- grad_tokens: bfloat16 [8, 64, 16, 16, 1024], P('fsdp', 'tile')
- grad_w_qkv: float32 [1024, 1536], P('fsdp', 'tile')
- grad_w_out: float32 [512, 1024], P('fsdp', 'tile')
Inputs may be any that keep to these rules, and one draw needn't show every extreme that they name: Exactly 8 tiles have corner_open = 0.
All inputs are finite; a program needn't handle non-finite values.
Results may differ from a plain program's by a relative error of at most 0.019.
The roundings to bfloat16 on the way count: a program that leaves them out, or rounds other values in their place, can miss the bound.
Values may be sent and summed in bfloat16 or wider, within the bound.
No kernel may reach another device: no remote copies, remote signals or barrier semaphores. Data moves between devices by JAX's collectives and lax.ppermute only.
A program may use at most 64 MiB of HBM per device.

v0:
```python
import jax
import jax.numpy as jnp
from jax import lax
from jax.sharding import PartitionSpec as P

HEADS = 8
HD = 64
WIN = 8
GRID_COLS = 8


EPSILON = 1e-05
TRAILING = (((1,), (1,)), ((), ()))
LEADING = (((0,), (0,)), ((), ()))


def shifted(block, axis, distance):
    devices = range(lax.axis_size(axis))
    route = [((i - distance) % len(devices), i) for i in devices]
    return lax.ppermute(block, axis, route)


def as_sent(array):

    def short(part):
        return part.astype(jnp.bfloat16) if part.dtype == jnp.float32 else part

    return jax.tree.map(short, array)


def position_bias(rel_bias, window, heads):
    span = 2 * window - 1
    places = jnp.arange(window * window, dtype=jnp.int32)
    row_of = places // window
    col_of = places % window
    offset = (row_of[:, None] - row_of[None, :] + window - 1) * span + (
        col_of[:, None] - col_of[None, :] + window - 1
    )
    onehot = (
        offset.reshape(-1)[:, None] == jnp.arange(span * span, dtype=jnp.int32)[None, :]
    ).astype(jnp.float32)
    table = rel_bias.reshape(heads, span * span)
    picked = jnp.dot(
        onehot, table.T, precision=lax.Precision.HIGHEST, preferred_element_type=jnp.float32
    )
    return picked.T.reshape(heads, window * window, window * window)


def orient_strip(strip, seam_code, along, across):
    strip = jnp.where(seam_code % 2 == 1, jnp.flip(strip, along), strip)
    return jnp.where(seam_code // 2 == 1, jnp.flip(strip, across), strip)


def turn_corner(corner_cells, seam_code):
    result = corner_cells
    for turns in range(1, 4):
        result = jnp.where(seam_code == turns, jnp.rot90(corner_cells, turns, axes=(0, 1)), result)
    return result


def assemble(own_block, east_strip, south_strip, corner_cells, tile_codes):
    east_strip = orient_strip(east_strip, tile_codes[0], 0, 1)
    south_strip = orient_strip(south_strip, tile_codes[1], 1, 0)
    corner_cells = turn_corner(corner_cells, tile_codes[2])
    upper = jnp.concatenate([own_block, east_strip], 1)
    lower = jnp.concatenate([south_strip, corner_cells], 1)
    return jnp.concatenate([upper, lower], 0)


def disassemble(region, tile_codes, inner_len):
    own_block = region[:inner_len, :inner_len]
    east_strip = orient_strip(region[:inner_len, inner_len:], tile_codes[0], 0, 1)
    south_strip = orient_strip(region[inner_len:, :inner_len], tile_codes[1], 1, 0)
    corner_cells = turn_corner(region[inner_len:, inner_len:], (4 - tile_codes[2]) % 4)
    return (own_block, east_strip, south_strip, corner_cells)


def place_home(own_block, west_part, north_part, corner_part, row_axis):
    upper = jnp.concatenate([corner_part, north_part], row_axis + 1)
    lower = jnp.concatenate([west_part, own_block], row_axis + 1)
    return jnp.concatenate([upper, lower], row_axis)


def region_mask(side_len, inner_len, open_flag):
    rows = lax.broadcasted_iota(jnp.int32, (side_len, side_len), 0)
    columns = lax.broadcasted_iota(jnp.int32, (side_len, side_len), 1)
    return (open_flag == 1) | (rows < inner_len) | (columns < inner_len)


def split_windows(blocks_in, window):
    side_len = blocks_in.shape[0]
    number = side_len // window
    width = blocks_in.shape[-1]
    blocks_in = blocks_in.reshape(number, window, number, window, width)
    return blocks_in.transpose(0, 2, 1, 3, 4).reshape(number * number, window * window, width)


def merge_windows(blocks_in, side_len, window):
    number = side_len // window
    width = blocks_in.shape[-1]
    blocks_in = blocks_in.reshape(number, number, window, window, width).transpose(0, 2, 1, 3, 4)
    return blocks_in.reshape(side_len * side_len, width)


def normalize(tokens_flat):
    values = tokens_flat.astype(jnp.float32)
    center = values - jnp.mean(values, -1, keepdims=True)
    variance = jnp.mean(center * center, -1, keepdims=True)
    inverse = lax.rsqrt(variance + EPSILON)
    return (center * inverse, inverse)


def per_device(tokens, w_qkv, w_out, rel_bias, seam_codes, corner_open, grad_out):
    tokens_here = tokens[:, 0]
    grads_here = grad_out[:, 0]
    samples = tokens_here.shape[0]
    side_len = tokens_here.shape[1]
    width = tokens_here.shape[-1]
    half_win = WIN // 2
    inner_len = side_len - half_win
    cell_count = side_len * side_len
    tile_codes = seam_codes[0]
    valid_cells = region_mask(side_len, inner_len, corner_open[0])
    bias_full = position_bias(rel_bias, WIN, HEADS)

    def build_all(own_block, east_strip, south_strip, corner_cells):

        def build_one(own_one, east_one, south_one, corner_one):
            return assemble(own_one, east_one, south_one, corner_one, tile_codes)

        return jax.vmap(build_one)(own_block, east_strip, south_strip, corner_cells)

    def split_all(region_vals):

        def split_one(region_one):
            return disassemble(region_one, tile_codes, inner_len)

        return jax.vmap(split_one)(region_vals)

    def to_windows(flat, columns):

        def window_one(block_one):
            return split_windows(block_one, WIN)

        return jax.vmap(window_one)(flat.reshape(samples, side_len, side_len, columns)).reshape(
            -1, WIN * WIN, columns
        )

    def from_windows(wins, columns):

        def merge_one(block_one):
            return merge_windows(block_one, side_len, WIN)

        return jax.vmap(merge_one)(wins.reshape(samples, -1, WIN * WIN, columns)).reshape(
            samples * cell_count, columns
        )

    east_in = shifted(tokens_here[:, half_win:, :half_win], "tile", -1)
    south_in = shifted(tokens_here[:, :half_win, half_win:], "tile", -GRID_COLS)
    corner_in = shifted(tokens_here[:, :half_win, :half_win], "tile", -(GRID_COLS + 1))
    region = build_all(tokens_here[:, half_win:, half_win:], east_in, south_in, corner_in).reshape(
        samples * cell_count, width
    )
    normed_f, inverse = normalize(region)
    normed = normed_f.astype(jnp.bfloat16)

    def add_rows(running, shard_rows, first_row):
        columns = lax.dynamic_slice_in_dim(normed, first_row, shard_rows.shape[0], 1)
        return running + jnp.dot(columns, shard_rows, preferred_element_type=jnp.float32)

    initial = jnp.zeros((normed.shape[0], w_qkv.shape[1]), jnp.float32)
    qkv = add_rows(initial, lax.all_gather(w_qkv, "fsdp", axis=0, tiled=True), jnp.int32(0)).astype(
        jnp.bfloat16
    )
    qkv_cols = qkv.shape[-1]
    window_qkv = to_windows(qkv, qkv_cols).reshape(-1, WIN * WIN, HEADS, 3, HD)
    window_valid = split_windows(valid_cells[:, :, None].astype(jnp.int32), WIN)[..., 0] == 1
    window_valid = jnp.tile(window_valid, (samples, 1))
    queries = window_qkv[:, :, :, 0]
    keys_part = window_qkv[:, :, :, 1]
    values_part = window_qkv[:, :, :, 2]
    scores = (
        jnp.einsum("wqhd,wkhd->whqk", queries, keys_part, preferred_element_type=jnp.float32)
        * HD ** (-0.5)
        + bias_full[None]
    )
    scores = jnp.where(window_valid[:, None, None, :], scores, -1e30)
    row_max = jnp.max(scores, -1, keepdims=True)
    expo = jnp.exp(scores - row_max)
    attn_probs = expo / jnp.sum(expo, -1, keepdims=True)
    attn_probs = attn_probs * window_valid[:, None, :, None].astype(jnp.float32)
    probs_b = attn_probs.astype(jnp.bfloat16)
    heads_w = jnp.einsum(
        "whqk,wkhd->wqhd", probs_b, values_part, preferred_element_type=jnp.float32
    ).astype(jnp.bfloat16)
    heads_out = from_windows(heads_w.reshape(-1, WIN * WIN, HEADS * HD), HEADS * HD)

    def add_rows(running, shard_rows, first_row):
        return jnp.dot(heads_out, shard_rows, preferred_element_type=jnp.float32)

    initial = jnp.zeros((heads_out.shape[0], w_out.shape[1]), jnp.float32)
    branch = (
        add_rows(initial, lax.all_gather(w_out, "fsdp", axis=0, tiled=True), jnp.int32(0))
        .astype(jnp.bfloat16)
        .reshape(samples, side_len, side_len, width)
    )
    own_block, east_out, south_out, corner_out = split_all(branch)
    from_west = shifted(east_out, "tile", 1)
    from_north = shifted(south_out, "tile", GRID_COLS)
    from_corner = jax.tree.map(
        lambda part, own: part.astype(own.dtype),
        shifted(as_sent(corner_out), "tile", GRID_COLS + 1),
        corner_out,
    )
    branch_tile = place_home(own_block, from_west, from_north, from_corner, 1)
    east_grad = shifted(grads_here[:, half_win:, :half_win], "tile", -1)
    south_grad = shifted(grads_here[:, :half_win, half_win:], "tile", -GRID_COLS)
    corner_grad = shifted(grads_here[:, :half_win, :half_win], "tile", -(GRID_COLS + 1))
    region_grad = build_all(
        grads_here[:, half_win:, half_win:], east_grad, south_grad, corner_grad
    ).reshape(samples * cell_count, width)
    grad_heads = lax.dot_general(
        region_grad,
        lax.all_gather(w_out, "fsdp", axis=0, tiled=True),
        TRAILING,
        preferred_element_type=jnp.float32,
    ).astype(jnp.bfloat16)
    out_left, out_right = (heads_out, region_grad)
    output = (tokens_here.astype(jnp.float32) + branch_tile.astype(jnp.float32)).astype(
        jnp.bfloat16
    )
    grad_w = to_windows(grad_heads, HEADS * HD).reshape(-1, WIN * WIN, HEADS, HD)
    dprobs = jnp.einsum("wqhd,wkhd->whqk", grad_w, values_part, preferred_element_type=jnp.float32)
    dvalues = jnp.einsum(
        "whqk,wqhd->wkhd", probs_b, grad_w, preferred_element_type=jnp.float32
    ).astype(jnp.bfloat16)
    delta = jnp.sum(dprobs * attn_probs, -1, keepdims=True)
    dscores = (attn_probs * (dprobs - delta) * HD ** (-0.5)).astype(jnp.bfloat16)
    dqueries = jnp.einsum(
        "whqk,wkhd->wqhd", dscores, keys_part, preferred_element_type=jnp.float32
    ).astype(jnp.bfloat16)
    dkeys = jnp.einsum(
        "whqk,wqhd->wkhd", dscores, queries, preferred_element_type=jnp.float32
    ).astype(jnp.bfloat16)
    dqkv_w = jnp.stack([dqueries, dkeys, dvalues], axis=3)
    dqkv = from_windows(dqkv_w.reshape(-1, WIN * WIN, HEADS * 3 * HD), HEADS * 3 * HD)
    dnormed = lax.dot_general(
        dqkv,
        lax.all_gather(w_qkv, "fsdp", axis=0, tiled=True),
        TRAILING,
        preferred_element_type=jnp.float32,
    )
    dnorm_in = inverse * (
        dnormed
        - jnp.mean(dnormed, -1, keepdims=True)
        - normed_f * jnp.mean(dnormed * normed_f, -1, keepdims=True)
    )
    own_norm, east_norm, south_norm, corner_norm = split_all(
        dnorm_in.reshape(samples, side_len, side_len, width)
    )
    norm_west = shifted(east_norm, "tile", 1)
    norm_north = shifted(south_norm, "tile", GRID_COLS)
    norm_corner = shifted(corner_norm, "tile", GRID_COLS + 1)
    norm_tile = place_home(own_norm, norm_west, norm_north, norm_corner, 1)
    grad_tokens = (grads_here.astype(jnp.float32) + norm_tile).astype(jnp.bfloat16)
    rows_part = lax.slice_in_dim(normed, 0, w_qkv.shape[0] * lax.axis_size("fsdp"), axis=1)
    share_qkv = lax.psum_scatter(
        lax.dot_general(rows_part, dqkv, LEADING, preferred_element_type=jnp.float32).astype(
            jnp.bfloat16
        ),
        "fsdp",
        scatter_dimension=0,
        tiled=True,
    ).astype(jnp.float32)
    rows_part = out_left
    share_out = lax.psum_scatter(
        lax.dot_general(rows_part, out_right, LEADING, preferred_element_type=jnp.float32).astype(
            jnp.bfloat16
        ),
        "fsdp",
        scatter_dimension=0,
        tiled=True,
    ).astype(jnp.float32)
    grad_w_qkv, grad_w_out = (
        lax.psum_scatter(share_qkv, "tile", scatter_dimension=1, tiled=True),
        lax.psum_scatter(share_out, "tile", scatter_dimension=1, tiled=True),
    )
    return (output[:, None], grad_tokens[:, None], grad_w_qkv, grad_w_out)


def solution(mesh):
    placed = (
        P("fsdp", "tile", None, None, None),
        P("fsdp", None),
        P("fsdp", None),
        P(),
        P("tile", None),
        P("tile"),
        P("fsdp", "tile", None, None, None),
    )
    return jax.shard_map(
        per_device,
        mesh=mesh,
        in_specs=placed,
        out_specs=(
            P("fsdp", "tile", None, None, None),
            P("fsdp", "tile", None, None, None),
            P("fsdp", "tile"),
            P("fsdp", "tile"),
        ),
        check_vma=False,
    )
```

profile of v0, /device:TPU:4, one launch (start us, length us, event | category | flops | bytes accessed | tf_op | source)
XLA Modules:
  0.0 981.4 jit_solution(6199171249558342560)
XLA Ops:
  8.8 13.7 %collective-permute-start.2 = (bf16[1,4,4,1024]{3,2,1,0:T(4,128)(2,1)S(1)}, bf16[1,4,4,1024]{3,2,1,0:T(4,128)(2,1)S(1)}, u32[]{:S(2)}, u32[]{:S(2)}) collective-permute-start(bf16[1,4,4,1024]{3,2,1,0:T(4,128)(2,1)S(1)} %slice.103), channel_id=1, source_target_pairs={{72,0},{80,8},{88,16},{96,24},{104,32},{112,40},{120,48},{128,56},... | collective-permute-start | bytes 98312 | tf_op jit(solution)/shard_map/ppermute | solution.py:20
  23.5 2.9 collective-permute-start.1
  27.3 2.7 collective-permute-start
  30.9 1.9 collective-permute-start.8
  33.7 2.0 collective-permute-start.7
  37.7 2.6 convolution_bitcast_fusion
  40.2 1.4 fusion.46
  50.4 2.4 collective-permute-start.6
  58.1 108.5 %all-gather.3.cloned.1.call-done = bf16[1024,1536]{1,0:T(8,128)(2,1)} async-done(((bf16[128,1536]{1,0:T(8,128)(2,1)}), bf16[1024,1536]{1,0:T(8,128)(2,1)}) %all-gather.3.cloned.1.call-update) | async-done | bytes 3145744 | tf_op jit(solution)/shard_map/all_gather | solution.py:172
  166.7 2.9 convolution_convert_fusion.1
  170.5 4.1 reshape.392
  174.6 3.6 fusion.42
  178.2 2.5 copy.105
  180.7 2.1 fusion.9
  182.8 1.4 fusion.47
  185.3 1.5 convolution_convert_fusion.2
  187.2 65.4 %all-gather.5.cloned.1.call-done = bf16[512,1024]{1,0:T(8,128)(2,1)} async-done(((bf16[64,1024]{1,0:T(8,128)(2,1)}), bf16[512,1024]{1,0:T(8,128)(2,1)}) %all-gather.5.cloned.1.call-update) | async-done | bytes 1048592 | tf_op jit(solution)/shard_map/all_gather | solution.py:203
  252.6 1.7 convolution_convert_fusion.8
  255.0 2.1 fusion.14
  257.2 1.4 fusion.23
  258.6 3.4 fusion.13
  261.9 3.8 fusion.12
  265.7 2.6 pad_maximum_fusion
  268.4 4.4 copy.88
  272.7 2.7 reshape_reshape_reshape.7
  277.6 2.7 convolution_convert_fusion
  281.1 1.3 dynamic-slice
  288.0 2.5 rev.130
  290.5 2.5 rev.131
  294.0 2.6 rev.121
  296.7 1.8 broadcast_select_fusion.6
  298.5 1.9 collective-permute-start.5
  300.4 4.2 rev.118
  305.3 1.9 collective-permute-start.4
  307.6 2.5 rev.115
  310.0 1.4 fusion.34
  311.5 2.0 collective-permute-start.3
  314.7 2.7 collective-permute-start.11
  317.4 3.2 rev.132
  320.7 1.9 collective-permute-start.10
  324.4 1.7 collective-permute-done.3
  326.1 1.9 collective-permute-start.9
  331.1 10.2 %collective-permute-done.9 = f32[1,4,4,1024]{3,2,1,0:T(4,128)S(1)} collective-permute-done((f32[1,4,4,1024]{3,2,1,0:T(4,128)S(1)}, f32[1,4,4,1024]{3,2,1,0:T(4,128)S(1)}, u32[]{:S(2)}, u32[]{:S(2)}) %collective-permute-start.9) | collective-permute-done | bytes 65568 | tf_op jit(solution)/shard_map/ppermute | solution.py:20
  343.3 23.9 %reduce-scatter.9.cloned.1.call-done = bf16[64,1024]{1,0:T(8,128)(2,1)} async-done(((bf16[512,1024]{1,0:T(8,128)(2,1)}), bf16[64,1024]{1,0:T(8,128)(2,1)}) %reduce-scatter.9.cloned.1.call-update) | async-done | bytes 131088 | tf_op jit(solution)/shard_map/reduce_scatter | solution.py:276
  367.2 1.8 copy.103
  370.0 172.9 %reduce-scatter.7.cloned.1.call-done = bf16[128,1536]{1,0:T(8,128)(2,1)} async-done(((bf16[1024,1536]{1,0:T(8,128)(2,1)}), bf16[128,1536]{1,0:T(8,128)(2,1)}) %reduce-scatter.7.cloned.1.call-update) | async-done | bytes 393232 | tf_op jit(solution)/shard_map/reduce_scatter | solution.py:267
  542.8 425.1 %all-reduce.2 = f32[128,1536]{1,0:T(8,128)S(1)} all-reduce(bf16[128,1536]{1,0:T(8,128)(2,1)} %reduce-scatter.7.cloned.1.call-done), channel_id=3, replica_groups=mesh['tile'=64,'fsdp'=8] {'tile'}, use_global_device_ids=true, to_apply=%region_8.9.clone | all-reduce | flops 196608 | bytes 1179648
  968.7 6.1 reduce-scatter.11.cloned.1.call-done
  (130 shorter events, 35.3 us)
Async XLA Ops:
  7.2 40.7 %copy-start.4 = (bf16[1,1,16,16,1024]{4,3,2,1,0:T(8,128)(2,1)S(1)}, bf16[1,1,16,16,1024]{4,3,2,1,0:T(8,128)(2,1)}, u32[]{:S(2)}) copy-start(bf16[1,1,16,16,1024]{4,3,2,1,0:T(8,128)(2,1)} %param.13) | copy-start | bytes 1572868
  7.2 159.5 %all-gather.3.cloned.1.call-start = ((), (), s32[]{:S(2)}) async-start(), calls=%async_computation.3 | async-start | bytes 3538944 | tf_op jit(solution)/shard_map/all_gather | solution.py:172
  7.9 244.7 %all-gather.5.cloned.1.call-start = ((), (), s32[]{:S(2)}) async-start(), calls=%async_computation.4 | async-start | bytes 1179648 | tf_op jit(solution)/shard_map/all_gather | solution.py:203
  8.8 41.6 %collective-permute-start.2 = (bf16[1,4,4,1024]{3,2,1,0:T(4,128)(2,1)S(1)}, bf16[1,4,4,1024]{3,2,1,0:T(4,128)(2,1)S(1)}, u32[]{:S(2)}, u32[]{:S(2)}) collective-permute-start(bf16[1,4,4,1024]{3,2,1,0:T(4,128)(2,1)S(1)} %slice.103), channel_id=1, source_target_pairs={{72,0},{80,8},{88,16},{96,24},{104,32},{112,40},{120,48},{128,56},... | collective-permute-start | bytes 98312 | tf_op jit(solution)/shard_map/ppermute | solution.py:20
  23.5 31.2 %collective-permute-start.1 = (bf16[1,4,12,1024]{3,2,1,0:T(8,128)(2,1)S(1)}, bf16[1,4,12,1024]{3,2,1,0:T(8,128)(2,1)S(1)}, u32[]{:S(2)}, u32[]{:S(2)}) collective-permute-start(bf16[1,4,12,1024]{3,2,1,0:T(8,128)(2,1)S(1)} %slice.102), channel_id=1, source_target_pairs={{64,0},{72,8},{80,16},{88,24},{96,32},{104,40},{112,48},{120,56},{... | collective-permute-start | bytes 294920 | tf_op jit(solution)/shard_map/ppermute | solution.py:20
  27.3 26.8 %collective-permute-start = (bf16[1,12,4,1024]{3,2,1,0:T(4,128)(2,1)S(1)}, bf16[1,12,4,1024]{3,2,1,0:T(4,128)(2,1)S(1)}, u32[]{:S(2)}, u32[]{:S(2)}) collective-permute-start(bf16[1,12,4,1024]{3,2,1,0:T(4,128)(2,1)S(1)} %slice.101), channel_id=1, source_target_pairs={{8,0},{16,8},{24,16},{32,24},{40,32},{48,40},{56,48},{64,56},{72,6... | collective-permute-start | bytes 294920 | tf_op jit(solution)/shard_map/ppermute | solution.py:20
  30.9 22.0 %collective-permute-start.8 = (bf16[1,4,4,1024]{3,2,1,0:T(4,128)(2,1)S(1)}, bf16[1,4,4,1024]{3,2,1,0:T(4,128)(2,1)S(1)}, u32[]{:S(2)}, u32[]{:S(2)}) collective-permute-start(bf16[1,4,4,1024]{3,2,1,0:T(4,128)(2,1)S(1)} %slice.114), channel_id=1, source_target_pairs={{72,0},{80,8},{88,16},{96,24},{104,32},{112,40},{120,48},{128,56},... | collective-permute-start | bytes 98312 | tf_op jit(solution)/shard_map/ppermute | solution.py:20
  33.7 22.6 %collective-permute-start.7 = (bf16[1,4,12,1024]{3,2,1,0:T(8,128)(2,1)S(1)}, bf16[1,4,12,1024]{3,2,1,0:T(8,128)(2,1)S(1)}, u32[]{:S(2)}, u32[]{:S(2)}) collective-permute-start(bf16[1,4,12,1024]{3,2,1,0:T(8,128)(2,1)S(1)} %slice.113), channel_id=1, source_target_pairs={{64,0},{72,8},{80,16},{88,24},{96,32},{104,40},{112,48},{120,56},{... | collective-permute-start | bytes 294920 | tf_op jit(solution)/shard_map/ppermute | solution.py:20
  35.8 331.4 %reduce-scatter.9.cloned.1.call-start = ((), (), s32[]{:S(2)}) async-start(), calls=%async_computation.6 | async-start | bytes 1179648 | tf_op jit(solution)/shard_map/reduce_scatter | solution.py:276
  50.4 6.8 collective-permute-start.6
  182.8 1.4 copy-start.6
  186.7 356.1 %reduce-scatter.7.cloned.1.call-start = ((), (), s32[]{:S(2)}) async-start(), calls=%async_computation.5 | async-start | bytes 3538944 | tf_op jit(solution)/shard_map/reduce_scatter | solution.py:267
  258.6 3.4 copy-start.7
  276.7 0.9 copy-start.1
  280.3 2.8 copy-start
  280.3 4.7 copy-start.2
  280.3 694.5 %reduce-scatter.11.cloned.1.call-start = ((), (), s32[]{:S(2)}) async-start(), calls=%async_computation.7 | async-start | bytes 532480
  283.1 1.9 copy-start.9
  296.7 33.4 %copy-start.3 = (bf16[1,1,16,16,1024]{4,3,2,1,0:T(8,128)(2,1)S(1)}, bf16[1,1,16,16,1024]{4,3,2,1,0:T(8,128)(2,1)}, u32[]{:S(2)}) copy-start(bf16[1,1,16,16,1024]{4,3,2,1,0:T(8,128)(2,1)} %param.7) | copy-start | bytes 1572868
  298.5 30.6 %collective-permute-start.5 = (bf16[1,12,4,1024]{3,2,1,0:T(4,128)(2,1)}, bf16[1,12,4,1024]{3,2,1,0:T(4,128)(2,1)}, u32[]{:S(2)}, u32[]{:S(2)}) collective-permute-start(bf16[1,12,4,1024]{3,2,1,0:T(4,128)(2,1)} %broadcast_select_fusion.6), channel_id=1, source_target_pairs={{504,0},{0,8},{8,16},{16,24},{24,32},{32,40},{40,48},{48,56},{56,6... | collective-permute-start | bytes 294920 | tf_op jit(solution)/shard_map/ppermute | solution.py:20
  305.3 22.7 %collective-permute-start.4 = (bf16[1,4,12,1024]{3,2,1,0:T(8,128)(2,1)}, bf16[1,4,12,1024]{3,2,1,0:T(8,128)(2,1)}, u32[]{:S(2)}, u32[]{:S(2)}) collective-permute-start(bf16[1,4,12,1024]{3,2,1,0:T(8,128)(2,1)} %reverse_select_fusion.3), channel_id=1, source_target_pairs={{448,0},{456,8},{464,16},{472,24},{480,32},{488,40},{496,48},{504,... | collective-permute-start | bytes 294920 | tf_op jit(solution)/shard_map/ppermute | solution.py:20
  311.5 12.0 %copy-start.8 = (f32[1,4,4,1024]{3,2,1,0:T(4,128)S(1)}, f32[1,4,4,1024]{3,2,1,0:T(4,128)}, u32[]{:S(2)}) copy-start(f32[1,4,4,1024]{3,2,1,0:T(4,128)} %rev.130) | copy-start | bytes 196612
  311.5 14.7 %collective-permute-start.3 = (bf16[1,4,4,1024]{3,2,1,0:T(4,128)(2,1)}, bf16[1,4,4,1024]{3,2,1,0:T(4,128)(2,1)}, u32[]{:S(2)}, u32[]{:S(2)}) collective-permute-start(bf16[1,4,4,1024]{3,2,1,0:T(4,128)(2,1)} %fusion.34), channel_id=1, source_target_pairs={{440,0},{448,8},{456,16},{464,24},{472,32},{480,40},{488,48},{496,... | collective-permute-start | bytes 98312 | tf_op jit(solution)/shard_map/ppermute | solution.py:20
  314.7 27.5 %collective-permute-start.11 = (f32[1,12,4,1024]{3,2,1,0:T(4,128)}, f32[1,12,4,1024]{3,2,1,0:T(4,128)}, u32[]{:S(2)}, u32[]{:S(2)}) collective-permute-start(f32[1,12,4,1024]{3,2,1,0:T(4,128)} %broadcast_select_fusion.4), channel_id=1, source_target_pairs={{504,0},{0,8},{8,16},{16,24},{24,32},{32,40},{40,48},{48,56},{56,6... | collective-permute-start | bytes 589832 | tf_op jit(solution)/shard_map/ppermute | solution.py:20
  320.7 20.6 %collective-permute-start.10 = (f32[1,4,12,1024]{3,2,1,0:T(8,128)S(1)}, f32[1,4,12,1024]{3,2,1,0:T(8,128)}, u32[]{:S(2)}, u32[]{:S(2)}) collective-permute-start(f32[1,4,12,1024]{3,2,1,0:T(8,128)S(1)} %reverse_select_fusion), channel_id=1, source_target_pairs={{448,0},{456,8},{464,16},{472,24},{480,32},{488,40},{496,48},{504,... | collective-permute-start | bytes 589832 | tf_op jit(solution)/shard_map/ppermute | solution.py:20
  324.4 44.6 %copy-start.5 = (bf16[1,1,16,16,1024]{4,3,2,1,0:T(8,128)(2,1)S(1)}, bf16[1,1,16,16,1024]{4,3,2,1,0:T(8,128)(2,1)}, u32[]{:S(2)}) copy-start(bf16[1,1,16,16,1024]{4,3,2,1,0:T(8,128)(2,1)} %param.13) | copy-start | bytes 1572868
  326.1 15.1 %collective-permute-start.9 = (f32[1,4,4,1024]{3,2,1,0:T(4,128)S(1)}, f32[1,4,4,1024]{3,2,1,0:T(4,128)S(1)}, u32[]{:S(2)}, u32[]{:S(2)}) collective-permute-start(f32[1,4,4,1024]{3,2,1,0:T(4,128)S(1)} %copy_select_fusion), channel_id=1, source_target_pairs={{440,0},{448,8},{456,16},{464,24},{472,32},{480,40},{488,48},{496,... | collective-permute-start | bytes 196616 | tf_op jit(solution)/shard_map/ppermute | solution.py:20
Sparse Core Ops, SparseCore 0:
  11.2 155.4 all-gather.2
  169.9 82.7 all-gather.4
  257.1 109.9 reduce-scatter.8
  372.5 170.2 reduce-scatter.6
  546.0 428.7 reduce-scatter.10
where the time goes:
time: 984 us; the launch traced here: 981 us
  blocking collectives  425 us (43%)
  waiting for transfers between devices  390 us (40%)
  local copies, waits for them, and re-layouts  59 us (6%)
  starting transfers between devices  38.3 us (4%)
  matrix products  26 us (3%)
  between operations  23.9 us (2%)
  other arithmetic  18.8 us (2%)
    unnamed x1, blocking collectives  425 us
    reduce_scatter x1, waiting for transfers between devices, per_device(): lax.psum_scatter(lax.dot_general(rows_part, dqkv, LEADING, preferred_elem...  173 us
    all_gather x1, waiting for transfers between devices, per_device(): lax.all_gather(w_qkv, 'fsdp', axis=0, tiled=True)  109 us
    all_gather x1, waiting for transfers between devices, per_device(): lax.all_gather(w_out, 'fsdp', axis=0, tiled=True)  65.4 us
    ppermute x12, starting transfers between devices, shifted(): return lax.ppermute(block, axis, route)  37.9 us
    reduce_scatter x1, waiting for transfers between devices, per_device(): lax.psum_scatter(lax.dot_general(rows_part, out_right, LEADING, preferred...  23.9 us
  transfers between devices with their start and end apart: 17, of which 8 were waited for; matrix products, arithmetic and copies ran while one was open for 10% of the time, Pallas kernels for 0%

commit v1 on v0

v1 whole, which is shorter than its diff:
```python
import functools
import jax
import jax.numpy as jnp
from jax import lax
from jax.experimental import pallas as pl
from jax.experimental.pallas import tpu as pltpu
from jax.sharding import Mesh, PartitionSpec as P

HEADS = 8
HD = 64
WIN = 8
GRID_COLS = 8
SIDE = 16
HALF = WIN // 2
INNER = SIDE - HALF
CELLS = SIDE * SIDE
EAST = INNER * HALF
CORNER = HALF * HALF
EPSILON = 1e-05
NEG = -1e30
TRAILING = (((1,), (1,)), ((), ()))
LEADING = (((0,), (0,)), ((), ()))
VMEM_LIMIT = 56 * 1024 * 1024

f32 = jnp.float32
bf16 = jnp.bfloat16


def mm(a, b, dims=(((1,), (0,)), ((), ()))):
    return lax.dot_general(a, b, dims, preferred_element_type=f32)


def region_coords(shape, axis):
    place = lax.broadcasted_iota(jnp.int32, shape, axis)
    window, inside = place >> 6, place & 63
    row = (window >> 1) * WIN + (inside >> 3)
    column = (window & 1) * WIN + (inside & 7)
    return row, column


def source_of(codes, shape, axis):
    row, column = region_coords(shape, axis)
    flip_one, flip_two = codes[0] & 1, codes[0] >> 1
    er = jnp.where(flip_one == 1, INNER - 1 - row, row)
    ec = column - INNER
    ec = jnp.where(flip_two == 1, HALF - 1 - ec, ec)
    flip_one, flip_two = codes[1] & 1, codes[1] >> 1
    sc = jnp.where(flip_one == 1, INNER - 1 - column, column)
    sr = row - INNER
    sr = jnp.where(flip_two == 1, HALF - 1 - sr, sr)
    i, j = row - INNER, column - INNER
    turn = codes[2]
    last = HALF - 1
    cr = jnp.where(turn == 0, i, jnp.where(turn == 1, j, jnp.where(turn == 2, last - i, last - j)))
    cc = jnp.where(turn == 0, j, jnp.where(turn == 1, last - i, jnp.where(turn == 2, last - j, i)))
    own = (row + HALF) * SIDE + column + HALF
    east = CELLS + er * HALF + ec
    south = CELLS + EAST + sr * INNER + sc
    corner = CELLS + 2 * EAST + cr * HALF + cc
    low_row, low_column = row < INNER, column < INNER
    return jnp.where(
        low_row, jnp.where(low_column, own, east), jnp.where(low_column, south, corner)
    )


def onehot(condition):
    return jnp.where(condition, 1.0, 0.0).astype(bf16)


def gather_matrices(codes):
    source = source_of(codes, (CELLS, 1), 0)
    own = onehot(source == lax.broadcasted_iota(jnp.int32, (CELLS, CELLS), 1))
    halo = onehot(source - CELLS == lax.broadcasted_iota(jnp.int32, (CELLS, 128), 1))
    return own, halo


def scatter_matrices(codes):
    source = source_of(codes, (1, CELLS), 1)
    own = onehot(source == lax.broadcasted_iota(jnp.int32, (CELLS, CELLS), 0))
    halo = onehot(source - CELLS == lax.broadcasted_iota(jnp.int32, (128, CELLS), 0))
    return own, halo


def arrived_matrix():
    place = lax.broadcasted_iota(jnp.int32, (CELLS, 1), 0)
    row, column = place >> 4, place & 15
    west = (row - HALF) * HALF + column
    north = EAST + row * INNER + column - HALF
    corner = 2 * EAST + row * HALF + column
    low_row, low_column = row < HALF, column < HALF
    index = jnp.where(
        low_row,
        jnp.where(low_column, corner, north),
        jnp.where(low_column, west, -1),
    )
    return onehot(index == lax.broadcasted_iota(jnp.int32, (CELLS, 128), 1))


def prep_kernel(ints_ref, tok_ref, dy_ref, e_ref, s_ref, c_ref, normed_ref, normf_ref, inv_ref, rdy_ref):
    codes = [ints_ref[k] for k in range(3)]
    own, halo = gather_matrices(codes)
    pad = jnp.zeros((128 - 2 * EAST - CORNER, tok_ref.shape[1]), bf16)

    def region(main, which):
        edge = jnp.concatenate([e_ref[which], s_ref[which], c_ref[which], pad], axis=0)
        return mm(own, main) + mm(halo, edge)

    values = region(tok_ref[...], 0)
    center = values - jnp.mean(values, -1, keepdims=True)
    variance = jnp.mean(center * center, -1, keepdims=True)
    inverse = lax.rsqrt(variance + EPSILON)
    normed_f = center * inverse
    normf_ref[...] = normed_f
    normed_ref[...] = normed_f.astype(bf16)
    inv_ref[...] = jnp.broadcast_to(inverse, inv_ref.shape)
    rdy_ref[...] = region(dy_ref[...], 1).astype(bf16)


def attention(open_flag, qkv, grad_heads, bias_ref, heads_ref, dqkv_ref):
    rows = lax.broadcasted_iota(jnp.int32, (128, 128), 0)
    cols = lax.broadcasted_iota(jnp.int32, (128, 128), 1)
    same = (rows >> 6) == (cols >> 6)

    def closed(place):
        inside = place & 63
        return (place >= 64) & ((inside >> 3) >= HALF) & ((inside & 7) >= HALF)

    shut = open_flag == 0
    masks = [
        jnp.where(same, 0.0, NEG),
        jnp.where(same & jnp.logical_not(shut & closed(cols)), 0.0, NEG),
    ]
    place = lax.broadcasted_iota(jnp.int32, (128, 1), 0)
    keep = jnp.where(shut & closed(place), 0.0, 1.0)
    scale = HD ** (-0.5)
    for block in range(2):
        span = pl.ds(block * 128, 128)
        for pair in range(HEADS // 2):
            wide = qkv[span, pl.ds(pair * 384, 384)]
            grads = grad_heads[span, pl.ds(pair * 128, 128)]
            outs, parts = [], []
            for one in range(2):
                head = pair * 2 + one
                q = wide[:, one * 192 : one * 192 + 64]
                k = wide[:, one * 192 + 64 : one * 192 + 128]
                v = wide[:, one * 192 + 128 : one * 192 + 192]
                g = grads[:, one * 64 : one * 64 + 64]
                b64 = bias_ref[head]
                b = jnp.concatenate([b64, b64], axis=1)
                b = jnp.concatenate([b, b], axis=0)
                s = mm(q, k, TRAILING) * scale + b + masks[block]
                e = jnp.exp(s - jnp.max(s, -1, keepdims=True))
                probs = e / jnp.sum(e, -1, keepdims=True)
                if block == 1:
                    probs = probs * keep
                pb = probs.astype(bf16)
                outs.append(mm(pb, v).astype(bf16))
                dp = mm(g, v, TRAILING)
                dv = mm(pb, g, LEADING).astype(bf16)
                delta = jnp.sum(dp * probs, -1, keepdims=True)
                ds = (probs * (dp - delta) * scale).astype(bf16)
                dq = mm(ds, k).astype(bf16)
                dk = mm(ds, q, LEADING).astype(bf16)
                parts += [dq, dk, dv]
            heads_ref[span, pl.ds(pair * 128, 128)] = jnp.concatenate(outs, axis=1)
            dqkv_ref[span, pl.ds(pair * 384, 384)] = jnp.concatenate(parts, axis=1)


def main_kernel(ints_ref, normed_ref, rdy_ref, mine_ref, other_ref, bias_ref, dqkv_ref, heads_ref, qkv_ref, gh_ref):
    core = ints_ref[4]
    normed = normed_ref[...]
    for ref, owner in ((mine_ref, core), (other_ref, 1 - core)):
        for y in range(3):
            start = pl.multiple_of((y * 2 + owner) * 256, 256)
            qkv_ref[:, pl.ds(start, 256)] = mm(normed, ref[y]).astype(bf16)
    total = None
    for ref, owner in ((mine_ref, core), (other_ref, 1 - core)):
        for half in range(2):
            block = out_block(ref, half)
            start = pl.multiple_of(half * 512 + owner * 256, 256)
            term = mm(rdy_ref[:, pl.ds(start, 256)], block, TRAILING)
            total = term if total is None else total + term
    gh_ref[...] = total.astype(bf16)
    attention(ints_ref[3], qkv_ref, gh_ref, bias_ref, heads_ref, dqkv_ref)


def out_block(ref, half):
    return jnp.concatenate([ref[3, pl.ds(k * 128 + half * 64, 64)] for k in range(8)], axis=0)


def home_kernel(
    ints_ref, normf_ref, inv_ref, tok_ref, dy_ref, mine_ref, other_ref, dqkv_ref, heads_ref,
    out_ref, gtok_ref, east_ref, south_ref, corner_ref, branch_ref,
):
    core = ints_ref[4]
    own, halo = scatter_matrices([ints_ref[k] for k in range(3)])
    dnormed = None
    for ref, owner in ((mine_ref, core), (other_ref, 1 - core)):
        for half in range(2):
            start = pl.multiple_of(half * 512 + owner * 256, 256)
            branch_ref[:, pl.ds(start, 256)] = mm(heads_ref[...], out_block(ref, half)).astype(bf16)
        for y in range(3):
            start = pl.multiple_of((y * 2 + owner) * 256, 256)
            term = mm(dqkv_ref[:, pl.ds(start, 256)], ref[y], TRAILING)
            dnormed = term if dnormed is None else dnormed + term

    def edges(which, values):
        edge = mm(halo, values).astype(bf16)
        east_ref[which] = edge[:EAST]
        south_ref[which] = edge[EAST : 2 * EAST]
        corner_ref[which] = edge[2 * EAST : 2 * EAST + CORNER]

    branch = branch_ref[...]
    edges(0, branch)
    out_ref[...] = (tok_ref[...].astype(f32) + mm(own, branch)).astype(bf16)
    normed_f = normf_ref[...]
    dnorm = inv_ref[:, :1] * (
        dnormed
        - jnp.mean(dnormed, -1, keepdims=True)
        - normed_f * jnp.mean(dnormed * normed_f, -1, keepdims=True)
    )
    high = dnorm.astype(bf16)
    low = (dnorm - high.astype(f32)).astype(bf16)
    edges(1, high)
    gtok_ref[...] = (dy_ref[...].astype(f32) + (mm(own, high) + mm(own, low))).astype(bf16)


def finish_kernel(out_ref, gtok_ref, west_ref, north_ref, corner_ref, out2_ref, gtok2_ref):
    place = arrived_matrix()
    pad = jnp.zeros((128 - 2 * EAST - CORNER, out_ref.shape[1]), bf16)
    for which, (part, result) in enumerate(((out_ref, out2_ref), (gtok_ref, gtok2_ref))):
        edge = jnp.concatenate([west_ref[which], north_ref[which], corner_ref[which], pad], axis=0)
        result[...] = (part[...].astype(f32) + mm(place, edge)).astype(bf16)


def grads_kernel(ints_ref, normed_ref, rdy_ref, dqkv_ref, heads_ref, send_ref, keep_ref, tq_ref, to_ref):
    core = ints_ref[4]
    tq_ref[...] = mm(dqkv_ref[...], normed_ref[...], LEADING)
    heads = heads_ref[...]
    twice = []
    for head in range(HEADS):
        one = heads[:, head * HD : (head + 1) * HD]
        twice += [one, one]
    to_ref[...] = mm(rdy_ref[...], jnp.concatenate(twice, axis=1), LEADING)
    lower = lax.broadcasted_iota(jnp.int32, (8, 256), 1) & 127 < 64
    for out_ref, owner in ((send_ref, 1 - core), (keep_ref, core)):
        for y in range(4):
            for x in range(4):
                lanes = pl.ds(x * 256, 256)
                rows = [
                    tq_ref[pl.ds(pl.multiple_of(z * 192 + y * 48 + owner * 24, 8), 24), lanes]
                    for z in range(8)
                ]
                for z in range(8):
                    start = z * 128 + y * 32 + owner * 16
                    low = to_ref[pl.ds(pl.multiple_of(start, 8), 8), lanes]
                    high = to_ref[pl.ds(pl.multiple_of(start + 8, 8), 8), lanes]
                    rows.append(jnp.where(lower, low, high))
                out_ref[y, x] = jnp.concatenate(rows, axis=0).astype(bf16)


def pair_kernel(keep_ref, got_ref, out_ref):
    out_ref[...] = (keep_ref[...].astype(f32) + got_ref[...].astype(f32)).astype(bf16)


def plane_kernel(got_ref, out_ref):
    total = got_ref[0].astype(f32)
    for part in range(1, 16):
        total = total + got_ref[part].astype(f32)
    for z in range(8):
        rows = jnp.concatenate([total[z * 24 : z * 24 + 24], total[192 + z * 8 : 200 + z * 8]], axis=0)
        out_ref[z, 0] = rows[:, :128]
        out_ref[z, 1] = rows[:, 128:]


def last_kernel(got_ref, gq_ref, go_ref):
    total = got_ref[0]
    for part in range(1, 16):
        total = total + got_ref[part]
    square = jnp.concatenate([total, jnp.zeros((96, 128), f32)], axis=0).T
    gq_ref[...] = square[:, :24]
    go_ref[...] = jnp.concatenate([square[:64, 24:32], square[64:, 24:32]], axis=1)


def call(kernel, outs, *args, smem=0, scratch=(), flops=0, name=None):
    specs = [pl.BlockSpec(memory_space=pltpu.SMEM)] * smem + [pl.BlockSpec(memory_space=pltpu.VMEM)] * (
        len(args) - smem
    )
    shapes = [jax.ShapeDtypeStruct(s, d) for s, d in outs]
    size = sum(a.size * a.dtype.itemsize for a in (*args, *shapes))
    return pl.pallas_call(
        kernel,
        out_shape=shapes,
        in_specs=specs,
        out_specs=[pl.BlockSpec(memory_space=pltpu.VMEM)] * len(outs),
        scratch_shapes=list(scratch),
        compiler_params=pltpu.CompilerParams(vmem_limit_bytes=VMEM_LIMIT),
        cost_estimate=pl.CostEstimate(flops=flops, bytes_accessed=size, transcendentals=0),
        name=name,
    )(*args)


def position_bias(rel_bias):
    span = 2 * WIN - 1
    places = jnp.arange(WIN * WIN, dtype=jnp.int32)
    row_of = places // WIN
    col_of = places % WIN
    offset = (row_of[:, None] - row_of[None, :] + WIN - 1) * span + (
        col_of[:, None] - col_of[None, :] + WIN - 1
    )
    onehot_table = (
        offset.reshape(-1)[:, None] == jnp.arange(span * span, dtype=jnp.int32)[None, :]
    ).astype(f32)
    picked = jnp.dot(
        onehot_table,
        rel_bias.reshape(HEADS, span * span).T,
        precision=lax.Precision.HIGHEST,
        preferred_element_type=f32,
    )
    return picked.T.reshape(HEADS, WIN * WIN, WIN * WIN)


TILE_AXES = ("zl", "y", "c")


def shifted(block, distance):
    count = lax.axis_size(TILE_AXES)
    return lax.ppermute(block, TILE_AXES, [((i - distance) % count, i) for i in range(count)])


def per_device(tokens, w_qkv, w_out, rel_bias, seam_codes, corner_open, grad_out):
    width = tokens.shape[-1]
    both = jnp.stack([tokens[0, 0], grad_out[0, 0]])
    tok = tokens.reshape(CELLS, width)
    dy = grad_out.reshape(CELLS, width)
    core = lax.axis_index("c")
    ints = jnp.concatenate([seam_codes[0], corner_open, core[None]]).astype(jnp.int32)

    packed = jnp.concatenate(
        [w_qkv, jnp.concatenate([w_out[:, :512], w_out[:, 512:]], axis=0)], axis=1
    )
    block_at = (lax.axis_index("y") * 2 + core) * 256
    piece = lax.dynamic_slice(packed, (0, block_at), (128, 256))
    across = lax.ppermute(piece, "zh", [(0, 1), (1, 0)])
    first = lax.axis_index("zh") == 0
    piece = jnp.stack([jnp.where(first, piece, across), jnp.where(first, across, piece)])
    mine = lax.all_to_all(
        jnp.broadcast_to(piece[None], (16, 2, 128, 256)), ("y", "x"), 0, 0, tiled=True
    ).reshape(4, width, 256)
    other = lax.ppermute(mine, "c", [(0, 1), (1, 0)])

    east = shifted(both[:, HALF:, :HALF].reshape(2, EAST, width), -1)
    south = shifted(both[:, :HALF, HALF:].reshape(2, EAST, width), -GRID_COLS)
    corner = shifted(both[:, :HALF, :HALF].reshape(2, CORNER, width), -(GRID_COLS + 1))
    bias = position_bias(rel_bias)
    normed, normed_f, inverse, region_dy = call(
        prep_kernel,
        [((CELLS, width), bf16), ((CELLS, width), f32), ((CELLS, 128), f32), ((CELLS, width), bf16)],
        ints, tok, dy, east, south, corner,
        smem=1, flops=4 * 256 * 384 * 1024, name="prep",
    )
    dqkv, heads = call(
        main_kernel,
        [((CELLS, 1536), bf16), ((CELLS, 512), bf16)],
        ints, normed, region_dy, mine, other, bias,
        smem=1, scratch=[pltpu.VMEM((CELLS, 1536), bf16), pltpu.VMEM((CELLS, 512), bf16)],
        flops=2 * 256 * 1024 * 2048, name="attend",
    )
    send, keep = call(
        grads_kernel,
        [((4, 4, 256, 256), bf16), ((4, 4, 256, 256), bf16)],
        ints, normed, region_dy, dqkv, heads,
        smem=1, scratch=[pltpu.VMEM((1536, 1024), f32), pltpu.VMEM((1024, 1024), f32)],
        flops=2 * 256 * 1024 * 2560, name="weight_grads",
    )
    got = lax.ppermute(send, "c", [(0, 1), (1, 0)])
    out_part, gtok_part, east, south, corner = call(
        home_kernel,
        [
            ((CELLS, width), bf16), ((CELLS, width), bf16),
            ((2, EAST, width), bf16), ((2, EAST, width), bf16), ((2, CORNER, width), bf16),
        ],
        ints, normed_f, inverse, tok, dy, mine, other, dqkv, heads,
        smem=1, scratch=[pltpu.VMEM((CELLS, width), bf16)], flops=2 * 256 * 1024 * 2800, name="home",
    )
    west = shifted(east, 1)
    north = shifted(south, GRID_COLS)
    corner = shifted(corner, GRID_COLS + 1)
    (pair,) = call(pair_kernel, [((4, 4, 256, 256), bf16)], keep, got, name="pair_sum")
    plane = lax.all_to_all(pair.reshape(16, 256, 256), ("y", "x"), 0, 0, tiled=True)
    (plane,) = call(plane_kernel, [((8, 2, 32, 128), f32)], plane, name="plane_sum")
    column = lax.all_to_all(plane.reshape(16, 32, 128), ("zl", "zh"), 0, 0, tiled=True)
    grad_w_qkv, grad_w_out = call(
        last_kernel, [((128, 24), f32), ((64, 16), f32)], column, name="column_sum"
    )
    output, grad_tokens = call(
        finish_kernel, [((CELLS, width), bf16), ((CELLS, width), bf16)],
        out_part, gtok_part, west, north, corner, name="finish",
    )
    return (
        output.reshape(tokens.shape), grad_tokens.reshape(tokens.shape), grad_w_qkv, grad_w_out
    )


def solution(mesh):
    fine = Mesh(mesh.devices.reshape(8, 4, 2, 4, 2), ("zl", "y", "c", "x", "zh"))
    fsdp = ("x", "zh")
    acts = P(fsdp, TILE_AXES, None, None, None)
    return jax.shard_map(
        per_device,
        mesh=fine,
        in_specs=(
            acts, P(fsdp, None), P(fsdp, None), P(), P(TILE_AXES, None), P(TILE_AXES), acts,
        ),
        out_specs=(acts, acts, P(fsdp, TILE_AXES), P(fsdp, TILE_AXES)),
        check_vma=False,
    )
```

time: 984 us -> 201 us (0.20)
  the two profiles are of different devices: /device:TPU:4 before, /device:TPU:2 now
where the time goes in v1:
time: 201 us; the launch traced here: 200 us
  blocking collectives  65.4 us (33%)
  starting transfers between devices  54.8 us (27%)
  Pallas kernels  40.3 us (20%)
  waiting for transfers between devices  23.7 us (12%)
  local copies, waits for them, and re-layouts  10.4 us (5%)
  matrix products  2.57 us (1%)
    pallas_call x8, Pallas kernels, call(): pl.pallas_call(kernel, out_shape=shapes, in_specs=specs, out_specs=[pl.Bl...  40.3 us
    all_to_all x1, blocking collectives, per_device(): lax.all_to_all(pair.reshape(16, 256, 256), ('y', 'x'), 0, 0, tiled=True)  33.6 us
    all_to_all x1, blocking collectives, per_device(): lax.all_to_all(jnp.broadcast_to(piece[None], (16, 2, 128, 256)), ('y', 'x...  31.9 us
    ppermute x6, starting transfers between devices, shifted(): lax.ppermute(block, TILE_AXES, [((i - distance) % count, i) for i in rang...  25.9 us
    ppermute x1, starting transfers between devices, per_device(): across = lax.ppermute(piece, 'zh', [(0, 1), (1, 0)])  15.7 us
    ppermute x6, waiting for transfers between devices, shifted(): lax.ppermute(block, TILE_AXES, [((i - distance) % count, i) for i in rang...  15.1 us
    all_to_all x1, starting transfers between devices, per_device(): lax.all_to_all(plane.reshape(16, 32, 128), ('zl', 'zh'), 0, 0, tiled=True)  9.36 us
    unnamed x25, local copies, waits for them, and re-layouts  7.35 us
  transfers between devices with their start and end apart: 10, of which 3 were waited for; matrix products, arithmetic and copies ran while one was open for 3% of the time, Pallas kernels for 6%

profile of v1, /device:TPU:2, one launch (start us, length us, event | category | flops | bytes accessed | tf_op | source)
XLA Modules:
  0.0 200.5 jit_solution(5979838970827780023)
XLA Ops:
  0.6 0.9 fusion.3
  1.5 0.9 fusion.1
  2.5 15.7 %collective-permute-start.3 = (bf16[128,256]{1,0:T(8,128)(2,1)S(1)}, bf16[128,256]{1,0:T(8,128)(2,1)S(1)}, u32[]{:S(2)}, u32[]{:S(2)}) collective-permute-start(bf16[128,256]{1,0:T(8,128)(2,1)S(1)} %fusion.1), channel_id=1, source_target_pairs={{0,1},{1,0},{2,3},{3,2},{4,5},{5,4},{6,7},{7,6},{8,9},{9,8},{10,11... | collective-permute-start | bytes 196616 | tf_op jit(solution)/shard_map/ppermute | solution.py:344
  18.2 4.2 %collective-permute-done.3 = bf16[128,256]{1,0:T(8,128)(2,1)S(1)} collective-permute-done((bf16[128,256]{1,0:T(8,128)(2,1)S(1)}, bf16[128,256]{1,0:T(8,128)(2,1)S(1)}, u32[]{:S(2)}, u32[]{:S(2)}) %collective-permute-start.3) | collective-permute-done | bytes 65568 | tf_op jit(solution)/shard_map/ppermute | solution.py:344
  22.4 0.2 broadcast_in_dim.5
  22.7 31.9 %all_to_all.15 = bf16[16,2,128,256]{3,2,1,0:T(8,128)(2,1)S(1)} all-to-all(bf16[16,2,128,256]{3,2,1,0:T(8,128)(2,1)S(1)} %broadcast_in_dim.5), channel_id=1, replica_groups=mesh['zl'=8,'y'=4,'c'=2,'x'=4,'zh'=2] {'y','x'}, dimensions={0} | all-to-all | bytes 4194304 | tf_op jit(solution)/shard_map/all_to_all | solution.py:347
  54.6 1.9 collective-permute-start.4
  56.5 0.6 reshape.132
  57.2 12.7 %collective-permute-start.2 = (bf16[2,16,1024]{2,1,0:T(8,128)(2,1)}, bf16[2,16,1024]{2,1,0:T(8,128)(2,1)}, u32[]{:S(2)}, u32[]{:S(2)}) collective-permute-start(bf16[2,16,1024]{2,1,0:T(8,128)(2,1)} %reshape.132), channel_id=1, source_target_pairs={{72,0},{80,8},{88,16},{96,24},{104,32},{112,40},{120,48},{128,56},... | collective-permute-start | bytes 196616 | tf_op jit(solution)/shard_map/ppermute | solution.py:328
  69.9 0.1 pad_maximum_fusion.1
  70.0 0.1 reshape.130
  70.1 3.0 %collective-permute-start = (bf16[2,48,1024]{2,1,0:T(8,128)(2,1)S(1)}, bf16[2,48,1024]{2,1,0:T(8,128)(2,1)S(1)}, u32[]{:S(2)}, u32[]{:S(2)}) collective-permute-start(bf16[2,48,1024]{2,1,0:T(8,128)(2,1)S(1)} %reshape.130), channel_id=1, source_target_pairs={{8,0},{16,8},{24,16},{32,24},{40,32},{48,40},{56,48},{64,56},{72,6... | collective-permute-start | bytes 589832 | tf_op jit(solution)/shard_map/ppermute | solution.py:328
  73.1 0.1 pad_maximum_fusion
  73.1 0.2 copy.13
  73.4 2.3 %collective-permute-start.1 = (bf16[2,48,1024]{2,1,0:T(8,128)(2,1)S(1)}, bf16[2,48,1024]{2,1,0:T(8,128)(2,1)S(1)}, u32[]{:S(2)}, u32[]{:S(2)}) collective-permute-start(bf16[2,48,1024]{2,1,0:T(8,128)(2,1)S(1)} %copy.14), channel_id=1, source_target_pairs={{64,0},{72,8},{80,16},{88,24},{96,32},{104,40},{112,48},{120,56},{... | collective-permute-start | bytes 589832 | tf_op jit(solution)/shard_map/ppermute | solution.py:328
  75.7 0.1 add_add_fusion
  75.8 0.1 add.63
  75.9 0.8 copy.15
  76.7 0.1 reshape.134
  76.8 2.6 %convolution_bitcast_fusion = f32[8,4096]{1,0:T(8,128)S(1)} fusion(f32[8,225]{1,0:T(8,128)S(1)} %reshape.134, s32[4096]{0:T(1024)S(1)} %add.63), kind=kOutput, calls=%fused_computation | convolution fusion | flops 89395200 | bytes 154656 | tf_op jit(solution)/shard_map/dot_general | solution.py:314
  80.1 0.8 reshape.135.bias_ref
  80.9 0.6 pad_add_fusion.ints_ref
  81.5 0.0 collective-permute-done.1.s_ref
  81.5 0.6 copy-done.5
  82.2 0.1 copy-done.6
  82.2 3.5 %prep.1 = (bf16[256,1024]{1,0:T(8,128)(2,1)}, f32[256,1024]{1,0:T(8,128)}, f32[256,128]{1,0:T(8,128)}, bf16[256,1024]{1,0:T(8,128)(2,1)}) custom-call(s32[5]{0:T(128)} %pad_add_fusion.ints_ref, bf16[256,1024]{1,0:T(8,128)(2,1)} %bitcast.22, bf16[256,1024]{1,0:T(8,128)(2,1)} %bitcast.27, bf16[2,48,1024]{2,1,0:T(8,128)(2,1)} %copy-done.5, ...), custom_call_target="tpu_custom_call" | custom-call | flops 402653184 | bytes 3735572 | tf_op jit(solution)/shard_map/prep/pallas_call | solution.py:291
  85.8 14.3 %attend.1 = (bf16[256,1536]{1,0:T(8,128)(2,1)}, bf16[256,512]{1,0:T(8,128)(2,1)}) custom-call(s32[5]{0:T(128)} %pad_add_fusion.ints_ref, bf16[256,1024]{1,0:T(8,128)(2,1)} %get-tuple-element.23.normed_ref, bf16[256,1024]{1,0:T(8,128)(2,1)} %get-tuple-element.24.rdy_ref, bf16[4,1024,256]{2,1,0:T(8,128)(2,1)} %bitcast.20, ...), custom_call_target="tpu_custom_call" | custom-call | flops 1073741824 | bytes 6422548 | tf_op jit(solution)/shard_map/attend/pallas_call | solution.py:291
  100.1 5.4 %weight_grads.1 = (bf16[4,4,256,256]{3,2,1,0:T(8,128)(2,1)}, bf16[4,4,256,256]{3,2,1,0:T(8,128)(2,1)}) custom-call(s32[5]{0:T(128)} %pad_add_fusion.ints_ref, bf16[256,1024]{1,0:T(8,128)(2,1)} %get-tuple-element.23.normed_ref, bf16[256,1024]{1,0:T(8,128)(2,1)} %get-tuple-element.24.rdy_ref, bf16[256,1536]{1,0:T(8,128)(2,1)} %get-tuple-element.25.dqkv_ref, ...), custom_call_target="tpu_custom_call" | custom-call | flops 1342177280 | bytes 6291476 | tf_op jit(solution)/shard_map/weight_grads/pallas_call | solution.py:291
  105.5 1.9 collective-permute-start.8
  107.4 4.3 %collective-permute-done.8.got_ref = bf16[4,4,256,256]{3,2,1,0:T(8,128)(2,1)S(1)} collective-permute-done((bf16[4,4,256,256]{3,2,1,0:T(8,128)(2,1)}, bf16[4,4,256,256]{3,2,1,0:T(8,128)(2,1)S(1)}, u32[]{:S(2)}, u32[]{:S(2)}) %collective-permute-start.8) | collective-permute-done | bytes 2097184 | tf_op jit(solution)/shard_map/ppermute | solution.py:376
  111.7 1.4 copy-done.3
  113.1 4.1 %pair_sum.1 = bf16[4,4,256,256]{3,2,1,0:T(8,128)(2,1)} custom-call(bf16[4,4,256,256]{3,2,1,0:T(8,128)(2,1)} %get-tuple-element.34.keep_ref, bf16[4,4,256,256]{3,2,1,0:T(8,128)(2,1)} %copy-done.3), custom_call_target="tpu_custom_call" | custom-call | bytes 6291456 | tf_op jit(solution)/shard_map/pair_sum/pallas_call | solution.py:291
  117.2 33.6 %all_to_all.16.got_ref = bf16[16,256,256]{2,1,0:T(8,128)(2,1)} all-to-all(bf16[16,256,256]{2,1,0:T(8,128)(2,1)} %bitcast.32), channel_id=1, replica_groups=mesh['zl'=8,'y'=4,'c'=2,'x'=4,'zh'=2] {'y','x'}, dimensions={0} | all-to-all | bytes 4194304 | tf_op jit(solution)/shard_map/all_to_all | solution.py:390
  150.7 2.6 %plane_sum.1 = f32[8,2,32,128]{3,2,1,0:T(8,128)} custom-call(bf16[16,256,256]{2,1,0:T(8,128)(2,1)} %all_to_all.16.got_ref), custom_call_target="tpu_custom_call" | custom-call | bytes 2359296 | tf_op jit(solution)/shard_map/plane_sum/pallas_call | solution.py:291
  153.3 9.4 %all-to-all-start.2 = ((f32[16,32,128]{2,1,0:T(8,128)}), f32[16,32,128]{2,1,0:T(8,128)S(1)}, u32[]{:S(2)}, u32[]{:S(2)}) async-start(f32[16,32,128]{2,1,0:T(8,128)} %bitcast.33), calls=%async_computation.2 | async-start | bytes 524288 | tf_op jit(solution)/shard_map/all_to_all | solution.py:392
  162.7 6.1 %home.1 = (bf16[256,1024]{1,0:T(8,128)(2,1)}, bf16[256,1024]{1,0:T(8,128)(2,1)}, bf16[2,48,1024]{2,1,0:T(8,128)(2,1)}, bf16[2,48,1024]{2,1,0:T(8,128)(2,1)}, bf16[2,16,1024]{2,1,0:T(8,128)(2,1)}) custom-call(s32[5]{0:T(128)} %pad_add_fusion.ints_ref, f32[256,1024]{1,0:T(8,128)} %get-tuple-element.21.normf_ref, f32[256,128]{1,0:T(8,128)} %get-tuple-element.22.inv_ref, ...), custom_call_target="tpu_custom_call" | custom-call | flops 1468006400 | bytes 8978452 | tf_op jit(solution)/shard_map/home/pallas_call | solution.py:291
  168.8 1.9 collective-permute-start.5
  170.7 3.8 %collective-permute-start.6 = (bf16[2,48,1024]{2,1,0:T(8,128)(2,1)}, bf16[2,48,1024]{2,1,0:T(8,128)(2,1)S(1)}, u32[]{:S(2)}, u32[]{:S(2)}) collective-permute-start(bf16[2,48,1024]{2,1,0:T(8,128)(2,1)} %get-tuple-element.30), channel_id=1, source_target_pairs={{448,0},{456,8},{464,16},{472,24},{480,32},{488,40},{496,48},{504,... | collective-permute-start | bytes 589832 | tf_op jit(solution)/shard_map/ppermute | solution.py:328
  174.5 2.1 %collective-permute-start.7 = (bf16[2,16,1024]{2,1,0:T(8,128)(2,1)}, bf16[2,16,1024]{2,1,0:T(8,128)(2,1)S(1)}, u32[]{:S(2)}, u32[]{:S(2)}) collective-permute-start(bf16[2,16,1024]{2,1,0:T(8,128)(2,1)} %get-tuple-element.31), channel_id=1, source_target_pairs={{440,0},{448,8},{456,16},{464,24},{472,32},{480,40},{488,48},{496,... | collective-permute-start | bytes 196616 | tf_op jit(solution)/shard_map/ppermute | solution.py:328
  176.7 15.1 %collective-permute-done.7.corner_ref = bf16[2,16,1024]{2,1,0:T(8,128)(2,1)S(1)} collective-permute-done((bf16[2,16,1024]{2,1,0:T(8,128)(2,1)}, bf16[2,16,1024]{2,1,0:T(8,128)(2,1)S(1)}, u32[]{:S(2)}, u32[]{:S(2)}) %collective-permute-start.7) | collective-permute-done | bytes 65568 | tf_op jit(solution)/shard_map/ppermute | solution.py:328
  191.8 0.6 copy-done.9
  192.4 0.1 copy-done.7
  192.5 0.1 copy-done.8
  192.5 2.6 %finish.1 = (bf16[256,1024]{1,0:T(8,128)(2,1)}, bf16[256,1024]{1,0:T(8,128)(2,1)}) custom-call(bf16[256,1024]{1,0:T(8,128)(2,1)} %get-tuple-element.27.out_ref, bf16[256,1024]{1,0:T(8,128)(2,1)} %get-tuple-element.28.gtok_ref, bf16[2,48,1024]{2,1,0:T(8,128)(2,1)} %copy-done.7, bf16[2,48,1024]{2,1,0:T(8,128)(2,1)} %copy-done.8, bf16[2,16,1024]{2,1,0:T(8,128)(2,1)} %copy-done.9), custom_call_target="tpu_custom_call" | custom-call | bytes 2555904 | tf_op jit(solution)/shard_map/finish/pallas_call | solution.py:291
  195.1 0.7 copy-done.4
  195.8 1.7 column_sum.1
  197.5 1.5 copy.16
  199.1 1.4 copy.17
  (26 shorter events, 0.1 us)
Async XLA Ops:
  2.5 19.9 %collective-permute-start.3 = (bf16[128,256]{1,0:T(8,128)(2,1)S(1)}, bf16[128,256]{1,0:T(8,128)(2,1)S(1)}, u32[]{:S(2)}, u32[]{:S(2)}) collective-permute-start(bf16[128,256]{1,0:T(8,128)(2,1)S(1)} %fusion.1), channel_id=1, source_target_pairs={{0,1},{1,0},{2,3},{3,2},{4,5},{5,4},{6,7},{7,6},{8,9},{9,8},{10,11... | collective-permute-start | bytes 196616 | tf_op jit(solution)/shard_map/ppermute | solution.py:344
  22.7 33.8 %copy-start.1 = (bf16[1,1,16,16,1024]{4,3,2,1,0:T(8,128)(2,1)S(1)}, bf16[1,1,16,16,1024]{4,3,2,1,0:T(8,128)(2,1)}, u32[]{:S(2)}) copy-start(bf16[1,1,16,16,1024]{4,3,2,1,0:T(8,128)(2,1)} %param.7) | copy-start | bytes 1572868
  22.7 33.8 %copy-start.2 = (bf16[1,1,16,16,1024]{4,3,2,1,0:T(8,128)(2,1)S(1)}, bf16[1,1,16,16,1024]{4,3,2,1,0:T(8,128)(2,1)}, u32[]{:S(2)}) copy-start(bf16[1,1,16,16,1024]{4,3,2,1,0:T(8,128)(2,1)} %param.13) | copy-start | bytes 1572868
  54.6 18.6 %copy-start = (bf16[16,2,128,256]{3,2,1,0:T(8,128)(2,1)}, bf16[16,2,128,256]{3,2,1,0:T(8,128)(2,1)S(1)}, u32[]{:S(2)}) copy-start(bf16[16,2,128,256]{3,2,1,0:T(8,128)(2,1)S(1)} %all_to_all.15) | copy-start | bytes 6291460
  54.6 31.2 %collective-permute-start.4 = (bf16[4,1024,256]{2,1,0:T(8,128)(2,1)S(1)}, bf16[4,1024,256]{2,1,0:T(8,128)(2,1)}, u32[]{:S(2)}, u32[]{:S(2)}) collective-permute-start(bf16[4,1024,256]{2,1,0:T(8,128)(2,1)S(1)} %bitcast.19), channel_id=1, source_target_pairs={{0,8},{8,0},{1,9},{9,1},{2,10},{10,2},{3,11},{11,3},{4,12},{12,4},... | collective-permute-start | bytes 6291464 | tf_op jit(solution)/shard_map/ppermute | solution.py:350
  57.2 24.3 %collective-permute-start.2 = (bf16[2,16,1024]{2,1,0:T(8,128)(2,1)}, bf16[2,16,1024]{2,1,0:T(8,128)(2,1)}, u32[]{:S(2)}, u32[]{:S(2)}) collective-permute-start(bf16[2,16,1024]{2,1,0:T(8,128)(2,1)} %reshape.132), channel_id=1, source_target_pairs={{72,0},{80,8},{88,16},{96,24},{104,32},{112,40},{120,48},{128,56},... | collective-permute-start | bytes 196616 | tf_op jit(solution)/shard_map/ppermute | solution.py:328
  70.0 10.9 %copy-start.10 = (s32[1,3]{1,0:T(1,128)S(1)}, s32[1,3]{1,0:T(1,128)}, u32[]{:S(2)}) copy-start(s32[1,3]{1,0:T(1,128)} %param.11) | copy-start | bytes 40
  70.1 11.4 %collective-permute-start = (bf16[2,48,1024]{2,1,0:T(8,128)(2,1)S(1)}, bf16[2,48,1024]{2,1,0:T(8,128)(2,1)S(1)}, u32[]{:S(2)}, u32[]{:S(2)}) collective-permute-start(bf16[2,48,1024]{2,1,0:T(8,128)(2,1)S(1)} %reshape.130), channel_id=1, source_target_pairs={{8,0},{16,8},{24,16},{32,24},{40,32},{48,40},{56,48},{64,56},{72,6... | collective-permute-start | bytes 589832 | tf_op jit(solution)/shard_map/ppermute | solution.py:328
  73.4 8.1 %collective-permute-start.1 = (bf16[2,48,1024]{2,1,0:T(8,128)(2,1)S(1)}, bf16[2,48,1024]{2,1,0:T(8,128)(2,1)S(1)}, u32[]{:S(2)}, u32[]{:S(2)}) collective-permute-start(bf16[2,48,1024]{2,1,0:T(8,128)(2,1)S(1)} %copy.14), channel_id=1, source_target_pairs={{64,0},{72,8},{80,16},{88,24},{96,32},{104,40},{112,48},{120,56},{... | collective-permute-start | bytes 589832 | tf_op jit(solution)/shard_map/ppermute | solution.py:328
  81.5 0.7 copy-start.5
  81.5 0.7 copy-start.6
  105.5 6.3 %collective-permute-start.8 = (bf16[4,4,256,256]{3,2,1,0:T(8,128)(2,1)}, bf16[4,4,256,256]{3,2,1,0:T(8,128)(2,1)S(1)}, u32[]{:S(2)}, u32[]{:S(2)}) collective-permute-start(bf16[4,4,256,256]{3,2,1,0:T(8,128)(2,1)} %get-tuple-element.35), channel_id=1, source_target_pairs={{0,8},{8,0},{1,9},{9,1},{2,10},{10,2},{3,11},{11,3},{4,12},{12,4},... | collective-permute-start | bytes 6291464 | tf_op jit(solution)/shard_map/ppermute | solution.py:376
  111.7 1.4 copy-start.3
  153.3 41.8 %all-to-all-start.2 = ((f32[16,32,128]{2,1,0:T(8,128)}), f32[16,32,128]{2,1,0:T(8,128)S(1)}, u32[]{:S(2)}, u32[]{:S(2)}) async-start(f32[16,32,128]{2,1,0:T(8,128)} %bitcast.33), calls=%async_computation.2 | async-start | bytes 524288 | tf_op jit(solution)/shard_map/all_to_all | solution.py:392
  168.8 23.0 %collective-permute-start.5 = (bf16[2,48,1024]{2,1,0:T(8,128)(2,1)}, bf16[2,48,1024]{2,1,0:T(8,128)(2,1)S(1)}, u32[]{:S(2)}, u32[]{:S(2)}) collective-permute-start(bf16[2,48,1024]{2,1,0:T(8,128)(2,1)} %get-tuple-element.29), channel_id=1, source_target_pairs={{504,0},{0,8},{8,16},{16,24},{24,32},{32,40},{40,48},{48,56},{56,6... | collective-permute-start | bytes 589832 | tf_op jit(solution)/shard_map/ppermute | solution.py:328
  170.7 21.1 %collective-permute-start.6 = (bf16[2,48,1024]{2,1,0:T(8,128)(2,1)}, bf16[2,48,1024]{2,1,0:T(8,128)(2,1)S(1)}, u32[]{:S(2)}, u32[]{:S(2)}) collective-permute-start(bf16[2,48,1024]{2,1,0:T(8,128)(2,1)} %get-tuple-element.30), channel_id=1, source_target_pairs={{448,0},{456,8},{464,16},{472,24},{480,32},{488,40},{496,48},{504,... | collective-permute-start | bytes 589832 | tf_op jit(solution)/shard_map/ppermute | solution.py:328
  174.5 17.2 %collective-permute-start.7 = (bf16[2,16,1024]{2,1,0:T(8,128)(2,1)}, bf16[2,16,1024]{2,1,0:T(8,128)(2,1)S(1)}, u32[]{:S(2)}, u32[]{:S(2)}) collective-permute-start(bf16[2,16,1024]{2,1,0:T(8,128)(2,1)} %get-tuple-element.31), channel_id=1, source_target_pairs={{440,0},{448,8},{456,16},{464,24},{472,32},{480,40},{488,48},{496,... | collective-permute-start | bytes 196616 | tf_op jit(solution)/shard_map/ppermute | solution.py:328
  191.7 0.6 copy-start.9
  191.7 0.7 copy-start.7
  191.8 0.8 copy-start.8
  195.1 0.7 copy-start.4

commit v2 on v1

--- a/solution.py
+++ b/solution.py
@@ -96,7 +96,7 @@
     return onehot(index == lax.broadcasted_iota(jnp.int32, (CELLS, 128), 1))
 
 
-def prep_kernel(ints_ref, tok_ref, dy_ref, e_ref, s_ref, c_ref, normed_ref, normf_ref, inv_ref, rdy_ref):
+def prep_kernel(ints_ref, tok_ref, dy_ref, e_ref, s_ref, c_ref, sides_ref, normf_ref, inv_ref):
     codes = [ints_ref[k] for k in range(3)]
     own, halo = gather_matrices(codes)
     pad = jnp.zeros((128 - 2 * EAST - CORNER, tok_ref.shape[1]), bf16)
@@ -111,64 +111,67 @@
     inverse = lax.rsqrt(variance + EPSILON)
     normed_f = center * inverse
     normf_ref[...] = normed_f
-    normed_ref[...] = normed_f.astype(bf16)
+    sides_ref[0] = normed_f.astype(bf16)
     inv_ref[...] = jnp.broadcast_to(inverse, inv_ref.shape)
-    rdy_ref[...] = region(dy_ref[...], 1).astype(bf16)
-
-
-def attention(open_flag, qkv, grad_heads, bias_ref, heads_ref, dqkv_ref):
-    rows = lax.broadcasted_iota(jnp.int32, (128, 128), 0)
-    cols = lax.broadcasted_iota(jnp.int32, (128, 128), 1)
-    same = (rows >> 6) == (cols >> 6)
+    sides_ref[1] = region(dy_ref[...], 1).astype(bf16)
+
+
+def attention(open_flag, qkv, grad_heads, bias_ref, back_ref):
+    keys = lax.broadcasted_iota(jnp.int32, (128, 128), 0)
+    queries = lax.broadcasted_iota(jnp.int32, (128, 128), 1)
+    lower = lax.broadcasted_iota(jnp.int32, (64, 128), 1) < 64
 
     def closed(place):
         inside = place & 63
         return (place >= 64) & ((inside >> 3) >= HALF) & ((inside & 7) >= HALF)
 
     shut = open_flag == 0
-    masks = [
-        jnp.where(same, 0.0, NEG),
-        jnp.where(same & jnp.logical_not(shut & closed(cols)), 0.0, NEG),
-    ]
-    place = lax.broadcasted_iota(jnp.int32, (128, 1), 0)
-    keep = jnp.where(shut & closed(place), 0.0, 1.0)
-    scale = HD ** (-0.5)
-    for block in range(2):
-        span = pl.ds(block * 128, 128)
-        for pair in range(HEADS // 2):
+    no_key = jnp.where(shut & closed(keys), NEG, 0.0)
+    query = lax.broadcasted_iota(jnp.int32, (1, 128), 1)
+    keep = jnp.where(shut & closed(query), 0.0, 1.0)
+    scale = jnp.asarray(HD ** (-0.5), bf16)
+    for pair in range(HEADS // 2):
+        tables = []
+        for one in range(2):
+            table = bias_ref[pair * 2 + one]
+            tables.append(jnp.concatenate([jnp.where(lower, table, NEG), jnp.where(lower, NEG, table)], axis=0))
+        units = [(block, one) for block in range(2) for one in range(2)]
+        q, k, v, g = [], [], [], []
+        for block, one in units:
+            span = pl.ds(block * 128, 128)
             wide = qkv[span, pl.ds(pair * 384, 384)]
-            grads = grad_heads[span, pl.ds(pair * 128, 128)]
-            outs, parts = [], []
-            for one in range(2):
-                head = pair * 2 + one
-                q = wide[:, one * 192 : one * 192 + 64]
-                k = wide[:, one * 192 + 64 : one * 192 + 128]
-                v = wide[:, one * 192 + 128 : one * 192 + 192]
-                g = grads[:, one * 64 : one * 64 + 64]
-                b64 = bias_ref[head]
-                b = jnp.concatenate([b64, b64], axis=1)
-                b = jnp.concatenate([b, b], axis=0)
-                s = mm(q, k, TRAILING) * scale + b + masks[block]
-                e = jnp.exp(s - jnp.max(s, -1, keepdims=True))
-                probs = e / jnp.sum(e, -1, keepdims=True)
-                if block == 1:
-                    probs = probs * keep
-                pb = probs.astype(bf16)
-                outs.append(mm(pb, v).astype(bf16))
-                dp = mm(g, v, TRAILING)
-                dv = mm(pb, g, LEADING).astype(bf16)
-                delta = jnp.sum(dp * probs, -1, keepdims=True)
-                ds = (probs * (dp - delta) * scale).astype(bf16)
-                dq = mm(ds, k).astype(bf16)
-                dk = mm(ds, q, LEADING).astype(bf16)
-                parts += [dq, dk, dv]
-            heads_ref[span, pl.ds(pair * 128, 128)] = jnp.concatenate(outs, axis=1)
-            dqkv_ref[span, pl.ds(pair * 384, 384)] = jnp.concatenate(parts, axis=1)
-
-
-def main_kernel(ints_ref, normed_ref, rdy_ref, mine_ref, other_ref, bias_ref, dqkv_ref, heads_ref, qkv_ref, gh_ref):
+            part = [wide[:, one * 192 + p * 64 : one * 192 + p * 64 + 64] for p in range(3)]
+            q.append(part[0] * scale)
+            k.append(part[1])
+            v.append(part[2])
+            g.append(grad_heads[span, pl.ds(pair * 128, 128)][:, one * 64 : one * 64 + 64])
+        n = range(4)
+        s = [mm(k[u], q[u], TRAILING) + tables[units[u][1]] for u in n]
+        s = [s[u] + no_key if units[u][0] == 1 else s[u] for u in n]
+        dp = [mm(v[u], g[u], TRAILING) for u in n]
+        e = [jnp.exp(s[u] - jnp.max(s[u], 0, keepdims=True)) for u in n]
+        r = [1.0 / jnp.sum(e[u], 0, keepdims=True) for u in n]
+        r = [r[u] * keep if units[u][0] == 1 else r[u] for u in n]
+        probs = [e[u] * r[u] for u in n]
+        pb = [probs[u].astype(bf16) for u in n]
+        ds = [
+            (probs[u] * (dp[u] - jnp.sum(dp[u] * probs[u], 0, keepdims=True))).astype(bf16) for u in n
+        ]
+        out = [mm(pb[u], v[u], LEADING).astype(bf16) for u in n]
+        dv = [mm(pb[u], g[u]).astype(bf16) for u in n]
+        dq = [mm(ds[u], k[u] * scale, LEADING).astype(bf16) for u in n]
+        dk = [mm(ds[u], q[u]).astype(bf16) for u in n]
+        for block in range(2):
+            span, u = pl.ds(block * 128, 128), block * 2
+            back_ref[span, pl.ds(1536 + pair * 128, 128)] = jnp.concatenate([out[u], out[u + 1]], axis=1)
+            back_ref[span, pl.ds(pair * 384, 384)] = jnp.concatenate(
+                [dq[u], dk[u], dv[u], dq[u + 1], dk[u + 1], dv[u + 1]], axis=1
+            )
+
+
+def main_kernel(ints_ref, sides_ref, mine_ref, other_ref, bias_ref, back_ref, qkv_ref, gh_ref):
     core = ints_ref[4]
-    normed = normed_ref[...]
+    normed = sides_ref[0]
     for ref, owner in ((mine_ref, core), (other_ref, 1 - core)):
         for y in range(3):
             start = pl.multiple_of((y * 2 + owner) * 256, 256)
@@ -176,12 +179,11 @@
     total = None
     for ref, owner in ((mine_ref, core), (other_ref, 1 - core)):
         for half in range(2):
-            block = out_block(ref, half)
             start = pl.multiple_of(half * 512 + owner * 256, 256)
-            term = mm(rdy_ref[:, pl.ds(start, 256)], block, TRAILING)
+            term = mm(sides_ref[1, :, pl.ds(start, 256)], out_block(ref, half), TRAILING)
             total = term if total is None else total + term
     gh_ref[...] = total.astype(bf16)
-    attention(ints_ref[3], qkv_ref, gh_ref, bias_ref, heads_ref, dqkv_ref)
+    attention(ints_ref[3], qkv_ref, gh_ref, bias_ref, back_ref)
 
 
 def out_block(ref, half):
@@ -189,19 +191,20 @@
 
 
 def home_kernel(
-    ints_ref, normf_ref, inv_ref, tok_ref, dy_ref, mine_ref, other_ref, dqkv_ref, heads_ref,
+    ints_ref, normf_ref, inv_ref, tok_ref, dy_ref, mine_ref, other_ref, back_ref,
     out_ref, gtok_ref, east_ref, south_ref, corner_ref, branch_ref,
 ):
     core = ints_ref[4]
     own, halo = scatter_matrices([ints_ref[k] for k in range(3)])
+    heads = back_ref[:, 1536:]
     dnormed = None
     for ref, owner in ((mine_ref, core), (other_ref, 1 - core)):
         for half in range(2):
             start = pl.multiple_of(half * 512 + owner * 256, 256)
-            branch_ref[:, pl.ds(start, 256)] = mm(heads_ref[...], out_block(ref, half)).astype(bf16)
+            branch_ref[:, pl.ds(start, 256)] = mm(heads, out_block(ref, half)).astype(bf16)
         for y in range(3):
             start = pl.multiple_of((y * 2 + owner) * 256, 256)
-            term = mm(dqkv_ref[:, pl.ds(start, 256)], ref[y], TRAILING)
+            term = mm(back_ref[:, pl.ds(start, 256)], ref[y], TRAILING)
             dnormed = term if dnormed is None else dnormed + term
 
     def edges(which, values):
@@ -233,53 +236,58 @@
         result[...] = (part[...].astype(f32) + mm(place, edge)).astype(bf16)
 
 
-def grads_kernel(ints_ref, normed_ref, rdy_ref, dqkv_ref, heads_ref, send_ref, keep_ref, tq_ref, to_ref):
+def grads_kernel(ints_ref, sides_ref, back_ref, peer_sides_ref, peer_back_ref, out_ref, tq_ref, to_ref):
     core = ints_ref[4]
-    tq_ref[...] = mm(dqkv_ref[...], normed_ref[...], LEADING)
-    heads = heads_ref[...]
+
+    def two(ref, peer_ref, index):
+        return jnp.concatenate([ref[index], peer_ref[index]], axis=0)
+
+    back = (slice(None), slice(0, 1536))
+    tq_ref[...] = mm(two(back_ref, peer_back_ref, back), two(sides_ref, peer_sides_ref, 0), LEADING)
+    heads = two(back_ref, peer_back_ref, (slice(None), slice(1536, 2048)))
     twice = []
     for head in range(HEADS):
         one = heads[:, head * HD : (head + 1) * HD]
         twice += [one, one]
-    to_ref[...] = mm(rdy_ref[...], jnp.concatenate(twice, axis=1), LEADING)
+    to_ref[...] = mm(two(sides_ref, peer_sides_ref, 1), jnp.concatenate(twice, axis=1), LEADING)
     lower = lax.broadcasted_iota(jnp.int32, (8, 256), 1) & 127 < 64
-    for out_ref, owner in ((send_ref, 1 - core), (keep_ref, core)):
-        for y in range(4):
-            for x in range(4):
-                lanes = pl.ds(x * 256, 256)
-                rows = [
-                    tq_ref[pl.ds(pl.multiple_of(z * 192 + y * 48 + owner * 24, 8), 24), lanes]
-                    for z in range(8)
-                ]
-                for z in range(8):
-                    start = z * 128 + y * 32 + owner * 16
-                    low = to_ref[pl.ds(pl.multiple_of(start, 8), 8), lanes]
-                    high = to_ref[pl.ds(pl.multiple_of(start + 8, 8), 8), lanes]
-                    rows.append(jnp.where(lower, low, high))
-                out_ref[y, x] = jnp.concatenate(rows, axis=0).astype(bf16)
-
-
-def pair_kernel(keep_ref, got_ref, out_ref):
-    out_ref[...] = (keep_ref[...].astype(f32) + got_ref[...].astype(f32)).astype(bf16)
-
-
-def plane_kernel(got_ref, out_ref):
+    for y in range(4):
+        for x in range(4):
+            lanes = pl.ds(x * 256, 256)
+            rows = [
+                tq_ref[pl.ds(pl.multiple_of(z * 192 + y * 48 + core * 24, 8), 24), lanes]
+                for z in range(8)
+            ]
+            for z in range(8):
+                start = z * 128 + y * 32 + core * 16
+                low = to_ref[pl.ds(pl.multiple_of(start, 8), 8), lanes]
+                high = to_ref[pl.ds(pl.multiple_of(start + 8, 8), 8), lanes]
+                rows.append(jnp.where(lower, low, high))
+            out_ref[y, x] = jnp.concatenate(rows, axis=0).astype(bf16)
+
+
+def plane_kernel(got_ref, out_ref, total_ref):
+    step = pl.program_id(0)
     total = got_ref[0].astype(f32)
     for part in range(1, 16):
         total = total + got_ref[part].astype(f32)
-    for z in range(8):
-        rows = jnp.concatenate([total[z * 24 : z * 24 + 24], total[192 + z * 8 : 200 + z * 8]], axis=0)
-        out_ref[z, 0] = rows[:, :128]
-        out_ref[z, 1] = rows[:, 128:]
+    total_ref[pl.ds(pl.multiple_of(step * 64, 64), 64)] = total
+
+    @pl.when(step == 3)
+    def _():
+        for z in range(8):
+            for half in range(2):
+                lanes = pl.ds(half * 128, 128)
+                out_ref[z, half, :24] = total_ref[pl.ds(z * 24, 24), lanes]
+                out_ref[z, half, 24:] = total_ref[pl.ds(192 + z * 8, 8), lanes]
 
 
 def last_kernel(got_ref, gq_ref, go_ref):
     total = got_ref[0]
     for part in range(1, 16):
         total = total + got_ref[part]
-    square = jnp.concatenate([total, jnp.zeros((96, 128), f32)], axis=0).T
-    gq_ref[...] = square[:, :24]
-    go_ref[...] = jnp.concatenate([square[:64, 24:32], square[64:, 24:32]], axis=1)
+    gq_ref[...] = total[:24]
+    go_ref[...] = jnp.concatenate([total[24:, :64], total[24:, 64:]], axis=0)
 
 
 def call(kernel, outs, *args, smem=0, scratch=(), flops=0, name=None):
@@ -305,8 +313,8 @@
     places = jnp.arange(WIN * WIN, dtype=jnp.int32)
     row_of = places // WIN
     col_of = places % WIN
-    offset = (row_of[:, None] - row_of[None, :] + WIN - 1) * span + (
-        col_of[:, None] - col_of[None, :] + WIN - 1
+    offset = (row_of[None, :] - row_of[:, None] + WIN - 1) * span + (
+        col_of[None, :] - col_of[:, None] + WIN - 1
     )
     onehot_table = (
         offset.reshape(-1)[:, None] == jnp.arange(span * span, dtype=jnp.int32)[None, :]
@@ -317,7 +325,8 @@
         precision=lax.Precision.HIGHEST,
         preferred_element_type=f32,
     )
-    return picked.T.reshape(HEADS, WIN * WIN, WIN * WIN)
+    table = picked.T.reshape(HEADS, WIN * WIN, WIN * WIN)
+    return jnp.concatenate([table, table], axis=2)
 
 
 TILE_AXES = ("zl", "y", "c")
@@ -344,61 +353,76 @@
     across = lax.ppermute(piece, "zh", [(0, 1), (1, 0)])
     first = lax.axis_index("zh") == 0
     piece = jnp.stack([jnp.where(first, piece, across), jnp.where(first, across, piece)])
-    mine = lax.all_to_all(
-        jnp.broadcast_to(piece[None], (16, 2, 128, 256)), ("y", "x"), 0, 0, tiled=True
-    ).reshape(4, width, 256)
-    other = lax.ppermute(mine, "c", [(0, 1), (1, 0)])
+    many = jnp.broadcast_to(piece[None], (16, 2, 128, 256))
+    bias = position_bias(rel_bias)
+    many, both, bias, ints = lax.optimization_barrier((many, both, bias, ints))
+    mine = lax.all_to_all(many, ("y", "x"), 0, 0, tiled=True).reshape(4, width, 256)
+
+    def swapped(block):
+        return lax.ppermute(block, "c", [(0, 1), (1, 0)])
 
     east = shifted(both[:, HALF:, :HALF].reshape(2, EAST, width), -1)
     south = shifted(both[:, :HALF, HALF:].reshape(2, EAST, width), -GRID_COLS)
     corner = shifted(both[:, :HALF, :HALF].reshape(2, CORNER, width), -(GRID_COLS + 1))
-    bias = position_bias(rel_bias)
-    normed, normed_f, inverse, region_dy = call(
+    sides, normed_f, inverse = call(
         prep_kernel,
-        [((CELLS, width), bf16), ((CELLS, width), f32), ((CELLS, 128), f32), ((CELLS, width), bf16)],
+        [((2, CELLS, width), bf16), ((CELLS, width), f32), ((CELLS, 128), f32)],
         ints, tok, dy, east, south, corner,
         smem=1, flops=4 * 256 * 384 * 1024, name="prep",
     )
-    dqkv, heads = call(
+    mine, sides = lax.optimization_barrier((mine, sides))
+    other = swapped(mine)
+    peer_sides = swapped(sides)
+    (back,) = call(
         main_kernel,
-        [((CELLS, 1536), bf16), ((CELLS, 512), bf16)],
-        ints, normed, region_dy, mine, other, bias,
+        [((CELLS, 2048), bf16)],
+        ints, sides, mine, other, bias,
         smem=1, scratch=[pltpu.VMEM((CELLS, 1536), bf16), pltpu.VMEM((CELLS, 512), bf16)],
         flops=2 * 256 * 1024 * 2048, name="attend",
     )
-    send, keep = call(
+    peer_back = swapped(back)
+    (pair,) = call(
         grads_kernel,
-        [((4, 4, 256, 256), bf16), ((4, 4, 256, 256), bf16)],
-        ints, normed, region_dy, dqkv, heads,
+        [((4, 4, 256, 256), bf16)],
+        ints, sides, back, peer_sides, peer_back,
         smem=1, scratch=[pltpu.VMEM((1536, 1024), f32), pltpu.VMEM((1024, 1024), f32)],
-        flops=2 * 256 * 1024 * 2560, name="weight_grads",
-    )
-    got = lax.ppermute(send, "c", [(0, 1), (1, 0)])
+        flops=2 * 512 * 1024 * 2560, name="weight_grads",
+    )
     out_part, gtok_part, east, south, corner = call(
         home_kernel,
         [
             ((CELLS, width), bf16), ((CELLS, width), bf16),
             ((2, EAST, width), bf16), ((2, EAST, width), bf16), ((2, CORNER, width), bf16),
         ],
-        ints, normed_f, inverse, tok, dy, mine, other, dqkv, heads,
+        ints, normed_f, inverse, tok, dy, mine, other, back,
         smem=1, scratch=[pltpu.VMEM((CELLS, width), bf16)], flops=2 * 256 * 1024 * 2800, name="home",
     )
     west = shifted(east, 1)
     north = shifted(south, GRID_COLS)
     corner = shifted(corner, GRID_COLS + 1)
-    (pair,) = call(pair_kernel, [((4, 4, 256, 256), bf16)], keep, got, name="pair_sum")
     plane = lax.all_to_all(pair.reshape(16, 256, 256), ("y", "x"), 0, 0, tiled=True)
-    (plane,) = call(plane_kernel, [((8, 2, 32, 128), f32)], plane, name="plane_sum")
+    plane, west, north, corner = lax.optimization_barrier((plane, west, north, corner))
+    plane = pl.pallas_call(
+        plane_kernel,
+        grid=(4,),
+        out_shape=jax.ShapeDtypeStruct((8, 2, 32, 128), f32),
+        in_specs=[pl.BlockSpec((16, 64, 256), lambda i: (0, i, 0))],
+        out_specs=pl.BlockSpec((8, 2, 32, 128), lambda i: (0, 0, 0, 0)),
+        scratch_shapes=[pltpu.VMEM((256, 256), f32)],
+        compiler_params=pltpu.CompilerParams(vmem_limit_bytes=VMEM_LIMIT),
+        cost_estimate=pl.CostEstimate(flops=0, bytes_accessed=2**21, transcendentals=0),
+        name="plane_sum",
+    )(plane)
     column = lax.all_to_all(plane.reshape(16, 32, 128), ("zl", "zh"), 0, 0, tiled=True)
     grad_w_qkv, grad_w_out = call(
-        last_kernel, [((128, 24), f32), ((64, 16), f32)], column, name="column_sum"
+        last_kernel, [((24, 128), f32), ((16, 64), f32)], column, name="column_sum"
     )
     output, grad_tokens = call(
         finish_kernel, [((CELLS, width), bf16), ((CELLS, width), bf16)],
         out_part, gtok_part, west, north, corner, name="finish",
     )
     return (
-        output.reshape(tokens.shape), grad_tokens.reshape(tokens.shape), grad_w_qkv, grad_w_out
+        output.reshape(tokens.shape), grad_tokens.reshape(tokens.shape), grad_w_qkv.T, grad_w_out.T
     )
 
 

time: 201 us -> 166 us (0.83)
  the two profiles are of different devices: /device:TPU:2 before, /device:TPU:32 now
where the time goes in v2:
time: 166 us
  starting transfers between devices  65.8 us (40%)
  waiting for transfers between devices  51.1 us (31%)
  Pallas kernels  30.6 us (18%)
  local copies, waits for them, and re-layouts  11.4 us (7%)
  other arithmetic  2.57 us (2%)
  matrix products  2.56 us (2%)
    pallas_call x6, Pallas kernels, call(): pl.pallas_call(kernel, out_shape=shapes, in_specs=specs, out_specs=[pl.Bl...  27.4 us
    ppermute x6, starting transfers between devices, shifted(): lax.ppermute(block, TILE_AXES, [((i - distance) % count, i) for i in rang...  24.2 us
    all_to_all x1, waiting for transfers between devices, per_device(): lax.all_to_all(plane.reshape(16, 32, 128), ('zl', 'zh'), 0, 0, tiled=True)  17.6 us
    ppermute x6, waiting for transfers between devices, shifted(): lax.ppermute(block, TILE_AXES, [((i - distance) % count, i) for i in rang...  17 us
    ppermute x1, starting transfers between devices, per_device(): across = lax.ppermute(piece, 'zh', [(0, 1), (1, 0)])  14.8 us
    all_to_all x1, starting transfers between devices, per_device(): lax.all_to_all(plane.reshape(16, 32, 128), ('zl', 'zh'), 0, 0, tiled=True)  8.27 us
    all_to_all x1, starting transfers between devices, per_device(): lax.all_to_all(many, ('y', 'x'), 0, 0, tiled=True).reshape(4, width, 256)  7.03 us
    ppermute x3, starting transfers between devices, swapped(): return lax.ppermute(block, 'c', [(0, 1), (1, 0)])  6.34 us
  transfers between devices with their start and end apart: 13, of which 7 were waited for; matrix products, arithmetic and copies ran while one was open for 5% of the time, Pallas kernels for 12%

profile of v2, /device:TPU:32, one launch (start us, length us, event | category | flops | bytes accessed | tf_op | source)
XLA Modules:
  0.0 165.6 jit_solution(6309744167593496110)
XLA Ops:
  0.7 1.0 fusion.3
  1.6 0.9 fusion.1
  2.6 14.8 %collective-permute-start = (bf16[128,256]{1,0:T(8,128)(2,1)S(1)}, bf16[128,256]{1,0:T(8,128)(2,1)S(1)}, u32[]{:S(2)}, u32[]{:S(2)}) collective-permute-start(bf16[128,256]{1,0:T(8,128)(2,1)S(1)} %fusion.1), channel_id=1, source_target_pairs={{0,1},{1,0},{2,3},{3,2},{4,5},{5,4},{6,7},{7,6},{8,9},{9,8},{10,11... | collective-permute-start | bytes 196616 | tf_op jit(solution)/shard_map/ppermute | solution.py:353
  17.4 0.8 copy.11
  18.3 0.1 reshape.128
  18.4 0.1 add_add_fusion
  18.5 0.1 add.63
  18.5 2.6 %convolution_bitcast_fusion = f32[8,4096]{1,0:T(8,128)S(1)} fusion(f32[8,225]{1,0:T(8,128)S(1)} %reshape.128, s32[4096]{0:T(1024)S(1)} %add.63), kind=kOutput, calls=%fused_computation | convolution fusion | flops 89395200 | bytes 154656 | tf_op jit(solution)/shard_map/dot_general | solution.py:322
  21.1 0.1 reshape.129
  21.2 0.8 pad_maximum_fusion.1.bias_ref
  22.7 0.1 pad_maximum_fusion
  22.8 0.6 pad_add_fusion.ints_ref
  23.5 1.6 broadcast_in_dim.4
  25.1 7.0 %all-to-all-start = ((bf16[16,2,128,256]{3,2,1,0:T(8,128)(2,1)}), bf16[16,2,128,256]{3,2,1,0:T(8,128)(2,1)S(1)}, u32[]{:S(2)}, u32[]{:S(2)}) async-start(bf16[16,2,128,256]{3,2,1,0:T(8,128)(2,1)} %broadcast_in_dim.4), calls=%async_computation | async-start | bytes 4194304 | tf_op jit(solution)/shard_map/all_to_all | solution.py:359
  32.1 0.7 slice.17
  32.8 0.1 slice.18
  32.9 1.7 %reshape.132 = bf16[2,48,1024]{2,1,0:T(8,128)(2,1)} reshape(bf16[2,12,4,1024]{3,2,1,0:T(4,128)(2,1)} %slice.17) | data formatting | bytes 393216 | tf_op jit(solution)/shard_map/reshape | solution.py:364
  34.6 4.1 %collective-permute-start.1 = (bf16[2,48,1024]{2,1,0:T(8,128)(2,1)}, bf16[2,48,1024]{2,1,0:T(8,128)(2,1)}, u32[]{:S(2)}, u32[]{:S(2)}) collective-permute-start(bf16[2,48,1024]{2,1,0:T(8,128)(2,1)} %reshape.132), channel_id=1, source_target_pairs={{8,0},{16,8},{24,16},{32,24},{40,32},{48,40},{56,48},{64,56},{72,6... | collective-permute-start | bytes 589832 | tf_op jit(solution)/shard_map/ppermute | solution.py:337
  38.7 0.2 copy.12
  38.9 5.7 %collective-permute-start.2 = (bf16[2,48,1024]{2,1,0:T(8,128)(2,1)S(1)}, bf16[2,48,1024]{2,1,0:T(8,128)(2,1)}, u32[]{:S(2)}, u32[]{:S(2)}) collective-permute-start(bf16[2,48,1024]{2,1,0:T(8,128)(2,1)S(1)} %copy.13), channel_id=1, source_target_pairs={{64,0},{72,8},{80,16},{88,24},{96,32},{104,40},{112,48},{120,56},{... | collective-permute-start | bytes 589832 | tf_op jit(solution)/shard_map/ppermute | solution.py:337
  44.6 5.4 %collective-permute-start.3 = (bf16[2,16,1024]{2,1,0:T(8,128)(2,1)S(1)}, bf16[2,16,1024]{2,1,0:T(8,128)(2,1)S(1)}, u32[]{:S(2)}, u32[]{:S(2)}) collective-permute-start(bf16[2,16,1024]{2,1,0:T(8,128)(2,1)S(1)} %reshape.134), channel_id=1, source_target_pairs={{72,0},{80,8},{88,16},{96,24},{104,32},{112,40},{120,48},{128,56},... | collective-permute-start | bytes 196616 | tf_op jit(solution)/shard_map/ppermute | solution.py:337
  50.0 3.4 %collective-permute-done.3.c_ref = bf16[2,16,1024]{2,1,0:T(8,128)(2,1)S(1)} collective-permute-done((bf16[2,16,1024]{2,1,0:T(8,128)(2,1)S(1)}, bf16[2,16,1024]{2,1,0:T(8,128)(2,1)S(1)}, u32[]{:S(2)}, u32[]{:S(2)}) %collective-permute-start.3) | collective-permute-done | bytes 65568 | tf_op jit(solution)/shard_map/ppermute | solution.py:337
  53.4 0.6 copy-done.9
  54.0 3.6 %prep.1 = (bf16[2,256,1024]{2,1,0:T(8,128)(2,1)}, f32[256,1024]{1,0:T(8,128)}, f32[256,128]{1,0:T(8,128)}) custom-call(s32[5]{0:T(128)} %pad_add_fusion.ints_ref, bf16[256,1024]{1,0:T(8,128)(2,1)} %bitcast.24, bf16[256,1024]{1,0:T(8,128)(2,1)} %bitcast.27, bf16[2,48,1024]{2,1,0:T(8,128)(2,1)} %collective-permute-done.1.e_ref, ...), custom_call_target="tpu_custom_call" | custom-call | flops 402653184 | bytes 3735572 | tf_op jit(solution)/shard_map/prep/pallas_call | solution.py:299
  57.6 6.3 %all-to-all-done = bf16[16,2,128,256]{3,2,1,0:T(8,128)(2,1)S(1)} async-done(((bf16[16,2,128,256]{3,2,1,0:T(8,128)(2,1)}), bf16[16,2,128,256]{3,2,1,0:T(8,128)(2,1)S(1)}, u32[]{:S(2)}, u32[]{:S(2)}) %all-to-all-start) | async-done | bytes 2097184 | tf_op jit(solution)/shard_map/all_to_all | solution.py:359
  63.9 1.9 %collective-permute-start.4 = (bf16[4,1024,256]{2,1,0:T(8,128)(2,1)S(1)}, bf16[4,1024,256]{2,1,0:T(8,128)(2,1)S(1)}, u32[]{:S(2)}, u32[]{:S(2)}) collective-permute-start(bf16[4,1024,256]{2,1,0:T(8,128)(2,1)S(1)} %bitcast.21), channel_id=1, source_target_pairs={{0,8},{8,0},{1,9},{9,1},{2,10},{10,2},{3,11},{11,3},{4,12},{12,4},... | collective-permute-start | bytes 6291464 | tf_op jit(solution)/shard_map/ppermute | solution.py:362
  65.8 2.4 %collective-permute-start.5 = (bf16[2,256,1024]{2,1,0:T(8,128)(2,1)}, bf16[2,256,1024]{2,1,0:T(8,128)(2,1)S(1)}, u32[]{:S(2)}, u32[]{:S(2)}) collective-permute-start(bf16[2,256,1024]{2,1,0:T(8,128)(2,1)} %get-tuple-element.33.sides_ref), channel_id=1, source_target_pairs={{0,8},{8,0},{1,9},{9,1},{2,10},{10,2},{3,11},{11,3},{4,12},{12,4},... | collective-permute-start | bytes 3145736 | tf_op jit(solution)/shard_map/ppermute | solution.py:362
  68.2 1.7 %collective-permute-done.4.other_ref = bf16[4,1024,256]{2,1,0:T(8,128)(2,1)S(1)} collective-permute-done((bf16[4,1024,256]{2,1,0:T(8,128)(2,1)S(1)}, bf16[4,1024,256]{2,1,0:T(8,128)(2,1)S(1)}, u32[]{:S(2)}, u32[]{:S(2)}) %collective-permute-start.4) | collective-permute-done | bytes 2097184 | tf_op jit(solution)/shard_map/ppermute | solution.py:362
  69.9 1.4 copy-done.2
  71.3 6.9 %attend.1.back_ref = bf16[256,2048]{1,0:T(8,128)(2,1)} custom-call(s32[5]{0:T(128)} %pad_add_fusion.ints_ref, bf16[2,256,1024]{2,1,0:T(8,128)(2,1)} %get-tuple-element.33.sides_ref, bf16[4,1024,256]{2,1,0:T(8,128)(2,1)} %bitcast.22, bf16[4,1024,256]{2,1,0:T(8,128)(2,1)} %copy-done.2, f32[8,64,128]{2,1,0:T(8,128)} %pad_maximum_fusion.1.bias_ref), custom_call_target="tpu_custom_call" | custom-call | flops 1073741824 | bytes 6553620 | tf_op jit(solution)/shard_map/attend/pallas_call | solution.py:299
  78.1 2.0 %collective-permute-start.6 = (bf16[256,2048]{1,0:T(8,128)(2,1)}, bf16[256,2048]{1,0:T(8,128)(2,1)S(1)}, u32[]{:S(2)}, u32[]{:S(2)}) collective-permute-start(bf16[256,2048]{1,0:T(8,128)(2,1)} %attend.1.back_ref), channel_id=1, source_target_pairs={{0,8},{8,0},{1,9},{9,1},{2,10},{10,2},{3,11},{11,3},{4,12},{12,4},... | collective-permute-start | bytes 3145736 | tf_op jit(solution)/shard_map/ppermute | solution.py:362
  80.2 2.7 %collective-permute-done.6.peer_back_ref = bf16[256,2048]{1,0:T(8,128)(2,1)S(1)} collective-permute-done((bf16[256,2048]{1,0:T(8,128)(2,1)}, bf16[256,2048]{1,0:T(8,128)(2,1)S(1)}, u32[]{:S(2)}, u32[]{:S(2)}) %collective-permute-start.6) | collective-permute-done | bytes 1048608 | tf_op jit(solution)/shard_map/ppermute | solution.py:362
  82.9 1.0 copy-done.12
  83.9 6.6 %weight_grads.1 = bf16[4,4,256,256]{3,2,1,0:T(8,128)(2,1)} custom-call(s32[5]{0:T(128)} %pad_add_fusion.ints_ref, bf16[2,256,1024]{2,1,0:T(8,128)(2,1)} %get-tuple-element.33.sides_ref, bf16[256,2048]{1,0:T(8,128)(2,1)} %attend.1.back_ref, bf16[2,256,1024]{2,1,0:T(8,128)(2,1)} %copy-done.11, bf16[256,2048]{1,0:T(8,128)(2,1)} %copy-done.12), custom_call_target="tpu_custom_call" | custom-call | flops 2684354560 | bytes 6291476 | tf_op jit(solution)/shard_map/weight_grads/pallas_call | solution.py:299
  90.5 5.1 %all-to-all-start.1 = ((bf16[16,256,256]{2,1,0:T(8,128)(2,1)}), bf16[16,256,256]{2,1,0:T(8,128)(2,1)S(1)}, u32[]{:S(2)}, u32[]{:S(2)}) async-start(bf16[16,256,256]{2,1,0:T(8,128)(2,1)} %bitcast.30), calls=%async_computation.1 | async-start | bytes 4194304 | tf_op jit(solution)/shard_map/all_to_all | solution.py:403
  95.6 6.1 %home.1 = (bf16[256,1024]{1,0:T(8,128)(2,1)}, bf16[256,1024]{1,0:T(8,128)(2,1)}, bf16[2,48,1024]{2,1,0:T(8,128)(2,1)}, bf16[2,48,1024]{2,1,0:T(8,128)(2,1)}, bf16[2,16,1024]{2,1,0:T(8,128)(2,1)}) custom-call(s32[5]{0:T(128)} %pad_add_fusion.ints_ref, f32[256,1024]{1,0:T(8,128)} %get-tuple-element.28.normf_ref, f32[256,128]{1,0:T(8,128)} %get-tuple-element.29.inv_ref, ...), custom_call_target="tpu_custom_call" | custom-call | flops 1468006400 | bytes 8978452 | tf_op jit(solution)/shard_map/home/pallas_call | solution.py:299
  101.7 2.0 %collective-permute-start.7 = (bf16[2,48,1024]{2,1,0:T(8,128)(2,1)}, bf16[2,48,1024]{2,1,0:T(8,128)(2,1)S(1)}, u32[]{:S(2)}, u32[]{:S(2)}) collective-permute-start(bf16[2,48,1024]{2,1,0:T(8,128)(2,1)} %get-tuple-element.37), channel_id=1, source_target_pairs={{504,0},{0,8},{8,16},{16,24},{24,32},{32,40},{40,48},{48,56},{56,6... | collective-permute-start | bytes 589832 | tf_op jit(solution)/shard_map/ppermute | solution.py:337
  103.7 2.9 %collective-permute-start.8 = (bf16[2,48,1024]{2,1,0:T(8,128)(2,1)}, bf16[2,48,1024]{2,1,0:T(8,128)(2,1)S(1)}, u32[]{:S(2)}, u32[]{:S(2)}) collective-permute-start(bf16[2,48,1024]{2,1,0:T(8,128)(2,1)} %get-tuple-element.38), channel_id=1, source_target_pairs={{448,0},{456,8},{464,16},{472,24},{480,32},{488,40},{496,48},{504,... | collective-permute-start | bytes 589832 | tf_op jit(solution)/shard_map/ppermute | solution.py:337
  106.6 4.2 %collective-permute-start.9 = (bf16[2,16,1024]{2,1,0:T(8,128)(2,1)}, bf16[2,16,1024]{2,1,0:T(8,128)(2,1)S(1)}, u32[]{:S(2)}, u32[]{:S(2)}) collective-permute-start(bf16[2,16,1024]{2,1,0:T(8,128)(2,1)} %get-tuple-element.39), channel_id=1, source_target_pairs={{440,0},{448,8},{456,16},{464,24},{472,32},{480,40},{488,48},{496,... | collective-permute-start | bytes 196616 | tf_op jit(solution)/shard_map/ppermute | solution.py:337
  110.9 13.6 %collective-permute-done.9.corner_ref = bf16[2,16,1024]{2,1,0:T(8,128)(2,1)S(1)} collective-permute-done((bf16[2,16,1024]{2,1,0:T(8,128)(2,1)}, bf16[2,16,1024]{2,1,0:T(8,128)(2,1)S(1)}, u32[]{:S(2)}, u32[]{:S(2)}) %collective-permute-start.9) | collective-permute-done | bytes 65568 | tf_op jit(solution)/shard_map/ppermute | solution.py:337
  124.5 5.7 %all-to-all-done.1.got_ref = bf16[16,256,256]{2,1,0:T(8,128)(2,1)S(1)} async-done(((bf16[16,256,256]{2,1,0:T(8,128)(2,1)}), bf16[16,256,256]{2,1,0:T(8,128)(2,1)S(1)}, u32[]{:S(2)}, u32[]{:S(2)}) %all-to-all-start.1) | async-done | bytes 2097184 | tf_op jit(solution)/shard_map/all_to_all | solution.py:403
  130.2 1.3 copy-done.1
  131.6 3.2 %plane_sum.1 = f32[8,2,32,128]{3,2,1,0:T(8,128)} custom-call(bf16[16,256,256]{2,1,0:T(8,128)(2,1)} %copy-done.1), custom_call_target="tpu_custom_call" | custom-call | bytes 2097152 | tf_op jit(solution)/shard_map/plane_sum/pallas_call | solution.py:405
  134.7 8.3 %all-to-all-start.2 = ((f32[16,32,128]{2,1,0:T(8,128)}), f32[16,32,128]{2,1,0:T(8,128)S(1)}, u32[]{:S(2)}, u32[]{:S(2)}) async-start(f32[16,32,128]{2,1,0:T(8,128)} %bitcast.31), calls=%async_computation.2 | async-start | bytes 524288 | tf_op jit(solution)/shard_map/all_to_all | solution.py:416
  143.0 2.6 %finish.1 = (bf16[256,1024]{1,0:T(8,128)(2,1)}, bf16[256,1024]{1,0:T(8,128)(2,1)}) custom-call(bf16[256,1024]{1,0:T(8,128)(2,1)} %get-tuple-element.35.out_ref, bf16[256,1024]{1,0:T(8,128)(2,1)} %get-tuple-element.36.gtok_ref, bf16[2,48,1024]{2,1,0:T(8,128)(2,1)} %copy-done.6, bf16[2,48,1024]{2,1,0:T(8,128)(2,1)} %copy-done.7, bf16[2,16,1024]{2,1,0:T(8,128)(2,1)} %copy-done.8), custom_call_target="tpu_custom_call" | custom-call | bytes 2555904 | tf_op jit(solution)/shard_map/finish/pallas_call | solution.py:299
  145.6 17.6 %all-to-all-done.2.got_ref = f32[16,32,128]{2,1,0:T(8,128)S(1)} async-done(((f32[16,32,128]{2,1,0:T(8,128)}), f32[16,32,128]{2,1,0:T(8,128)S(1)}, u32[]{:S(2)}, u32[]{:S(2)}) %all-to-all-start.2) | async-done | bytes 262176 | tf_op jit(solution)/shard_map/all_to_all | solution.py:416
  163.2 0.7 copy-done.5
  163.9 1.6 column_sum.1
  (33 shorter events, 0.2 us)
Async XLA Ops:
  0.6 22.1 %copy-start.4 = (bf16[1,1,16,16,1024]{4,3,2,1,0:T(8,128)(2,1)S(1)}, bf16[1,1,16,16,1024]{4,3,2,1,0:T(8,128)(2,1)}, u32[]{:S(2)}) copy-start(bf16[1,1,16,16,1024]{4,3,2,1,0:T(8,128)(2,1)} %param.13) | copy-start | bytes 1572868
  0.6 22.1 %copy-start.3 = (bf16[1,1,16,16,1024]{4,3,2,1,0:T(8,128)(2,1)S(1)}, bf16[1,1,16,16,1024]{4,3,2,1,0:T(8,128)(2,1)}, u32[]{:S(2)}) copy-start(bf16[1,1,16,16,1024]{4,3,2,1,0:T(8,128)(2,1)} %param.7) | copy-start | bytes 1572868
  2.6 20.9 %collective-permute-start = (bf16[128,256]{1,0:T(8,128)(2,1)S(1)}, bf16[128,256]{1,0:T(8,128)(2,1)S(1)}, u32[]{:S(2)}, u32[]{:S(2)}) collective-permute-start(bf16[128,256]{1,0:T(8,128)(2,1)S(1)} %fusion.1), channel_id=1, source_target_pairs={{0,1},{1,0},{2,3},{3,2},{4,5},{5,4},{6,7},{7,6},{8,9},{9,8},{10,11... | collective-permute-start | bytes 196616 | tf_op jit(solution)/shard_map/ppermute | solution.py:353
  18.4 4.5 %copy-start.10 = (s32[1,3]{1,0:T(1,128)S(1)}, s32[1,3]{1,0:T(1,128)}, u32[]{:S(2)}) copy-start(s32[1,3]{1,0:T(1,128)} %param.11) | copy-start | bytes 40
  25.1 38.8 %all-to-all-start = ((bf16[16,2,128,256]{3,2,1,0:T(8,128)(2,1)}), bf16[16,2,128,256]{3,2,1,0:T(8,128)(2,1)S(1)}, u32[]{:S(2)}, u32[]{:S(2)}) async-start(bf16[16,2,128,256]{3,2,1,0:T(8,128)(2,1)} %broadcast_in_dim.4), calls=%async_computation | async-start | bytes 4194304 | tf_op jit(solution)/shard_map/all_to_all | solution.py:359
  34.6 18.8 %collective-permute-start.1 = (bf16[2,48,1024]{2,1,0:T(8,128)(2,1)}, bf16[2,48,1024]{2,1,0:T(8,128)(2,1)}, u32[]{:S(2)}, u32[]{:S(2)}) collective-permute-start(bf16[2,48,1024]{2,1,0:T(8,128)(2,1)} %reshape.132), channel_id=1, source_target_pairs={{8,0},{16,8},{24,16},{32,24},{40,32},{48,40},{56,48},{64,56},{72,6... | collective-permute-start | bytes 589832 | tf_op jit(solution)/shard_map/ppermute | solution.py:337
  38.9 14.5 %collective-permute-start.2 = (bf16[2,48,1024]{2,1,0:T(8,128)(2,1)S(1)}, bf16[2,48,1024]{2,1,0:T(8,128)(2,1)}, u32[]{:S(2)}, u32[]{:S(2)}) collective-permute-start(bf16[2,48,1024]{2,1,0:T(8,128)(2,1)S(1)} %copy.13), channel_id=1, source_target_pairs={{64,0},{72,8},{80,16},{88,24},{96,32},{104,40},{112,48},{120,56},{... | collective-permute-start | bytes 589832 | tf_op jit(solution)/shard_map/ppermute | solution.py:337
  44.6 8.7 %collective-permute-start.3 = (bf16[2,16,1024]{2,1,0:T(8,128)(2,1)S(1)}, bf16[2,16,1024]{2,1,0:T(8,128)(2,1)S(1)}, u32[]{:S(2)}, u32[]{:S(2)}) collective-permute-start(bf16[2,16,1024]{2,1,0:T(8,128)(2,1)S(1)} %reshape.134), channel_id=1, source_target_pairs={{72,0},{80,8},{88,16},{96,24},{104,32},{112,40},{120,48},{128,56},... | collective-permute-start | bytes 196616 | tf_op jit(solution)/shard_map/ppermute | solution.py:337
  53.4 0.6 copy-start.9
  63.9 6.0 %copy-start = (bf16[16,2,128,256]{3,2,1,0:T(8,128)(2,1)}, bf16[16,2,128,256]{3,2,1,0:T(8,128)(2,1)S(1)}, u32[]{:S(2)}) copy-start(bf16[16,2,128,256]{3,2,1,0:T(8,128)(2,1)S(1)} %all-to-all-done) | copy-start | bytes 6291460
  63.9 6.0 %collective-permute-start.4 = (bf16[4,1024,256]{2,1,0:T(8,128)(2,1)S(1)}, bf16[4,1024,256]{2,1,0:T(8,128)(2,1)S(1)}, u32[]{:S(2)}, u32[]{:S(2)}) collective-permute-start(bf16[4,1024,256]{2,1,0:T(8,128)(2,1)S(1)} %bitcast.21), channel_id=1, source_target_pairs={{0,8},{8,0},{1,9},{9,1},{2,10},{10,2},{3,11},{11,3},{4,12},{12,4},... | collective-permute-start | bytes 6291464 | tf_op jit(solution)/shard_map/ppermute | solution.py:362
  65.8 14.4 %collective-permute-start.5 = (bf16[2,256,1024]{2,1,0:T(8,128)(2,1)}, bf16[2,256,1024]{2,1,0:T(8,128)(2,1)S(1)}, u32[]{:S(2)}, u32[]{:S(2)}) collective-permute-start(bf16[2,256,1024]{2,1,0:T(8,128)(2,1)} %get-tuple-element.33.sides_ref), channel_id=1, source_target_pairs={{0,8},{8,0},{1,9},{9,1},{2,10},{10,2},{3,11},{11,3},{4,12},{12,4},... | collective-permute-start | bytes 3145736 | tf_op jit(solution)/shard_map/ppermute | solution.py:362
  69.9 1.4 copy-start.2
  78.1 4.8 %collective-permute-start.6 = (bf16[256,2048]{1,0:T(8,128)(2,1)}, bf16[256,2048]{1,0:T(8,128)(2,1)S(1)}, u32[]{:S(2)}, u32[]{:S(2)}) collective-permute-start(bf16[256,2048]{1,0:T(8,128)(2,1)} %attend.1.back_ref), channel_id=1, source_target_pairs={{0,8},{8,0},{1,9},{9,1},{2,10},{10,2},{3,11},{11,3},{4,12},{12,4},... | collective-permute-start | bytes 3145736 | tf_op jit(solution)/shard_map/ppermute | solution.py:362
  80.2 2.7 %copy-start.11 = (bf16[2,256,1024]{2,1,0:T(8,128)(2,1)}, bf16[2,256,1024]{2,1,0:T(8,128)(2,1)S(1)}, u32[]{:S(2)}) copy-start(bf16[2,256,1024]{2,1,0:T(8,128)(2,1)S(1)} %collective-permute-done.5.peer_sides_ref) | copy-start | bytes 3145732
  82.9 1.0 copy-start.12
  90.5 39.7 %all-to-all-start.1 = ((bf16[16,256,256]{2,1,0:T(8,128)(2,1)}), bf16[16,256,256]{2,1,0:T(8,128)(2,1)S(1)}, u32[]{:S(2)}, u32[]{:S(2)}) async-start(bf16[16,256,256]{2,1,0:T(8,128)(2,1)} %bitcast.30), calls=%async_computation.1 | async-start | bytes 4194304 | tf_op jit(solution)/shard_map/all_to_all | solution.py:403
  101.7 22.7 %collective-permute-start.7 = (bf16[2,48,1024]{2,1,0:T(8,128)(2,1)}, bf16[2,48,1024]{2,1,0:T(8,128)(2,1)S(1)}, u32[]{:S(2)}, u32[]{:S(2)}) collective-permute-start(bf16[2,48,1024]{2,1,0:T(8,128)(2,1)} %get-tuple-element.37), channel_id=1, source_target_pairs={{504,0},{0,8},{8,16},{16,24},{24,32},{32,40},{40,48},{48,56},{56,6... | collective-permute-start | bytes 589832 | tf_op jit(solution)/shard_map/ppermute | solution.py:337
  103.7 20.8 %collective-permute-start.8 = (bf16[2,48,1024]{2,1,0:T(8,128)(2,1)}, bf16[2,48,1024]{2,1,0:T(8,128)(2,1)S(1)}, u32[]{:S(2)}, u32[]{:S(2)}) collective-permute-start(bf16[2,48,1024]{2,1,0:T(8,128)(2,1)} %get-tuple-element.38), channel_id=1, source_target_pairs={{448,0},{456,8},{464,16},{472,24},{480,32},{488,40},{496,48},{504,... | collective-permute-start | bytes 589832 | tf_op jit(solution)/shard_map/ppermute | solution.py:337
  106.6 17.8 %collective-permute-start.9 = (bf16[2,16,1024]{2,1,0:T(8,128)(2,1)}, bf16[2,16,1024]{2,1,0:T(8,128)(2,1)S(1)}, u32[]{:S(2)}, u32[]{:S(2)}) collective-permute-start(bf16[2,16,1024]{2,1,0:T(8,128)(2,1)} %get-tuple-element.39), channel_id=1, source_target_pairs={{440,0},{448,8},{456,16},{464,24},{472,32},{480,40},{488,48},{496,... | collective-permute-start | bytes 196616 | tf_op jit(solution)/shard_map/ppermute | solution.py:337
  124.4 18.6 %copy-start.8 = (bf16[2,16,1024]{2,1,0:T(8,128)(2,1)}, bf16[2,16,1024]{2,1,0:T(8,128)(2,1)S(1)}, u32[]{:S(2)}) copy-start(bf16[2,16,1024]{2,1,0:T(8,128)(2,1)S(1)} %collective-permute-done.9.corner_ref) | copy-start | bytes 196612
  124.5 18.6 %copy-start.6 = (bf16[2,48,1024]{2,1,0:T(8,128)(2,1)}, bf16[2,48,1024]{2,1,0:T(8,128)(2,1)S(1)}, u32[]{:S(2)}) copy-start(bf16[2,48,1024]{2,1,0:T(8,128)(2,1)S(1)} %collective-permute-done.7.west_ref) | copy-start | bytes 589828
  124.5 18.6 %copy-start.7 = (bf16[2,48,1024]{2,1,0:T(8,128)(2,1)}, bf16[2,48,1024]{2,1,0:T(8,128)(2,1)S(1)}, u32[]{:S(2)}) copy-start(bf16[2,48,1024]{2,1,0:T(8,128)(2,1)S(1)} %collective-permute-done.8.north_ref) | copy-start | bytes 589828
  130.2 1.3 copy-start.1
  134.7 28.5 %all-to-all-start.2 = ((f32[16,32,128]{2,1,0:T(8,128)}), f32[16,32,128]{2,1,0:T(8,128)S(1)}, u32[]{:S(2)}, u32[]{:S(2)}) async-start(f32[16,32,128]{2,1,0:T(8,128)} %bitcast.31), calls=%async_computation.2 | async-start | bytes 524288 | tf_op jit(solution)/shard_map/all_to_all | solution.py:416
  163.2 0.7 copy-start.5

commit v3 on v2

v3 whole, which is shorter than its diff:
```python
import functools
import jax
import jax.numpy as jnp
from jax import lax
from jax.experimental import pallas as pl
from jax.experimental.pallas import tpu as pltpu
from jax.sharding import Mesh, PartitionSpec as P

HEADS = 8
HD = 64
WIN = 8
GRID_COLS = 8
SIDE = 16
HALF = WIN // 2
INNER = SIDE - HALF
CELLS = SIDE * SIDE
FLAG_ROWS = 16
EAST = INNER * HALF
CORNER = HALF * HALF
EPSILON = 1e-05
NEG = -1e30
TRAILING = (((1,), (1,)), ((), ()))
LEADING = (((0,), (0,)), ((), ()))
VMEM_LIMIT = 56 * 1024 * 1024

f32 = jnp.float32
bf16 = jnp.bfloat16


def mm(a, b, dims=(((1,), (0,)), ((), ()))):
    return lax.dot_general(a, b, dims, preferred_element_type=f32)


def region_coords(shape, axis):
    place = lax.broadcasted_iota(jnp.int32, shape, axis)
    window, inside = place >> 6, place & 63
    row = (window >> 1) * WIN + (inside >> 3)
    column = (window & 1) * WIN + (inside & 7)
    return row, column


def source_of(codes, shape, axis):
    row, column = region_coords(shape, axis)
    flip_one, flip_two = codes[0] & 1, codes[0] >> 1
    er = jnp.where(flip_one == 1, INNER - 1 - row, row)
    ec = column - INNER
    ec = jnp.where(flip_two == 1, HALF - 1 - ec, ec)
    flip_one, flip_two = codes[1] & 1, codes[1] >> 1
    sc = jnp.where(flip_one == 1, INNER - 1 - column, column)
    sr = row - INNER
    sr = jnp.where(flip_two == 1, HALF - 1 - sr, sr)
    i, j = row - INNER, column - INNER
    turn = codes[2]
    last = HALF - 1
    cr = jnp.where(turn == 0, i, jnp.where(turn == 1, j, jnp.where(turn == 2, last - i, last - j)))
    cc = jnp.where(turn == 0, j, jnp.where(turn == 1, last - i, jnp.where(turn == 2, last - j, i)))
    own = (row + HALF) * SIDE + column + HALF
    east = CELLS + er * HALF + ec
    south = CELLS + EAST + sr * INNER + sc
    corner = CELLS + 2 * EAST + cr * HALF + cc
    low_row, low_column = row < INNER, column < INNER
    return jnp.where(
        low_row, jnp.where(low_column, own, east), jnp.where(low_column, south, corner)
    )


def onehot(condition):
    return jnp.where(condition, 1.0, 0.0).astype(bf16)


def gather_matrices(codes):
    source = source_of(codes, (CELLS, 1), 0)
    own = onehot(source == lax.broadcasted_iota(jnp.int32, (CELLS, CELLS), 1))
    halo = onehot(source - CELLS == lax.broadcasted_iota(jnp.int32, (CELLS, 128), 1))
    return own, halo


def scatter_matrices(codes):
    source = source_of(codes, (1, CELLS), 1)
    own = onehot(source == lax.broadcasted_iota(jnp.int32, (CELLS, CELLS), 0))
    halo = onehot(source - CELLS == lax.broadcasted_iota(jnp.int32, (128, CELLS), 0))
    return own, halo


def arrived_matrix():
    place = lax.broadcasted_iota(jnp.int32, (CELLS, 1), 0)
    row, column = place >> 4, place & 15
    west = (row - HALF) * HALF + column
    north = EAST + row * INNER + column - HALF
    corner = 2 * EAST + row * HALF + column
    low_row, low_column = row < HALF, column < HALF
    index = jnp.where(
        low_row,
        jnp.where(low_column, corner, north),
        jnp.where(low_column, west, -1),
    )
    return onehot(index == lax.broadcasted_iota(jnp.int32, (CELLS, 128), 1))


def prep_kernel(ints_ref, tok_ref, dy_ref, e_ref, s_ref, c_ref, sides_ref, normf_ref, inv_ref):
    codes = [ints_ref[k] for k in range(3)]
    own, halo = gather_matrices(codes)
    pad = jnp.zeros((128 - 2 * EAST - CORNER, tok_ref.shape[1]), bf16)

    def region(main, which):
        edge = jnp.concatenate([e_ref[which], s_ref[which], c_ref[which], pad], axis=0)
        return mm(own, main) + mm(halo, edge)

    values = region(tok_ref[...], 0)
    center = values - jnp.mean(values, -1, keepdims=True)
    variance = jnp.mean(center * center, -1, keepdims=True)
    inverse = lax.rsqrt(variance + EPSILON)
    normed_f = center * inverse
    normf_ref[...] = normed_f
    sides_ref[0, :CELLS] = normed_f.astype(bf16)
    flag = jnp.where(ints_ref[3] == 0, 0.0, 1.0)
    sides_ref[0, CELLS:] = jnp.full((FLAG_ROWS, tok_ref.shape[1]), flag, f32).astype(bf16)
    sides_ref[1, CELLS:] = jnp.zeros((FLAG_ROWS, tok_ref.shape[1]), bf16)
    inv_ref[...] = jnp.broadcast_to(inverse, inv_ref.shape)
    sides_ref[1, :CELLS] = region(dy_ref[...], 1).astype(bf16)


def piece_kernel(spot_ref, wq_ref, wo_ref, out_ref):
    core, y = spot_ref[0], spot_ref[2]
    wq, wo = wq_ref[...], wo_ref[...]
    head = y * 2 + core
    part = wq[:, :192]
    for k in range(1, HEADS):
        part = jnp.where(head == k, wq[:, k * 192 : (k + 1) * 192], part)
    quarter = wo[:, :256]
    for k in range(1, 4):
        quarter = jnp.where(y == k, wo[:, k * 256 : (k + 1) * 256], quarter)
    group = [quarter[:, k * 64 : (k + 1) * 64] for k in range(4)]
    low = jnp.concatenate([group[0], group[2]], axis=1)
    high = jnp.concatenate([group[1], group[3]], axis=1)
    out_ref[...] = jnp.concatenate(
        [part, jnp.zeros((128, 64), bf16), jnp.concatenate([low, high], axis=0)], axis=1
    )


def slots_kernel(spot_ref, here_ref, there_ref, out_ref):
    core, zh = spot_ref[0], spot_ref[1]
    here, there = here_ref[...], there_ref[...]
    first = jnp.where(zh == 0, here, there)
    second = jnp.where(zh == 0, there, here)
    out = jnp.where(core == zh, here, there)[:, 256:]
    slot = jnp.concatenate(
        [
            jnp.concatenate([first[:, :192], out[:, :64]], axis=1),
            jnp.concatenate([second[:, :192], out[:, 64:]], axis=1),
        ],
        axis=0,
    )
    for k in range(16):
        out_ref[k] = slot


def attend_kernel(
    ints_ref, sides_ref, peer_ref, got_ref, bias_ref, back_ref, wo_ref, send_ref, qkv_ref, gh_ref
):
    core = ints_ref[4]
    both = [jnp.concatenate([sides_ref[k, :CELLS], peer_ref[k, :CELLS]], axis=0) for k in range(2)]
    for s in range(4):
        qkv_ref[:, pl.ds(s * 256, 256)] = mm(both[0], got_ref[s]).astype(bf16)
        for y in range(4):
            row = [got_ref[y, pl.ds(s * 256 + q * 64, 64), pl.ds(128, 128)][:, 64:] for q in range(4)]
            wo_ref[pl.ds(s * 64, 64), pl.ds(y * 256, 256)] = jnp.concatenate(row, axis=1)
    gh_ref[...] = mm(both[1], wo_ref[...], TRAILING).astype(bf16)
    keys = lax.broadcasted_iota(jnp.int32, (128, 128), 0)
    lower = lax.broadcasted_iota(jnp.int32, (64, 128), 1) < 64
    query = lax.broadcasted_iota(jnp.int32, (1, 128), 1)

    def closed(place):
        inside = place & 63
        return (place >= 64) & ((inside >> 3) >= HALF) & ((inside & 7) >= HALF)

    no_key, keep = [], []
    for ref in (sides_ref, peer_ref):
        flag = ref[0, CELLS:, :128].astype(f32)[:1]
        no_key.append(jnp.where(closed(keys) & (flag == 0.0), NEG, 0.0))
        keep.append(jnp.where(closed(query) & (flag == 0.0), 0.0, 1.0))
    scale = jnp.asarray(HD ** (-0.5), bf16)
    n = range(4)
    for head in range(4):
        table = bias_ref[head * 2 + core]
        table = jnp.concatenate([jnp.where(lower, table, NEG), jnp.where(lower, NEG, table)], axis=0)
        q, k, v, g = [], [], [], []
        for block in n:
            wide = qkv_ref[pl.ds(block * 128, 128), pl.ds(head * 256, 256)]
            q.append(wide[:, :64] * scale)
            k.append(wide[:, 64:128])
            v.append(wide[:, 128:192])
            pair = gh_ref[pl.ds(block * 128, 128), pl.ds(head // 2 * 128, 128)]
            g.append(pair[:, head % 2 * 64 : head % 2 * 64 + 64])
        score = [mm(k[u], q[u], TRAILING) + table for u in n]
        score = [score[u] + no_key[u // 2] if u % 2 == 1 else score[u] for u in n]
        dp = [mm(v[u], g[u], TRAILING) for u in n]
        e = [jnp.exp(score[u] - jnp.max(score[u], 0, keepdims=True)) for u in n]
        r = [1.0 / jnp.sum(e[u], 0, keepdims=True) for u in n]
        r = [r[u] * keep[u // 2] if u % 2 == 1 else r[u] for u in n]
        probs = [e[u] * r[u] for u in n]
        pb = [probs[u].astype(bf16) for u in n]
        ds = [
            (probs[u] * (dp[u] - jnp.sum(dp[u] * probs[u], 0, keepdims=True))).astype(bf16) for u in n
        ]
        out = [mm(pb[u], v[u], LEADING).astype(bf16) for u in n]
        dv = [mm(pb[u], g[u]).astype(bf16) for u in n]
        dq = [mm(ds[u], k[u] * scale, LEADING).astype(bf16) for u in n]
        dk = [mm(ds[u], q[u]).astype(bf16) for u in n]
        for u in n:
            back_ref[pl.ds(u * 128, 128), pl.ds(head * 256, 256)] = jnp.concatenate(
                [dq[u], dk[u], dv[u], out[u]], axis=1
            )
    branch, dnormed = head_parts(got_ref, wo_ref, back_ref[pl.ds(CELLS, CELLS)])
    send_ref[0] = branch.astype(bf16)
    send_ref[1] = dnormed.astype(bf16)


def grads_kernel(sides_ref, peer_ref, back_ref, out_ref, tq_ref, to_ref):
    both = [jnp.concatenate([sides_ref[k, :CELLS], peer_ref[k, :CELLS]], axis=0) for k in range(2)]
    back = back_ref[...]
    tq_ref[...] = mm(back, both[0], LEADING)
    twice = []
    for head in range(4):
        one = back[:, head * 256 + 192 : head * 256 + 256]
        twice += [one, one]
    to_ref[...] = mm(both[1], jnp.concatenate(twice, axis=1), LEADING)
    lower = lax.broadcasted_iota(jnp.int32, (8, 128), 1) < 64
    for y in range(4):
        for owner in range(2):
            for x in range(4):
                rows = [
                    tq_ref[pl.ds(s * 256 + y * 48 + owner * 24, 24), pl.ds(x * 256, 256)]
                    for s in range(4)
                ]
                for z in range(4):
                    sides = []
                    for upper in range(2):
                        start = (z + upper * 4) * 128 + y * 32 + owner * 16
                        low = to_ref[pl.ds(start, 8), pl.ds(x * 128, 128)]
                        high = to_ref[pl.ds(start + 8, 8), pl.ds(x * 128, 128)]
                        sides.append(jnp.where(lower, low, high))
                    rows.append(jnp.concatenate(sides, axis=1))
                out_ref[y, owner, x] = jnp.concatenate(rows, axis=0).astype(bf16)


def head_parts(got_ref, wo_ref, back):
    lanes = lax.broadcasted_iota(jnp.int32, (CELLS, 256), 1)
    heads = jnp.concatenate([back[:, s * 256 + 192 : s * 256 + 256] for s in range(4)], axis=1)
    total = None
    for s in range(4):
        part = jnp.where(lanes < 192, back[:, s * 256 : s * 256 + 256], 0)
        term = mm(part, got_ref[s], TRAILING)
        total = term if total is None else total + term
    return mm(heads, wo_ref[...]), total


def home_kernel(
    ints_ref, normf_ref, inv_ref, tok_ref, dy_ref, got_ref, wo_ref, back_ref, came_ref,
    out_ref, gtok_ref, east_ref, south_ref, corner_ref,
):
    own, halo = scatter_matrices([ints_ref[k] for k in range(3)])

    def edges(which, values):
        edge = mm(halo, values).astype(bf16)
        east_ref[which] = edge[:EAST]
        south_ref[which] = edge[EAST : 2 * EAST]
        corner_ref[which] = edge[2 * EAST : 2 * EAST + CORNER]

    branch, dnormed = head_parts(got_ref, wo_ref, back_ref[pl.ds(0, CELLS)])
    branch = (branch + came_ref[0].astype(f32)).astype(bf16)
    edges(0, branch)
    out_ref[...] = (tok_ref[...].astype(f32) + mm(own, branch)).astype(bf16)
    dnormed = dnormed + came_ref[1].astype(f32)
    normed_f = normf_ref[...]
    dnorm = inv_ref[:, :1] * (
        dnormed
        - jnp.mean(dnormed, -1, keepdims=True)
        - normed_f * jnp.mean(dnormed * normed_f, -1, keepdims=True)
    )
    high = dnorm.astype(bf16)
    low = (dnorm - high.astype(f32)).astype(bf16)
    edges(1, high)
    gtok_ref[...] = (dy_ref[...].astype(f32) + (mm(own, high) + mm(own, low))).astype(bf16)


def finish_kernel(out_ref, gtok_ref, west_ref, north_ref, corner_ref, out2_ref, gtok2_ref):
    place = arrived_matrix()
    pad = jnp.zeros((128 - 2 * EAST - CORNER, out_ref.shape[1]), bf16)
    for which, (part, result) in enumerate(((out_ref, out2_ref), (gtok_ref, gtok2_ref))):
        edge = jnp.concatenate([west_ref[which], north_ref[which], corner_ref[which], pad], axis=0)
        result[...] = (part[...].astype(f32) + mm(place, edge)).astype(bf16)


def plane_kernel(got_ref, out_ref, total_ref):
    for core in range(2):
        total = None
        for y in range(4):
            for x in range(4):
                part = got_ref[y * 8 + core * 4 + x].astype(f32)
                total = part if total is None else total + part
        total_ref[core] = total
    for z in range(8):
        for half in range(2):
            out_ref[z, half, :24] = total_ref[z % 2, pl.ds(z // 2 * 24, 24), pl.ds(half * 128, 128)]
            out_ref[z, half, 24:] = total_ref[half, pl.ds(96 + z % 4 * 8, 8), pl.ds(z // 4 * 128, 128)]


def last_kernel(got_ref, gq_ref, go_ref):
    total = got_ref[0]
    for part in range(1, 16):
        total = total + got_ref[part]
    gq_ref[...] = total[:24]
    go_ref[...] = jnp.concatenate([total[24:, :64], total[24:, 64:]], axis=0)


def call(kernel, outs, *args, smem=0, scratch=(), flops=0, name=None):
    specs = [pl.BlockSpec(memory_space=pltpu.SMEM)] * smem + [pl.BlockSpec(memory_space=pltpu.VMEM)] * (
        len(args) - smem
    )
    shapes = [jax.ShapeDtypeStruct(s, d) for s, d in outs]
    size = sum(a.size * a.dtype.itemsize for a in (*args, *shapes))
    return pl.pallas_call(
        kernel,
        out_shape=shapes,
        in_specs=specs,
        out_specs=[pl.BlockSpec(memory_space=pltpu.VMEM)] * len(outs),
        scratch_shapes=list(scratch),
        compiler_params=pltpu.CompilerParams(vmem_limit_bytes=VMEM_LIMIT),
        cost_estimate=pl.CostEstimate(flops=flops, bytes_accessed=size, transcendentals=0),
        name=name,
    )(*args)


def position_bias(rel_bias):
    span = 2 * WIN - 1
    places = jnp.arange(WIN * WIN, dtype=jnp.int32)
    row_of = places // WIN
    col_of = places % WIN
    offset = (row_of[None, :] - row_of[:, None] + WIN - 1) * span + (
        col_of[None, :] - col_of[:, None] + WIN - 1
    )
    onehot_table = (
        offset.reshape(-1)[:, None] == jnp.arange(span * span, dtype=jnp.int32)[None, :]
    ).astype(f32)
    picked = jnp.dot(
        onehot_table,
        rel_bias.reshape(HEADS, span * span).T,
        precision=lax.Precision.HIGHEST,
        preferred_element_type=f32,
    )
    table = picked.T.reshape(HEADS, WIN * WIN, WIN * WIN)
    return jnp.concatenate([table, table], axis=2)


TILE_AXES = ("zl", "y", "c")


def shifted(block, distance):
    count = lax.axis_size(TILE_AXES)
    return lax.ppermute(block, TILE_AXES, [((i - distance) % count, i) for i in range(count)])


def per_device(tokens, w_qkv, w_out, rel_bias, seam_codes, corner_open, grad_out):
    width = tokens.shape[-1]
    both = jnp.stack([tokens[0, 0], grad_out[0, 0]])
    tok = tokens.reshape(CELLS, width)
    dy = grad_out.reshape(CELLS, width)
    order = jnp.arange(3, dtype=jnp.int32)
    spot = jnp.where(
        order == 0, lax.axis_index("c"), jnp.where(order == 1, lax.axis_index("zh"), lax.axis_index("y"))
    ).astype(jnp.int32)
    ints = jnp.concatenate([seam_codes[0], corner_open, lax.axis_index("c")[None]]).astype(jnp.int32)

    (piece,) = call(piece_kernel, [((128, 384), bf16)], spot, w_qkv, w_out, smem=1, name="piece")
    across = lax.ppermute(piece, "zh", [(0, 1), (1, 0)])
    bias = position_bias(rel_bias)
    across, both, bias = lax.optimization_barrier((across, both, bias))
    (many,) = call(slots_kernel, [((16, 256, 256), bf16)], spot, piece, across, smem=1, name="slots")
    mine = lax.all_to_all(many, ("y", "x"), 0, 0, tiled=True).reshape(4, width, 256)

    def swapped(block):
        return lax.ppermute(block, "c", [(0, 1), (1, 0)])

    east = shifted(both[:, HALF:, :HALF].reshape(2, EAST, width), -1)
    south = shifted(both[:, :HALF, HALF:].reshape(2, EAST, width), -GRID_COLS)
    corner = shifted(both[:, :HALF, :HALF].reshape(2, CORNER, width), -(GRID_COLS + 1))
    sides, normed_f, inverse = call(
        prep_kernel,
        [((2, CELLS + FLAG_ROWS, width), bf16), ((CELLS, width), f32), ((CELLS, 128), f32)],
        ints, tok, dy, east, south, corner,
        smem=1, flops=4 * 256 * 384 * 1024, name="prep",
    )
    peer = swapped(sides)
    mine, sides, peer = lax.optimization_barrier((mine, sides, peer))
    back, wo, send = call(
        attend_kernel,
        [((2 * CELLS, width), bf16), ((256, width), bf16), ((2, CELLS, width), bf16)],
        ints, sides, peer, mine, bias,
        smem=1, scratch=[pltpu.VMEM((2 * CELLS, 1024), bf16), pltpu.VMEM((2 * CELLS, 256), bf16)],
        flops=2 * 256 * 1024 * 2048, name="attend",
    )
    (pair,) = call(
        grads_kernel,
        [((4, 2, 4, 128, 256), bf16)],
        sides, peer, back,
        scratch=[pltpu.VMEM((1024, 1024), f32), pltpu.VMEM((1024, 512), f32)],
        flops=2 * 512 * 1024 * 1536, name="weight_grads",
    )
    came = swapped(send)
    out_part, gtok_part, east, south, corner = call(
        home_kernel,
        [
            ((CELLS, width), bf16), ((CELLS, width), bf16),
            ((2, EAST, width), bf16), ((2, EAST, width), bf16), ((2, CORNER, width), bf16),
        ],
        ints, normed_f, inverse, tok, dy, mine, wo, back, came, smem=1, flops=2 * 256 * 1024 * 900, name="home",
    )
    north = shifted(south, GRID_COLS)
    corner = shifted(corner, GRID_COLS + 1)
    west = shifted(east, 1)
    plane = lax.all_to_all(pair.reshape(32, 128, 256), ("y", "c", "x"), 0, 0, tiled=True)
    (plane,) = call(
        plane_kernel, [((8, 2, 32, 128), f32)], plane, scratch=[pltpu.VMEM((2, 128, 256), f32)], name="plane_sum"
    )
    plane, west, north, corner = lax.optimization_barrier((plane, west, north, corner))
    column = lax.all_to_all(plane.reshape(16, 32, 128), ("zl", "zh"), 0, 0, tiled=True)
    grad_w_qkv, grad_w_out = call(
        last_kernel, [((24, 128), f32), ((16, 64), f32)], column, name="column_sum"
    )
    output, grad_tokens = call(
        finish_kernel, [((CELLS, width), bf16), ((CELLS, width), bf16)],
        out_part, gtok_part, west, north, corner, name="finish",
    )
    return (
        output.reshape(tokens.shape), grad_tokens.reshape(tokens.shape), grad_w_qkv.T, grad_w_out.T
    )


def solution(mesh):
    fine = Mesh(mesh.devices.reshape(8, 4, 2, 4, 2), ("zl", "y", "c", "x", "zh"))
    fsdp = ("x", "zh")
    acts = P(fsdp, TILE_AXES, None, None, None)
    return jax.shard_map(
        per_device,
        mesh=fine,
        in_specs=(
            acts, P(fsdp, None), P(fsdp, None), P(), P(TILE_AXES, None), P(TILE_AXES), acts,
        ),
        out_specs=(acts, acts, P(fsdp, TILE_AXES), P(fsdp, TILE_AXES)),
        check_vma=False,
    )
```

time: 166 us -> 160 us (0.964)
  the two profiles are of different devices: /device:TPU:32 before, /device:TPU:38 now
where the time goes in v3:
time: 160 us; the launch traced here: 159 us
  starting transfers between devices  74.2 us (46%)
  waiting for transfers between devices  34.7 us (22%)
  Pallas kernels  33.4 us (21%)
  local copies, waits for them, and re-layouts  9.88 us (6%)
  other arithmetic  3.11 us (2%)
  matrix products  2.56 us (2%)
    pallas_call x9, Pallas kernels, call(): pl.pallas_call(kernel, out_shape=shapes, in_specs=specs, out_specs=[pl.Bl...  33.4 us
    ppermute x6, starting transfers between devices, shifted(): lax.ppermute(block, TILE_AXES, [((i - distance) % count, i) for i in rang...  26.7 us
    all_to_all x1, waiting for transfers between devices, per_device(): lax.all_to_all(plane.reshape(16, 32, 128), ('zl', 'zh'), 0, 0, tiled=True)  18.4 us
    ppermute x1, starting transfers between devices, per_device(): across = lax.ppermute(piece, 'zh', [(0, 1), (1, 0)])  14.8 us
    all_to_all x1, starting transfers between devices, per_device(): lax.all_to_all(plane.reshape(16, 32, 128), ('zl', 'zh'), 0, 0, tiled=True)  12 us
    all_to_all x1, waiting for transfers between devices, per_device(): lax.all_to_all(pair.reshape(32, 128, 256), ('y', 'c', 'x'), 0, 0, tiled=T...  9.16 us
    all_to_all x1, starting transfers between devices, per_device(): lax.all_to_all(many, ('y', 'x'), 0, 0, tiled=True).reshape(4, width, 256)  7.55 us
    all_to_all x1, starting transfers between devices, per_device(): lax.all_to_all(pair.reshape(32, 128, 256), ('y', 'c', 'x'), 0, 0, tiled=T...  7.25 us
  transfers between devices with their start and end apart: 12, of which 6 were waited for; matrix products, arithmetic and copies ran while one was open for 6% of the time, Pallas kernels for 9%

profile of v3, /device:TPU:38, one launch (start us, length us, event | category | flops | bytes accessed | tf_op | source)
XLA Modules:
  0.0 159.4 jit_solution(4857234804991310266)
XLA Ops:
  0.7 0.5 compare_select_fusion.1.spot_ref
  1.2 2.1 %piece.1.here_ref = bf16[128,384]{1,0:T(8,128)(2,1)} custom-call(s32[3]{0:T(128)} %compare_select_fusion.1.spot_ref, bf16[128,1536]{1,0:T(8,128)(2,1)} %wq_ref.1, bf16[64,1024]{1,0:T(8,128)(2,1)} %wo_ref.1), custom_call_target="tpu_custom_call" | custom-call | bytes 622604 | tf_op jit(solution)/shard_map/piece/pallas_call | solution.py:323
  3.2 14.8 %collective-permute-start = (bf16[128,384]{1,0:T(8,128)(2,1)}, bf16[128,384]{1,0:T(8,128)(2,1)S(1)}, u32[]{:S(2)}, u32[]{:S(2)}) collective-permute-start(bf16[128,384]{1,0:T(8,128)(2,1)} %piece.1.here_ref), channel_id=1, source_target_pairs={{0,1},{1,0},{2,3},{3,2},{4,5},{5,4},{6,7},{7,6},{8,9},{9,8},{10,11... | collective-permute-start | bytes 294920 | tf_op jit(solution)/shard_map/ppermute | solution.py:376
  18.1 0.8 copy.11
  18.9 0.1 reshape.129
  19.0 0.1 add_add_fusion
  19.1 0.1 add.55
  19.2 2.6 %convolution_bitcast_fusion = f32[8,4096]{1,0:T(8,128)S(1)} fusion(f32[8,225]{1,0:T(8,128)S(1)} %reshape.129, s32[4096]{0:T(1024)S(1)} %add.55), kind=kOutput, calls=%fused_computation | convolution fusion | flops 89395200 | bytes 154656 | tf_op jit(solution)/shard_map/dot_general | solution.py:346
  21.7 0.1 reshape.130
  21.9 1.1 pad_maximum_fusion
  22.9 0.8 pad_maximum_fusion.1.bias_ref
  23.8 0.6 copy-done.10
  24.4 2.5 %slots.1 = bf16[16,256,256]{2,1,0:T(8,128)(2,1)} custom-call(s32[3]{0:T(128)} %compare_select_fusion.1.spot_ref, bf16[128,384]{1,0:T(8,128)(2,1)} %piece.1.here_ref, bf16[128,384]{1,0:T(8,128)(2,1)} %copy-done.10), custom_call_target="tpu_custom_call" | custom-call | bytes 2293772 | tf_op jit(solution)/shard_map/slots/pallas_call | solution.py:323
  26.9 7.6 %all-to-all-start = ((bf16[16,256,256]{2,1,0:T(8,128)(2,1)}), bf16[16,256,256]{2,1,0:T(8,128)(2,1)S(1)}, u32[]{:S(2)}, u32[]{:S(2)}) async-start(bf16[16,256,256]{2,1,0:T(8,128)(2,1)} %slots.1), calls=%async_computation | async-start | bytes 4194304 | tf_op jit(solution)/shard_map/all_to_all | solution.py:380
  34.5 0.7 slice.9
  35.2 0.1 slice.10
  35.3 1.7 %reshape.131 = bf16[2,48,1024]{2,1,0:T(8,128)(2,1)} reshape(bf16[2,12,4,1024]{3,2,1,0:T(4,128)(2,1)} %slice.9) | data formatting | bytes 393216 | tf_op jit(solution)/shard_map/reshape | solution.py:385
  37.0 3.6 %collective-permute-start.1 = (bf16[2,48,1024]{2,1,0:T(8,128)(2,1)}, bf16[2,48,1024]{2,1,0:T(8,128)(2,1)}, u32[]{:S(2)}, u32[]{:S(2)}) collective-permute-start(bf16[2,48,1024]{2,1,0:T(8,128)(2,1)} %reshape.131), channel_id=1, source_target_pairs={{8,0},{16,8},{24,16},{32,24},{40,32},{48,40},{56,48},{64,56},{72,6... | collective-permute-start | bytes 589832 | tf_op jit(solution)/shard_map/ppermute | solution.py:361
  40.6 0.2 copy.12
  40.8 6.3 %collective-permute-start.2 = (bf16[2,48,1024]{2,1,0:T(8,128)(2,1)S(1)}, bf16[2,48,1024]{2,1,0:T(8,128)(2,1)}, u32[]{:S(2)}, u32[]{:S(2)}) collective-permute-start(bf16[2,48,1024]{2,1,0:T(8,128)(2,1)S(1)} %copy.13), channel_id=1, source_target_pairs={{64,0},{72,8},{80,16},{88,24},{96,32},{104,40},{112,48},{120,56},{... | collective-permute-start | bytes 589832 | tf_op jit(solution)/shard_map/ppermute | solution.py:361
  47.8 8.2 %collective-permute-start.3 = (bf16[2,16,1024]{2,1,0:T(8,128)(2,1)S(1)}, bf16[2,16,1024]{2,1,0:T(8,128)(2,1)S(1)}, u32[]{:S(2)}, u32[]{:S(2)}) collective-permute-start(bf16[2,16,1024]{2,1,0:T(8,128)(2,1)S(1)} %reshape.133), channel_id=1, source_target_pairs={{72,0},{80,8},{88,16},{96,24},{104,32},{112,40},{120,48},{128,56},... | collective-permute-start | bytes 196616 | tf_op jit(solution)/shard_map/ppermute | solution.py:361
  56.0 0.6 pad_add_fusion.ints_ref
  56.6 2.0 %collective-permute-done.3.c_ref = bf16[2,16,1024]{2,1,0:T(8,128)(2,1)S(1)} collective-permute-done((bf16[2,16,1024]{2,1,0:T(8,128)(2,1)S(1)}, bf16[2,16,1024]{2,1,0:T(8,128)(2,1)S(1)}, u32[]{:S(2)}, u32[]{:S(2)}) %collective-permute-start.3) | collective-permute-done | bytes 65568 | tf_op jit(solution)/shard_map/ppermute | solution.py:361
  58.6 0.6 copy-done.12
  59.2 3.6 %prep.1 = (bf16[2,272,1024]{2,1,0:T(8,128)(2,1)}, f32[256,1024]{1,0:T(8,128)}, f32[256,128]{1,0:T(8,128)}) custom-call(s32[5]{0:T(128)} %pad_add_fusion.ints_ref, bf16[256,1024]{1,0:T(8,128)(2,1)} %bitcast.19, bf16[256,1024]{1,0:T(8,128)(2,1)} %bitcast.22, bf16[2,48,1024]{2,1,0:T(8,128)(2,1)} %collective-permute-done.1.e_ref, ...), custom_call_target="tpu_custom_call" | custom-call | flops 402653184 | bytes 3801108 | tf_op jit(solution)/shard_map/prep/pallas_call | solution.py:323
  62.9 3.8 %collective-permute-start.4 = (bf16[2,272,1024]{2,1,0:T(8,128)(2,1)}, bf16[2,272,1024]{2,1,0:T(8,128)(2,1)S(1)}, u32[]{:S(2)}, u32[]{:S(2)}) collective-permute-start(bf16[2,272,1024]{2,1,0:T(8,128)(2,1)} %get-tuple-element.35.sides_ref), channel_id=1, source_target_pairs={{0,8},{8,0},{1,9},{9,1},{2,10},{10,2},{3,11},{11,3},{4,12},{12,4},... | collective-permute-start | bytes 3342344 | tf_op jit(solution)/shard_map/ppermute | solution.py:383
  66.6 2.6 %collective-permute-done.4.peer_ref = bf16[2,272,1024]{2,1,0:T(8,128)(2,1)S(1)} collective-permute-done((bf16[2,272,1024]{2,1,0:T(8,128)(2,1)}, bf16[2,272,1024]{2,1,0:T(8,128)(2,1)S(1)}, u32[]{:S(2)}, u32[]{:S(2)}) %collective-permute-start.4) | collective-permute-done | bytes 1114144 | tf_op jit(solution)/shard_map/ppermute | solution.py:383
  69.2 1.0 copy-done.5
  70.2 0.7 copy-done
  70.9 7.8 %attend.1 = (bf16[512,1024]{1,0:T(8,128)(2,1)}, bf16[256,1024]{1,0:T(8,128)(2,1)}, bf16[2,256,1024]{2,1,0:T(8,128)(2,1)}) custom-call(s32[5]{0:T(128)} %pad_add_fusion.ints_ref, bf16[2,272,1024]{2,1,0:T(8,128)(2,1)} %get-tuple-element.35.sides_ref, bf16[2,272,1024]{2,1,0:T(8,128)(2,1)} %copy-done.5, bf16[4,1024,256]{2,1,0:T(8,128)(2,1)} %bitcast.17, ...), custom_call_target="tpu_custom_call" | custom-call | flops 1073741824 | bytes 7208980 | tf_op jit(solution)/shard_map/attend/pallas_call | solution.py:323
  78.6 5.1 %weight_grads.1 = bf16[4,2,4,128,256]{4,3,2,1,0:T(8,128)(2,1)} custom-call(bf16[2,272,1024]{2,1,0:T(8,128)(2,1)} %get-tuple-element.35.sides_ref, bf16[2,272,1024]{2,1,0:T(8,128)(2,1)} %copy-done.5, bf16[512,1024]{1,0:T(8,128)(2,1)} %get-tuple-element.39.back_ref), custom_call_target="tpu_custom_call" | custom-call | flops 1610612736 | bytes 5373952 | tf_op jit(solution)/shard_map/weight_grads/pallas_call | solution.py:323
  83.7 7.3 %all-to-all-start.1 = ((bf16[32,128,256]{2,1,0:T(8,128)(2,1)}), bf16[32,128,256]{2,1,0:T(8,128)(2,1)S(1)}, u32[]{:S(2)}, u32[]{:S(2)}) async-start(bf16[32,128,256]{2,1,0:T(8,128)(2,1)} %bitcast.25), calls=%async_computation.1 | async-start | bytes 4194304 | tf_op jit(solution)/shard_map/all_to_all | solution.py:422
  91.0 2.1 %collective-permute-start.5 = (bf16[2,256,1024]{2,1,0:T(8,128)(2,1)S(1)}, bf16[2,256,1024]{2,1,0:T(8,128)(2,1)S(1)}, u32[]{:S(2)}, u32[]{:S(2)}) collective-permute-start(bf16[2,256,1024]{2,1,0:T(8,128)(2,1)S(1)} %copy-done.14), channel_id=1, source_target_pairs={{0,8},{8,0},{1,9},{9,1},{2,10},{10,2},{3,11},{11,3},{4,12},{12,4},... | collective-permute-start | bytes 3145736 | tf_op jit(solution)/shard_map/ppermute | solution.py:383
  93.0 2.5 %collective-permute-done.5.came_ref = bf16[2,256,1024]{2,1,0:T(8,128)(2,1)S(1)} collective-permute-done((bf16[2,256,1024]{2,1,0:T(8,128)(2,1)S(1)}, bf16[2,256,1024]{2,1,0:T(8,128)(2,1)S(1)}, u32[]{:S(2)}, u32[]{:S(2)}) %collective-permute-start.5) | collective-permute-done | bytes 1048608 | tf_op jit(solution)/shard_map/ppermute | solution.py:383
  95.5 1.0 copy-done.7
  96.6 5.7 %home.1 = (bf16[256,1024]{1,0:T(8,128)(2,1)}, bf16[256,1024]{1,0:T(8,128)(2,1)}, bf16[2,48,1024]{2,1,0:T(8,128)(2,1)}, bf16[2,48,1024]{2,1,0:T(8,128)(2,1)}, bf16[2,16,1024]{2,1,0:T(8,128)(2,1)}) custom-call(s32[5]{0:T(128)} %pad_add_fusion.ints_ref, f32[256,1024]{1,0:T(8,128)} %get-tuple-element.30.normf_ref, f32[256,128]{1,0:T(8,128)} %get-tuple-element.31.inv_ref, ...), custom_call_target="tpu_custom_call" | custom-call | flops 471859200 | bytes 8454164 | tf_op jit(solution)/shard_map/home/pallas_call | solution.py:323
  102.2 2.0 %collective-permute-start.6 = (bf16[2,48,1024]{2,1,0:T(8,128)(2,1)}, bf16[2,48,1024]{2,1,0:T(8,128)(2,1)S(1)}, u32[]{:S(2)}, u32[]{:S(2)}) collective-permute-start(bf16[2,48,1024]{2,1,0:T(8,128)(2,1)} %get-tuple-element.43), channel_id=1, source_target_pairs={{504,0},{0,8},{8,16},{16,24},{24,32},{32,40},{40,48},{48,56},{56,6... | collective-permute-start | bytes 589832 | tf_op jit(solution)/shard_map/ppermute | solution.py:361
  104.3 2.9 %collective-permute-start.7 = (bf16[2,48,1024]{2,1,0:T(8,128)(2,1)}, bf16[2,48,1024]{2,1,0:T(8,128)(2,1)S(1)}, u32[]{:S(2)}, u32[]{:S(2)}) collective-permute-start(bf16[2,48,1024]{2,1,0:T(8,128)(2,1)} %get-tuple-element.44), channel_id=1, source_target_pairs={{448,0},{456,8},{464,16},{472,24},{480,32},{488,40},{496,48},{504,... | collective-permute-start | bytes 589832 | tf_op jit(solution)/shard_map/ppermute | solution.py:361
  107.2 3.7 %collective-permute-start.8 = (bf16[2,16,1024]{2,1,0:T(8,128)(2,1)}, bf16[2,16,1024]{2,1,0:T(8,128)(2,1)S(1)}, u32[]{:S(2)}, u32[]{:S(2)}) collective-permute-start(bf16[2,16,1024]{2,1,0:T(8,128)(2,1)} %get-tuple-element.45), channel_id=1, source_target_pairs={{440,0},{448,8},{456,16},{464,24},{472,32},{480,40},{488,48},{496,... | collective-permute-start | bytes 196616 | tf_op jit(solution)/shard_map/ppermute | solution.py:361
  110.9 9.2 %all-to-all-done.1.got_ref = bf16[32,128,256]{2,1,0:T(8,128)(2,1)S(1)} async-done(((bf16[32,128,256]{2,1,0:T(8,128)(2,1)}), bf16[32,128,256]{2,1,0:T(8,128)(2,1)S(1)}, u32[]{:S(2)}, u32[]{:S(2)}) %all-to-all-start.1) | async-done | bytes 2097184 | tf_op jit(solution)/shard_map/all_to_all | solution.py:422
  120.1 1.3 copy-done.1
  121.4 2.6 %plane_sum.1 = f32[8,2,32,128]{3,2,1,0:T(8,128)} custom-call(bf16[32,128,256]{2,1,0:T(8,128)(2,1)} %copy-done.1), custom_call_target="tpu_custom_call" | custom-call | bytes 2359296 | tf_op jit(solution)/shard_map/plane_sum/pallas_call | solution.py:323
  124.0 0.1 collective-permute-done.8.corner_ref
  124.1 12.0 %all-to-all-start.2 = ((f32[16,32,128]{2,1,0:T(8,128)}), f32[16,32,128]{2,1,0:T(8,128)S(1)}, u32[]{:S(2)}, u32[]{:S(2)}) async-start(f32[16,32,128]{2,1,0:T(8,128)} %bitcast.26), calls=%async_computation.2 | async-start | bytes 524288 | tf_op jit(solution)/shard_map/all_to_all | solution.py:427
  136.1 2.6 %finish.1 = (bf16[256,1024]{1,0:T(8,128)(2,1)}, bf16[256,1024]{1,0:T(8,128)(2,1)}) custom-call(bf16[256,1024]{1,0:T(8,128)(2,1)} %get-tuple-element.41.out_ref, bf16[256,1024]{1,0:T(8,128)(2,1)} %get-tuple-element.42.gtok_ref, bf16[2,48,1024]{2,1,0:T(8,128)(2,1)} %copy-done.8, bf16[2,48,1024]{2,1,0:T(8,128)(2,1)} %copy-done.9, bf16[2,16,1024]{2,1,0:T(8,128)(2,1)} %copy-done.11), custom_call_target="tpu_custom_call" | custom-call | bytes 2555904 | tf_op jit(solution)/shard_map/finish/pallas_call | solution.py:323
  138.7 18.4 %all-to-all-done.2.got_ref = f32[16,32,128]{2,1,0:T(8,128)S(1)} async-done(((f32[16,32,128]{2,1,0:T(8,128)}), f32[16,32,128]{2,1,0:T(8,128)S(1)}, u32[]{:S(2)}, u32[]{:S(2)}) %all-to-all-start.2) | async-done | bytes 262176 | tf_op jit(solution)/shard_map/all_to_all | solution.py:427
  157.1 0.7 copy-done.6
  157.8 1.6 %column_sum.1 = (f32[24,128]{1,0:T(8,128)}, f32[16,64]{1,0:T(8,128)}) custom-call(f32[16,32,128]{2,1,0:T(8,128)} %copy-done.6), custom_call_target="tpu_custom_call" | custom-call | bytes 278528 | tf_op jit(solution)/shard_map/column_sum/pallas_call | solution.py:323
  (33 shorter events, 0.1 us)
Async XLA Ops:
  0.6 21.2 %copy-start.3 = (bf16[1,1,16,16,1024]{4,3,2,1,0:T(8,128)(2,1)S(1)}, bf16[1,1,16,16,1024]{4,3,2,1,0:T(8,128)(2,1)}, u32[]{:S(2)}) copy-start(bf16[1,1,16,16,1024]{4,3,2,1,0:T(8,128)(2,1)} %param.13) | copy-start | bytes 1572868
  0.6 21.2 %copy-start.2 = (bf16[1,1,16,16,1024]{4,3,2,1,0:T(8,128)(2,1)S(1)}, bf16[1,1,16,16,1024]{4,3,2,1,0:T(8,128)(2,1)}, u32[]{:S(2)}) copy-start(bf16[1,1,16,16,1024]{4,3,2,1,0:T(8,128)(2,1)} %param.7) | copy-start | bytes 1572868
  3.2 20.6 %collective-permute-start = (bf16[128,384]{1,0:T(8,128)(2,1)}, bf16[128,384]{1,0:T(8,128)(2,1)S(1)}, u32[]{:S(2)}, u32[]{:S(2)}) collective-permute-start(bf16[128,384]{1,0:T(8,128)(2,1)} %piece.1.here_ref), channel_id=1, source_target_pairs={{0,1},{1,0},{2,3},{3,2},{4,5},{5,4},{6,7},{7,6},{8,9},{9,8},{10,11... | collective-permute-start | bytes 294920 | tf_op jit(solution)/shard_map/ppermute | solution.py:376
  23.8 0.6 copy-start.10
  26.9 7.6 %copy-start.4 = (bf16[2,16,16,1024]{3,2,1,0:T(8,128)(2,1)S(1)}, bf16[2,16,16,1024]{3,2,1,0:T(8,128)(2,1)}, u32[]{:S(2)}) copy-start(bf16[2,16,16,1024]{3,2,1,0:T(8,128)(2,1)} %pad_maximum_fusion) | copy-start | bytes 3145732
  26.9 42.3 %all-to-all-start = ((bf16[16,256,256]{2,1,0:T(8,128)(2,1)}), bf16[16,256,256]{2,1,0:T(8,128)(2,1)S(1)}, u32[]{:S(2)}, u32[]{:S(2)}) async-start(bf16[16,256,256]{2,1,0:T(8,128)(2,1)} %slots.1), calls=%async_computation | async-start | bytes 4194304 | tf_op jit(solution)/shard_map/all_to_all | solution.py:380
  34.5 21.5 %copy-start.13 = (s32[1,3]{1,0:T(1,128)S(1)}, s32[1,3]{1,0:T(1,128)}, u32[]{:S(2)}) copy-start(s32[1,3]{1,0:T(1,128)} %param.11) | copy-start | bytes 40
  37.0 21.7 %collective-permute-start.1 = (bf16[2,48,1024]{2,1,0:T(8,128)(2,1)}, bf16[2,48,1024]{2,1,0:T(8,128)(2,1)}, u32[]{:S(2)}, u32[]{:S(2)}) collective-permute-start(bf16[2,48,1024]{2,1,0:T(8,128)(2,1)} %reshape.131), channel_id=1, source_target_pairs={{8,0},{16,8},{24,16},{32,24},{40,32},{48,40},{56,48},{64,56},{72,6... | collective-permute-start | bytes 589832 | tf_op jit(solution)/shard_map/ppermute | solution.py:361
  40.8 17.8 %collective-permute-start.2 = (bf16[2,48,1024]{2,1,0:T(8,128)(2,1)S(1)}, bf16[2,48,1024]{2,1,0:T(8,128)(2,1)}, u32[]{:S(2)}, u32[]{:S(2)}) collective-permute-start(bf16[2,48,1024]{2,1,0:T(8,128)(2,1)S(1)} %copy.13), channel_id=1, source_target_pairs={{64,0},{72,8},{80,16},{88,24},{96,32},{104,40},{112,48},{120,56},{... | collective-permute-start | bytes 589832 | tf_op jit(solution)/shard_map/ppermute | solution.py:361
  47.8 10.8 %collective-permute-start.3 = (bf16[2,16,1024]{2,1,0:T(8,128)(2,1)S(1)}, bf16[2,16,1024]{2,1,0:T(8,128)(2,1)S(1)}, u32[]{:S(2)}, u32[]{:S(2)}) collective-permute-start(bf16[2,16,1024]{2,1,0:T(8,128)(2,1)S(1)} %reshape.133), channel_id=1, source_target_pairs={{72,0},{80,8},{88,16},{96,24},{104,32},{112,40},{120,48},{128,56},... | collective-permute-start | bytes 196616 | tf_op jit(solution)/shard_map/ppermute | solution.py:361
  58.6 0.6 copy-start.12
  62.9 6.3 %collective-permute-start.4 = (bf16[2,272,1024]{2,1,0:T(8,128)(2,1)}, bf16[2,272,1024]{2,1,0:T(8,128)(2,1)S(1)}, u32[]{:S(2)}, u32[]{:S(2)}) collective-permute-start(bf16[2,272,1024]{2,1,0:T(8,128)(2,1)} %get-tuple-element.35.sides_ref), channel_id=1, source_target_pairs={{0,8},{8,0},{1,9},{9,1},{2,10},{10,2},{3,11},{11,3},{4,12},{12,4},... | collective-permute-start | bytes 3342344 | tf_op jit(solution)/shard_map/ppermute | solution.py:383
  69.2 1.0 copy-start.5
  69.2 1.7 %copy-start = (bf16[16,256,256]{2,1,0:T(8,128)(2,1)}, bf16[16,256,256]{2,1,0:T(8,128)(2,1)S(1)}, u32[]{:S(2)}) copy-start(bf16[16,256,256]{2,1,0:T(8,128)(2,1)S(1)} %all-to-all-done) | copy-start | bytes 6291460
  83.7 7.3 %copy-start.14 = (bf16[2,256,1024]{2,1,0:T(8,128)(2,1)S(1)}, bf16[2,256,1024]{2,1,0:T(8,128)(2,1)}, u32[]{:S(2)}) copy-start(bf16[2,256,1024]{2,1,0:T(8,128)(2,1)} %get-tuple-element.40) | copy-start | bytes 3145732
  83.7 36.4 %all-to-all-start.1 = ((bf16[32,128,256]{2,1,0:T(8,128)(2,1)}), bf16[32,128,256]{2,1,0:T(8,128)(2,1)S(1)}, u32[]{:S(2)}, u32[]{:S(2)}) async-start(bf16[32,128,256]{2,1,0:T(8,128)(2,1)} %bitcast.25), calls=%async_computation.1 | async-start | bytes 4194304 | tf_op jit(solution)/shard_map/all_to_all | solution.py:422
  91.0 4.6 %collective-permute-start.5 = (bf16[2,256,1024]{2,1,0:T(8,128)(2,1)S(1)}, bf16[2,256,1024]{2,1,0:T(8,128)(2,1)S(1)}, u32[]{:S(2)}, u32[]{:S(2)}) collective-permute-start(bf16[2,256,1024]{2,1,0:T(8,128)(2,1)S(1)} %copy-done.14), channel_id=1, source_target_pairs={{0,8},{8,0},{1,9},{9,1},{2,10},{10,2},{3,11},{11,3},{4,12},{12,4},... | collective-permute-start | bytes 3145736 | tf_op jit(solution)/shard_map/ppermute | solution.py:383
  95.5 1.0 copy-start.7
  102.2 21.8 %collective-permute-start.6 = (bf16[2,48,1024]{2,1,0:T(8,128)(2,1)}, bf16[2,48,1024]{2,1,0:T(8,128)(2,1)S(1)}, u32[]{:S(2)}, u32[]{:S(2)}) collective-permute-start(bf16[2,48,1024]{2,1,0:T(8,128)(2,1)} %get-tuple-element.43), channel_id=1, source_target_pairs={{504,0},{0,8},{8,16},{16,24},{24,32},{32,40},{40,48},{48,56},{56,6... | collective-permute-start | bytes 589832 | tf_op jit(solution)/shard_map/ppermute | solution.py:361
  104.3 19.8 %collective-permute-start.7 = (bf16[2,48,1024]{2,1,0:T(8,128)(2,1)}, bf16[2,48,1024]{2,1,0:T(8,128)(2,1)S(1)}, u32[]{:S(2)}, u32[]{:S(2)}) collective-permute-start(bf16[2,48,1024]{2,1,0:T(8,128)(2,1)} %get-tuple-element.44), channel_id=1, source_target_pairs={{448,0},{456,8},{464,16},{472,24},{480,32},{488,40},{496,48},{504,... | collective-permute-start | bytes 589832 | tf_op jit(solution)/shard_map/ppermute | solution.py:361
  107.2 16.8 %collective-permute-start.8 = (bf16[2,16,1024]{2,1,0:T(8,128)(2,1)}, bf16[2,16,1024]{2,1,0:T(8,128)(2,1)S(1)}, u32[]{:S(2)}, u32[]{:S(2)}) collective-permute-start(bf16[2,16,1024]{2,1,0:T(8,128)(2,1)} %get-tuple-element.45), channel_id=1, source_target_pairs={{440,0},{448,8},{456,16},{464,24},{472,32},{480,40},{488,48},{496,... | collective-permute-start | bytes 196616 | tf_op jit(solution)/shard_map/ppermute | solution.py:361
  120.1 1.3 copy-start.1
  124.0 12.1 %copy-start.11 = (bf16[2,16,1024]{2,1,0:T(8,128)(2,1)}, bf16[2,16,1024]{2,1,0:T(8,128)(2,1)S(1)}, u32[]{:S(2)}) copy-start(bf16[2,16,1024]{2,1,0:T(8,128)(2,1)S(1)} %collective-permute-done.8.corner_ref) | copy-start | bytes 196612
  124.0 12.1 %copy-start.8 = (bf16[2,48,1024]{2,1,0:T(8,128)(2,1)}, bf16[2,48,1024]{2,1,0:T(8,128)(2,1)S(1)}, u32[]{:S(2)}) copy-start(bf16[2,48,1024]{2,1,0:T(8,128)(2,1)S(1)} %collective-permute-done.6.west_ref) | copy-start | bytes 589828
  124.1 12.1 %copy-start.9 = (bf16[2,48,1024]{2,1,0:T(8,128)(2,1)}, bf16[2,48,1024]{2,1,0:T(8,128)(2,1)S(1)}, u32[]{:S(2)}) copy-start(bf16[2,48,1024]{2,1,0:T(8,128)(2,1)S(1)} %collective-permute-done.7.north_ref) | copy-start | bytes 589828
  124.1 33.1 %all-to-all-start.2 = ((f32[16,32,128]{2,1,0:T(8,128)}), f32[16,32,128]{2,1,0:T(8,128)S(1)}, u32[]{:S(2)}, u32[]{:S(2)}) async-start(f32[16,32,128]{2,1,0:T(8,128)} %bitcast.26), calls=%async_computation.2 | async-start | bytes 524288 | tf_op jit(solution)/shard_map/all_to_all | solution.py:427
  157.1 0.7 copy-start.6

commit v4 on v3

--- a/solution.py
+++ b/solution.py
@@ -156,16 +156,22 @@
 
 
 def attend_kernel(
-    ints_ref, sides_ref, peer_ref, got_ref, bias_ref, back_ref, wo_ref, send_ref, qkv_ref, gh_ref
+    ints_ref, sides_ref, peer_hbm, got_ref, bias_ref, back_ref, wo_ref, send_ref,
+    qkv_ref, gh_ref, peer_ref, sem,
 ):
     core = ints_ref[4]
-    both = [jnp.concatenate([sides_ref[k, :CELLS], peer_ref[k, :CELLS]], axis=0) for k in range(2)]
+    copy = pltpu.make_async_copy(peer_hbm, peer_ref, sem)
+    copy.start()
     for s in range(4):
-        qkv_ref[:, pl.ds(s * 256, 256)] = mm(both[0], got_ref[s]).astype(bf16)
+        qkv_ref[pl.ds(0, CELLS), pl.ds(s * 256, 256)] = mm(sides_ref[0, :CELLS], got_ref[s]).astype(bf16)
         for y in range(4):
             row = [got_ref[y, pl.ds(s * 256 + q * 64, 64), pl.ds(128, 128)][:, 64:] for q in range(4)]
             wo_ref[pl.ds(s * 64, 64), pl.ds(y * 256, 256)] = jnp.concatenate(row, axis=1)
-    gh_ref[...] = mm(both[1], wo_ref[...], TRAILING).astype(bf16)
+    gh_ref[pl.ds(0, CELLS)] = mm(sides_ref[1, :CELLS], wo_ref[...], TRAILING).astype(bf16)
+    copy.wait()
+    for s in range(4):
+        qkv_ref[pl.ds(CELLS, CELLS), pl.ds(s * 256, 256)] = mm(peer_ref[0, :CELLS], got_ref[s]).astype(bf16)
+    gh_ref[pl.ds(CELLS, CELLS)] = mm(peer_ref[1, :CELLS], wo_ref[...], TRAILING).astype(bf16)
     keys = lax.broadcasted_iota(jnp.int32, (128, 128), 0)
     lower = lax.broadcasted_iota(jnp.int32, (64, 128), 1) < 64
     query = lax.broadcasted_iota(jnp.int32, (1, 128), 1)
@@ -256,9 +262,11 @@
 
 
 def home_kernel(
-    ints_ref, normf_ref, inv_ref, tok_ref, dy_ref, got_ref, wo_ref, back_ref, came_ref,
-    out_ref, gtok_ref, east_ref, south_ref, corner_ref,
+    ints_ref, normf_ref, inv_ref, tok_ref, dy_ref, got_ref, wo_ref, back_ref, came_hbm,
+    out_ref, gtok_ref, east_ref, south_ref, corner_ref, came_ref, sem,
 ):
+    copy = pltpu.make_async_copy(came_hbm, came_ref, sem)
+    copy.start()
     own, halo = scatter_matrices([ints_ref[k] for k in range(3)])
 
     def edges(which, values):
@@ -268,6 +276,7 @@
         corner_ref[which] = edge[2 * EAST : 2 * EAST + CORNER]
 
     branch, dnormed = head_parts(got_ref, wo_ref, back_ref[pl.ds(0, CELLS)])
+    copy.wait()
     branch = (branch + came_ref[0].astype(f32)).astype(bf16)
     edges(0, branch)
     out_ref[...] = (tok_ref[...].astype(f32) + mm(own, branch)).astype(bf16)
@@ -314,10 +323,12 @@
     go_ref[...] = jnp.concatenate([total[24:, :64], total[24:, 64:]], axis=0)
 
 
-def call(kernel, outs, *args, smem=0, scratch=(), flops=0, name=None):
+def call(kernel, outs, *args, smem=0, hbm=(), scratch=(), flops=0, name=None):
     specs = [pl.BlockSpec(memory_space=pltpu.SMEM)] * smem + [pl.BlockSpec(memory_space=pltpu.VMEM)] * (
         len(args) - smem
     )
+    for k in hbm:
+        specs[k] = pl.BlockSpec(memory_space=pl.ANY)
     shapes = [jax.ShapeDtypeStruct(s, d) for s, d in outs]
     size = sum(a.size * a.dtype.itemsize for a in (*args, *shapes))
     return pl.pallas_call(
@@ -326,7 +337,7 @@
         in_specs=specs,
         out_specs=[pl.BlockSpec(memory_space=pltpu.VMEM)] * len(outs),
         scratch_shapes=list(scratch),
-        compiler_params=pltpu.CompilerParams(vmem_limit_bytes=VMEM_LIMIT),
+        compiler_params=pltpu.CompilerParams(vmem_limit_bytes=60 * 2**20 if hbm else VMEM_LIMIT),
         cost_estimate=pl.CostEstimate(flops=flops, bytes_accessed=size, transcendentals=0),
         name=name,
     )(*args)
@@ -397,7 +408,10 @@
         attend_kernel,
         [((2 * CELLS, width), bf16), ((256, width), bf16), ((2, CELLS, width), bf16)],
         ints, sides, peer, mine, bias,
-        smem=1, scratch=[pltpu.VMEM((2 * CELLS, 1024), bf16), pltpu.VMEM((2 * CELLS, 256), bf16)],
+        smem=1, hbm=(2,), scratch=[
+            pltpu.VMEM((2 * CELLS, 1024), bf16), pltpu.VMEM((2 * CELLS, 256), bf16),
+            pltpu.VMEM((2, CELLS + FLAG_ROWS, 1024), bf16), pltpu.SemaphoreType.DMA,
+        ],
         flops=2 * 256 * 1024 * 2048, name="attend",
     )
     (pair,) = call(
@@ -414,7 +428,8 @@
             ((CELLS, width), bf16), ((CELLS, width), bf16),
             ((2, EAST, width), bf16), ((2, EAST, width), bf16), ((2, CORNER, width), bf16),
         ],
-        ints, normed_f, inverse, tok, dy, mine, wo, back, came, smem=1, flops=2 * 256 * 1024 * 900, name="home",
+        ints, normed_f, inverse, tok, dy, mine, wo, back, came, smem=1, hbm=(8,),
+        scratch=[pltpu.VMEM((2, CELLS, width), bf16), pltpu.SemaphoreType.DMA], flops=2 * 256 * 1024 * 900, name="home",
     )
     north = shifted(south, GRID_COLS)
     corner = shifted(corner, GRID_COLS + 1)

time: 160 us -> 160 us (level)
    unnamed x31 -> x29, local copies, waits for them, and re-layouts: 6.88 us -> 6.9 us
  transfers between devices with their start and end apart: 12 -> 12, of which waited for: 6 -> 6; matrix products, arithmetic and copies ran while one was open for 6% -> 6% of each run, Pallas kernels for 9% -> 10%
where the time goes in v4:
time: 160 us; the launch traced here: 159 us
  starting transfers between devices  73.5 us (46%)
  Pallas kernels  34.6 us (22%)
  waiting for transfers between devices  34.2 us (21%)
  local copies, waits for them, and re-layouts  9.92 us (6%)
  other arithmetic  3.13 us (2%)
  matrix products  2.56 us (2%)
    pallas_call x9, Pallas kernels, call(): pl.pallas_call(kernel, out_shape=shapes, in_specs=specs, out_specs=[pl.Bl...  34.6 us
    ppermute x6, starting transfers between devices, shifted(): lax.ppermute(block, TILE_AXES, [((i - distance) % count, i) for i in rang...  26.7 us
    all_to_all x1, waiting for transfers between devices, per_device(): lax.all_to_all(plane.reshape(16, 32, 128), ('zl', 'zh'), 0, 0, tiled=True)  17.9 us
    ppermute x1, starting transfers between devices, per_device(): across = lax.ppermute(piece, 'zh', [(0, 1), (1, 0)])  14.8 us
    all_to_all x1, starting transfers between devices, per_device(): lax.all_to_all(plane.reshape(16, 32, 128), ('zl', 'zh'), 0, 0, tiled=True)  11.5 us
    all_to_all x1, waiting for transfers between devices, per_device(): lax.all_to_all(pair.reshape(32, 128, 256), ('y', 'c', 'x'), 0, 0, tiled=T...  7.91 us
    all_to_all x1, starting transfers between devices, per_device(): lax.all_to_all(many, ('y', 'x'), 0, 0, tiled=True).reshape(4, width, 256)  7.55 us
    all_to_all x1, starting transfers between devices, per_device(): lax.all_to_all(pair.reshape(32, 128, 256), ('y', 'c', 'x'), 0, 0, tiled=T...  7.11 us
  transfers between devices with their start and end apart: 12, of which 6 were waited for; matrix products, arithmetic and copies ran while one was open for 6% of the time, Pallas kernels for 10%

profile of v4, /device:TPU:38, one launch (start us, length us, event | category | flops | bytes accessed | tf_op | source)
XLA Modules:
  0.0 159.5 jit_solution(10476559534324793108)
XLA Ops:
  0.7 0.5 compare_select_fusion.1.spot_ref
  1.2 2.1 %piece.1.here_ref = bf16[128,384]{1,0:T(8,128)(2,1)} custom-call(s32[3]{0:T(128)} %compare_select_fusion.1.spot_ref, bf16[128,1536]{1,0:T(8,128)(2,1)} %wq_ref.1, bf16[64,1024]{1,0:T(8,128)(2,1)} %wo_ref.1), custom_call_target="tpu_custom_call" | custom-call | bytes 622604 | tf_op jit(solution)/shard_map/piece/pallas_call | solution.py:334
  3.2 14.8 %collective-permute-start = (bf16[128,384]{1,0:T(8,128)(2,1)}, bf16[128,384]{1,0:T(8,128)(2,1)S(1)}, u32[]{:S(2)}, u32[]{:S(2)}) collective-permute-start(bf16[128,384]{1,0:T(8,128)(2,1)} %piece.1.here_ref), channel_id=1, source_target_pairs={{0,1},{1,0},{2,3},{3,2},{4,5},{5,4},{6,7},{7,6},{8,9},{9,8},{10,11... | collective-permute-start | bytes 294920 | tf_op jit(solution)/shard_map/ppermute | solution.py:387
  18.1 0.8 copy.11
  18.9 0.1 reshape.129
  19.0 0.1 add_add_fusion
  19.1 0.1 add.55
  19.2 2.6 %convolution_bitcast_fusion = f32[8,4096]{1,0:T(8,128)S(1)} fusion(f32[8,225]{1,0:T(8,128)S(1)} %reshape.129, s32[4096]{0:T(1024)S(1)} %add.55), kind=kOutput, calls=%fused_computation | convolution fusion | flops 89395200 | bytes 154656 | tf_op jit(solution)/shard_map/dot_general | solution.py:357
  21.7 0.1 reshape.130
  21.9 1.1 pad_maximum_fusion
  23.0 0.8 pad_maximum_fusion.1.bias_ref
  23.8 0.6 copy-done.10
  24.4 2.5 %slots.1 = bf16[16,256,256]{2,1,0:T(8,128)(2,1)} custom-call(s32[3]{0:T(128)} %compare_select_fusion.1.spot_ref, bf16[128,384]{1,0:T(8,128)(2,1)} %piece.1.here_ref, bf16[128,384]{1,0:T(8,128)(2,1)} %copy-done.10), custom_call_target="tpu_custom_call" | custom-call | bytes 2293772 | tf_op jit(solution)/shard_map/slots/pallas_call | solution.py:334
  26.9 7.6 %all-to-all-start = ((bf16[16,256,256]{2,1,0:T(8,128)(2,1)}), bf16[16,256,256]{2,1,0:T(8,128)(2,1)S(1)}, u32[]{:S(2)}, u32[]{:S(2)}) async-start(bf16[16,256,256]{2,1,0:T(8,128)(2,1)} %slots.1), calls=%async_computation | async-start | bytes 4194304 | tf_op jit(solution)/shard_map/all_to_all | solution.py:391
  34.5 0.7 slice.9
  35.3 0.1 slice.10
  35.3 1.7 %reshape.131 = bf16[2,48,1024]{2,1,0:T(8,128)(2,1)} reshape(bf16[2,12,4,1024]{3,2,1,0:T(4,128)(2,1)} %slice.9) | data formatting | bytes 393216 | tf_op jit(solution)/shard_map/reshape | solution.py:396
  37.0 3.6 %collective-permute-start.1 = (bf16[2,48,1024]{2,1,0:T(8,128)(2,1)}, bf16[2,48,1024]{2,1,0:T(8,128)(2,1)}, u32[]{:S(2)}, u32[]{:S(2)}) collective-permute-start(bf16[2,48,1024]{2,1,0:T(8,128)(2,1)} %reshape.131), channel_id=1, source_target_pairs={{8,0},{16,8},{24,16},{32,24},{40,32},{48,40},{56,48},{64,56},{72,6... | collective-permute-start | bytes 589832 | tf_op jit(solution)/shard_map/ppermute | solution.py:372
  40.6 0.2 copy.12
  40.9 6.2 %collective-permute-start.2 = (bf16[2,48,1024]{2,1,0:T(8,128)(2,1)S(1)}, bf16[2,48,1024]{2,1,0:T(8,128)(2,1)}, u32[]{:S(2)}, u32[]{:S(2)}) collective-permute-start(bf16[2,48,1024]{2,1,0:T(8,128)(2,1)S(1)} %copy.13), channel_id=1, source_target_pairs={{64,0},{72,8},{80,16},{88,24},{96,32},{104,40},{112,48},{120,56},{... | collective-permute-start | bytes 589832 | tf_op jit(solution)/shard_map/ppermute | solution.py:372
  47.8 8.2 %collective-permute-start.3 = (bf16[2,16,1024]{2,1,0:T(8,128)(2,1)S(1)}, bf16[2,16,1024]{2,1,0:T(8,128)(2,1)S(1)}, u32[]{:S(2)}, u32[]{:S(2)}) collective-permute-start(bf16[2,16,1024]{2,1,0:T(8,128)(2,1)S(1)} %reshape.133), channel_id=1, source_target_pairs={{72,0},{80,8},{88,16},{96,24},{104,32},{112,40},{120,48},{128,56},... | collective-permute-start | bytes 196616 | tf_op jit(solution)/shard_map/ppermute | solution.py:372
  56.0 0.6 pad_add_fusion.ints_ref
  56.6 2.0 %collective-permute-done.3.c_ref = bf16[2,16,1024]{2,1,0:T(8,128)(2,1)S(1)} collective-permute-done((bf16[2,16,1024]{2,1,0:T(8,128)(2,1)S(1)}, bf16[2,16,1024]{2,1,0:T(8,128)(2,1)S(1)}, u32[]{:S(2)}, u32[]{:S(2)}) %collective-permute-start.3) | collective-permute-done | bytes 65568 | tf_op jit(solution)/shard_map/ppermute | solution.py:372
  58.7 0.6 copy-done.12
  59.3 3.6 %prep.1 = (bf16[2,272,1024]{2,1,0:T(8,128)(2,1)}, f32[256,1024]{1,0:T(8,128)}, f32[256,128]{1,0:T(8,128)}) custom-call(s32[5]{0:T(128)} %pad_add_fusion.ints_ref, bf16[256,1024]{1,0:T(8,128)(2,1)} %bitcast.19, bf16[256,1024]{1,0:T(8,128)(2,1)} %bitcast.22, bf16[2,48,1024]{2,1,0:T(8,128)(2,1)} %collective-permute-done.1.e_ref, ...), custom_call_target="tpu_custom_call" | custom-call | flops 402653184 | bytes 3801108 | tf_op jit(solution)/shard_map/prep/pallas_call | solution.py:334
  62.9 3.8 %collective-permute-start.4 = (bf16[2,272,1024]{2,1,0:T(8,128)(2,1)}, bf16[2,272,1024]{2,1,0:T(8,128)(2,1)S(1)}, u32[]{:S(2)}, u32[]{:S(2)}) collective-permute-start(bf16[2,272,1024]{2,1,0:T(8,128)(2,1)} %get-tuple-element.35.sides_ref), channel_id=1, source_target_pairs={{0,8},{8,0},{1,9},{9,1},{2,10},{10,2},{3,11},{11,3},{4,12},{12,4},... | collective-permute-start | bytes 3342344 | tf_op jit(solution)/shard_map/ppermute | solution.py:394
  66.7 2.6 %collective-permute-done.4.peer_hbm.peer_ref = bf16[2,272,1024]{2,1,0:T(8,128)(2,1)S(1)} collective-permute-done((bf16[2,272,1024]{2,1,0:T(8,128)(2,1)}, bf16[2,272,1024]{2,1,0:T(8,128)(2,1)S(1)}, u32[]{:S(2)}, u32[]{:S(2)}) %collective-permute-start.4) | collective-permute-done | bytes 1114144 | tf_op jit(solution)/shard_map/ppermute | solution.py:394
  69.2 1.0 copy-done.5
  70.2 0.7 copy-done
  70.9 7.8 %attend.1 = (bf16[512,1024]{1,0:T(8,128)(2,1)}, bf16[256,1024]{1,0:T(8,128)(2,1)}, bf16[2,256,1024]{2,1,0:T(8,128)(2,1)}) custom-call(s32[5]{0:T(128)} %pad_add_fusion.ints_ref, bf16[2,272,1024]{2,1,0:T(8,128)(2,1)} %get-tuple-element.35.sides_ref, bf16[2,272,1024]{2,1,0:T(8,128)(2,1)} %copy-done.5, bf16[4,1024,256]{2,1,0:T(8,128)(2,1)} %bitcast.17, ...), custom_call_target="tpu_custom_call" | custom-call | flops 1073741824 | bytes 7208980 | tf_op jit(solution)/shard_map/attend/pallas_call | solution.py:334
  78.7 5.1 %weight_grads.1 = bf16[4,2,4,128,256]{4,3,2,1,0:T(8,128)(2,1)} custom-call(bf16[2,272,1024]{2,1,0:T(8,128)(2,1)} %get-tuple-element.35.sides_ref, bf16[2,272,1024]{2,1,0:T(8,128)(2,1)} %copy-done.5, bf16[512,1024]{1,0:T(8,128)(2,1)} %get-tuple-element.39.back_ref), custom_call_target="tpu_custom_call" | custom-call | flops 1610612736 | bytes 5373952 | tf_op jit(solution)/shard_map/weight_grads/pallas_call | solution.py:334
  83.8 7.1 %all-to-all-start.1 = ((bf16[32,128,256]{2,1,0:T(8,128)(2,1)}), bf16[32,128,256]{2,1,0:T(8,128)(2,1)S(1)}, u32[]{:S(2)}, u32[]{:S(2)}) async-start(bf16[32,128,256]{2,1,0:T(8,128)(2,1)} %bitcast.25), calls=%async_computation.1 | async-start | bytes 4194304 | tf_op jit(solution)/shard_map/all_to_all | solution.py:437
  90.9 2.1 %collective-permute-start.5 = (bf16[2,256,1024]{2,1,0:T(8,128)(2,1)}, bf16[2,256,1024]{2,1,0:T(8,128)(2,1)S(1)}, u32[]{:S(2)}, u32[]{:S(2)}) collective-permute-start(bf16[2,256,1024]{2,1,0:T(8,128)(2,1)} %get-tuple-element.40), channel_id=1, source_target_pairs={{0,8},{8,0},{1,9},{9,1},{2,10},{10,2},{3,11},{11,3},{4,12},{12,4},... | collective-permute-start | bytes 3145736 | tf_op jit(solution)/shard_map/ppermute | solution.py:394
  93.0 2.7 %collective-permute-done.5.came_hbm = bf16[2,256,1024]{2,1,0:T(8,128)(2,1)S(1)} collective-permute-done((bf16[2,256,1024]{2,1,0:T(8,128)(2,1)}, bf16[2,256,1024]{2,1,0:T(8,128)(2,1)S(1)}, u32[]{:S(2)}, u32[]{:S(2)}) %collective-permute-start.5) | collective-permute-done | bytes 1048608 | tf_op jit(solution)/shard_map/ppermute | solution.py:394
  95.7 1.0 copy-done.7
  96.7 6.8 %home.1 = (bf16[256,1024]{1,0:T(8,128)(2,1)}, bf16[256,1024]{1,0:T(8,128)(2,1)}, bf16[2,48,1024]{2,1,0:T(8,128)(2,1)}, bf16[2,48,1024]{2,1,0:T(8,128)(2,1)}, bf16[2,16,1024]{2,1,0:T(8,128)(2,1)}) custom-call(s32[5]{0:T(128)} %pad_add_fusion.ints_ref, f32[256,1024]{1,0:T(8,128)} %get-tuple-element.30.normf_ref, f32[256,128]{1,0:T(8,128)} %get-tuple-element.31.inv_ref, ...), custom_call_target="tpu_custom_call" | custom-call | flops 471859200 | bytes 8454164 | tf_op jit(solution)/shard_map/home/pallas_call | solution.py:334
  103.5 2.1 %collective-permute-start.6 = (bf16[2,48,1024]{2,1,0:T(8,128)(2,1)}, bf16[2,48,1024]{2,1,0:T(8,128)(2,1)S(1)}, u32[]{:S(2)}, u32[]{:S(2)}) collective-permute-start(bf16[2,48,1024]{2,1,0:T(8,128)(2,1)} %get-tuple-element.43), channel_id=1, source_target_pairs={{504,0},{0,8},{8,16},{16,24},{24,32},{32,40},{40,48},{48,56},{56,6... | collective-permute-start | bytes 589832 | tf_op jit(solution)/shard_map/ppermute | solution.py:372
  105.6 2.9 %collective-permute-start.7 = (bf16[2,48,1024]{2,1,0:T(8,128)(2,1)}, bf16[2,48,1024]{2,1,0:T(8,128)(2,1)S(1)}, u32[]{:S(2)}, u32[]{:S(2)}) collective-permute-start(bf16[2,48,1024]{2,1,0:T(8,128)(2,1)} %get-tuple-element.44), channel_id=1, source_target_pairs={{448,0},{456,8},{464,16},{472,24},{480,32},{488,40},{496,48},{504,... | collective-permute-start | bytes 589832 | tf_op jit(solution)/shard_map/ppermute | solution.py:372
  108.5 3.7 %collective-permute-start.8 = (bf16[2,16,1024]{2,1,0:T(8,128)(2,1)}, bf16[2,16,1024]{2,1,0:T(8,128)(2,1)S(1)}, u32[]{:S(2)}, u32[]{:S(2)}) collective-permute-start(bf16[2,16,1024]{2,1,0:T(8,128)(2,1)} %get-tuple-element.45), channel_id=1, source_target_pairs={{440,0},{448,8},{456,16},{464,24},{472,32},{480,40},{488,48},{496,... | collective-permute-start | bytes 196616 | tf_op jit(solution)/shard_map/ppermute | solution.py:372
  112.2 7.9 %all-to-all-done.1.got_ref = bf16[32,128,256]{2,1,0:T(8,128)(2,1)S(1)} async-done(((bf16[32,128,256]{2,1,0:T(8,128)(2,1)}), bf16[32,128,256]{2,1,0:T(8,128)(2,1)S(1)}, u32[]{:S(2)}, u32[]{:S(2)}) %all-to-all-start.1) | async-done | bytes 2097184 | tf_op jit(solution)/shard_map/all_to_all | solution.py:437
  120.1 1.3 copy-done.1
  121.5 2.6 %plane_sum.1 = f32[8,2,32,128]{3,2,1,0:T(8,128)} custom-call(bf16[32,128,256]{2,1,0:T(8,128)(2,1)} %copy-done.1), custom_call_target="tpu_custom_call" | custom-call | bytes 2359296 | tf_op jit(solution)/shard_map/plane_sum/pallas_call | solution.py:334
  124.0 1.1 collective-permute-done.8.corner_ref
  125.2 11.5 %all-to-all-start.2 = ((f32[16,32,128]{2,1,0:T(8,128)}), f32[16,32,128]{2,1,0:T(8,128)S(1)}, u32[]{:S(2)}, u32[]{:S(2)}) async-start(f32[16,32,128]{2,1,0:T(8,128)} %bitcast.26), calls=%async_computation.2 | async-start | bytes 524288 | tf_op jit(solution)/shard_map/all_to_all | solution.py:442
  136.7 2.6 %finish.1 = (bf16[256,1024]{1,0:T(8,128)(2,1)}, bf16[256,1024]{1,0:T(8,128)(2,1)}) custom-call(bf16[256,1024]{1,0:T(8,128)(2,1)} %get-tuple-element.41.out_ref, bf16[256,1024]{1,0:T(8,128)(2,1)} %get-tuple-element.42.gtok_ref, bf16[2,48,1024]{2,1,0:T(8,128)(2,1)} %copy-done.8, bf16[2,48,1024]{2,1,0:T(8,128)(2,1)} %copy-done.9, bf16[2,16,1024]{2,1,0:T(8,128)(2,1)} %copy-done.11), custom_call_target="tpu_custom_call" | custom-call | bytes 2555904 | tf_op jit(solution)/shard_map/finish/pallas_call | solution.py:334
  139.3 17.9 %all-to-all-done.2.got_ref = f32[16,32,128]{2,1,0:T(8,128)S(1)} async-done(((f32[16,32,128]{2,1,0:T(8,128)}), f32[16,32,128]{2,1,0:T(8,128)S(1)}, u32[]{:S(2)}, u32[]{:S(2)}) %all-to-all-start.2) | async-done | bytes 262176 | tf_op jit(solution)/shard_map/all_to_all | solution.py:442
  157.2 0.7 copy-done.6
  157.8 1.6 %column_sum.1 = (f32[24,128]{1,0:T(8,128)}, f32[16,64]{1,0:T(8,128)}) custom-call(f32[16,32,128]{2,1,0:T(8,128)} %copy-done.6), custom_call_target="tpu_custom_call" | custom-call | bytes 278528 | tf_op jit(solution)/shard_map/column_sum/pallas_call | solution.py:334
  (31 shorter events, 0.1 us)
Async XLA Ops:
  0.6 21.2 %copy-start.3 = (bf16[1,1,16,16,1024]{4,3,2,1,0:T(8,128)(2,1)S(1)}, bf16[1,1,16,16,1024]{4,3,2,1,0:T(8,128)(2,1)}, u32[]{:S(2)}) copy-start(bf16[1,1,16,16,1024]{4,3,2,1,0:T(8,128)(2,1)} %param.13) | copy-start | bytes 1572868
  0.6 21.2 %copy-start.2 = (bf16[1,1,16,16,1024]{4,3,2,1,0:T(8,128)(2,1)S(1)}, bf16[1,1,16,16,1024]{4,3,2,1,0:T(8,128)(2,1)}, u32[]{:S(2)}) copy-start(bf16[1,1,16,16,1024]{4,3,2,1,0:T(8,128)(2,1)} %param.7) | copy-start | bytes 1572868
  3.2 20.6 %collective-permute-start = (bf16[128,384]{1,0:T(8,128)(2,1)}, bf16[128,384]{1,0:T(8,128)(2,1)S(1)}, u32[]{:S(2)}, u32[]{:S(2)}) collective-permute-start(bf16[128,384]{1,0:T(8,128)(2,1)} %piece.1.here_ref), channel_id=1, source_target_pairs={{0,1},{1,0},{2,3},{3,2},{4,5},{5,4},{6,7},{7,6},{8,9},{9,8},{10,11... | collective-permute-start | bytes 294920 | tf_op jit(solution)/shard_map/ppermute | solution.py:387
  23.8 0.6 copy-start.10
  26.9 7.6 %copy-start.4 = (bf16[2,16,16,1024]{3,2,1,0:T(8,128)(2,1)S(1)}, bf16[2,16,16,1024]{3,2,1,0:T(8,128)(2,1)}, u32[]{:S(2)}) copy-start(bf16[2,16,16,1024]{3,2,1,0:T(8,128)(2,1)} %pad_maximum_fusion) | copy-start | bytes 3145732
  26.9 42.3 %all-to-all-start = ((bf16[16,256,256]{2,1,0:T(8,128)(2,1)}), bf16[16,256,256]{2,1,0:T(8,128)(2,1)S(1)}, u32[]{:S(2)}, u32[]{:S(2)}) async-start(bf16[16,256,256]{2,1,0:T(8,128)(2,1)} %slots.1), calls=%async_computation | async-start | bytes 4194304 | tf_op jit(solution)/shard_map/all_to_all | solution.py:391
  34.5 21.5 %copy-start.13 = (s32[1,3]{1,0:T(1,128)S(1)}, s32[1,3]{1,0:T(1,128)}, u32[]{:S(2)}) copy-start(s32[1,3]{1,0:T(1,128)} %param.11) | copy-start | bytes 40
  37.0 21.7 %collective-permute-start.1 = (bf16[2,48,1024]{2,1,0:T(8,128)(2,1)}, bf16[2,48,1024]{2,1,0:T(8,128)(2,1)}, u32[]{:S(2)}, u32[]{:S(2)}) collective-permute-start(bf16[2,48,1024]{2,1,0:T(8,128)(2,1)} %reshape.131), channel_id=1, source_target_pairs={{8,0},{16,8},{24,16},{32,24},{40,32},{48,40},{56,48},{64,56},{72,6... | collective-permute-start | bytes 589832 | tf_op jit(solution)/shard_map/ppermute | solution.py:372
  40.9 17.8 %collective-permute-start.2 = (bf16[2,48,1024]{2,1,0:T(8,128)(2,1)S(1)}, bf16[2,48,1024]{2,1,0:T(8,128)(2,1)}, u32[]{:S(2)}, u32[]{:S(2)}) collective-permute-start(bf16[2,48,1024]{2,1,0:T(8,128)(2,1)S(1)} %copy.13), channel_id=1, source_target_pairs={{64,0},{72,8},{80,16},{88,24},{96,32},{104,40},{112,48},{120,56},{... | collective-permute-start | bytes 589832 | tf_op jit(solution)/shard_map/ppermute | solution.py:372
  47.8 10.8 %collective-permute-start.3 = (bf16[2,16,1024]{2,1,0:T(8,128)(2,1)S(1)}, bf16[2,16,1024]{2,1,0:T(8,128)(2,1)S(1)}, u32[]{:S(2)}, u32[]{:S(2)}) collective-permute-start(bf16[2,16,1024]{2,1,0:T(8,128)(2,1)S(1)} %reshape.133), channel_id=1, source_target_pairs={{72,0},{80,8},{88,16},{96,24},{104,32},{112,40},{120,48},{128,56},... | collective-permute-start | bytes 196616 | tf_op jit(solution)/shard_map/ppermute | solution.py:372
  58.6 0.6 copy-start.12
  62.9 6.3 %collective-permute-start.4 = (bf16[2,272,1024]{2,1,0:T(8,128)(2,1)}, bf16[2,272,1024]{2,1,0:T(8,128)(2,1)S(1)}, u32[]{:S(2)}, u32[]{:S(2)}) collective-permute-start(bf16[2,272,1024]{2,1,0:T(8,128)(2,1)} %get-tuple-element.35.sides_ref), channel_id=1, source_target_pairs={{0,8},{8,0},{1,9},{9,1},{2,10},{10,2},{3,11},{11,3},{4,12},{12,4},... | collective-permute-start | bytes 3342344 | tf_op jit(solution)/shard_map/ppermute | solution.py:394
  69.2 1.0 copy-start.5
  69.2 1.7 %copy-start = (bf16[16,256,256]{2,1,0:T(8,128)(2,1)}, bf16[16,256,256]{2,1,0:T(8,128)(2,1)S(1)}, u32[]{:S(2)}) copy-start(bf16[16,256,256]{2,1,0:T(8,128)(2,1)S(1)} %all-to-all-done) | copy-start | bytes 6291460
  83.8 36.3 %all-to-all-start.1 = ((bf16[32,128,256]{2,1,0:T(8,128)(2,1)}), bf16[32,128,256]{2,1,0:T(8,128)(2,1)S(1)}, u32[]{:S(2)}, u32[]{:S(2)}) async-start(bf16[32,128,256]{2,1,0:T(8,128)(2,1)} %bitcast.25), calls=%async_computation.1 | async-start | bytes 4194304 | tf_op jit(solution)/shard_map/all_to_all | solution.py:437
  90.9 4.8 %collective-permute-start.5 = (bf16[2,256,1024]{2,1,0:T(8,128)(2,1)}, bf16[2,256,1024]{2,1,0:T(8,128)(2,1)S(1)}, u32[]{:S(2)}, u32[]{:S(2)}) collective-permute-start(bf16[2,256,1024]{2,1,0:T(8,128)(2,1)} %get-tuple-element.40), channel_id=1, source_target_pairs={{0,8},{8,0},{1,9},{9,1},{2,10},{10,2},{3,11},{11,3},{4,12},{12,4},... | collective-permute-start | bytes 3145736 | tf_op jit(solution)/shard_map/ppermute | solution.py:394
  95.7 1.0 copy-start.7
  103.5 21.7 %collective-permute-start.6 = (bf16[2,48,1024]{2,1,0:T(8,128)(2,1)}, bf16[2,48,1024]{2,1,0:T(8,128)(2,1)S(1)}, u32[]{:S(2)}, u32[]{:S(2)}) collective-permute-start(bf16[2,48,1024]{2,1,0:T(8,128)(2,1)} %get-tuple-element.43), channel_id=1, source_target_pairs={{504,0},{0,8},{8,16},{16,24},{24,32},{32,40},{40,48},{48,56},{56,6... | collective-permute-start | bytes 589832 | tf_op jit(solution)/shard_map/ppermute | solution.py:372
  105.6 19.6 %collective-permute-start.7 = (bf16[2,48,1024]{2,1,0:T(8,128)(2,1)}, bf16[2,48,1024]{2,1,0:T(8,128)(2,1)S(1)}, u32[]{:S(2)}, u32[]{:S(2)}) collective-permute-start(bf16[2,48,1024]{2,1,0:T(8,128)(2,1)} %get-tuple-element.44), channel_id=1, source_target_pairs={{448,0},{456,8},{464,16},{472,24},{480,32},{488,40},{496,48},{504,... | collective-permute-start | bytes 589832 | tf_op jit(solution)/shard_map/ppermute | solution.py:372
  108.5 16.7 %collective-permute-start.8 = (bf16[2,16,1024]{2,1,0:T(8,128)(2,1)}, bf16[2,16,1024]{2,1,0:T(8,128)(2,1)S(1)}, u32[]{:S(2)}, u32[]{:S(2)}) collective-permute-start(bf16[2,16,1024]{2,1,0:T(8,128)(2,1)} %get-tuple-element.45), channel_id=1, source_target_pairs={{440,0},{448,8},{456,16},{464,24},{472,32},{480,40},{488,48},{496,... | collective-permute-start | bytes 196616 | tf_op jit(solution)/shard_map/ppermute | solution.py:372
  120.1 1.4 copy-start.1
  125.2 11.5 %copy-start.11 = (bf16[2,16,1024]{2,1,0:T(8,128)(2,1)}, bf16[2,16,1024]{2,1,0:T(8,128)(2,1)S(1)}, u32[]{:S(2)}) copy-start(bf16[2,16,1024]{2,1,0:T(8,128)(2,1)S(1)} %collective-permute-done.8.corner_ref) | copy-start | bytes 196612
  125.2 11.5 %copy-start.8 = (bf16[2,48,1024]{2,1,0:T(8,128)(2,1)}, bf16[2,48,1024]{2,1,0:T(8,128)(2,1)S(1)}, u32[]{:S(2)}) copy-start(bf16[2,48,1024]{2,1,0:T(8,128)(2,1)S(1)} %collective-permute-done.6.west_ref) | copy-start | bytes 589828
  125.2 11.5 %copy-start.9 = (bf16[2,48,1024]{2,1,0:T(8,128)(2,1)}, bf16[2,48,1024]{2,1,0:T(8,128)(2,1)S(1)}, u32[]{:S(2)}) copy-start(bf16[2,48,1024]{2,1,0:T(8,128)(2,1)S(1)} %collective-permute-done.7.north_ref) | copy-start | bytes 589828
  125.2 32.0 %all-to-all-start.2 = ((f32[16,32,128]{2,1,0:T(8,128)}), f32[16,32,128]{2,1,0:T(8,128)S(1)}, u32[]{:S(2)}, u32[]{:S(2)}) async-start(f32[16,32,128]{2,1,0:T(8,128)} %bitcast.26), calls=%async_computation.2 | async-start | bytes 524288 | tf_op jit(solution)/shard_map/all_to_all | solution.py:442
  157.2 0.7 copy-start.6
